TPU v7x, 256 devices: a whole 4x4x8 slice. The times are simulated.
256 devices in a mesh: seq: 4 (over y), res: 64 (over x, z, core).
Axes of the slice: x: 4, y: 4, z: 8, core: 2. Of those that a mesh axis runs over, the one named last changes fastest.
Arguments:
- alignment: int32 [3072, 1024], P(None, 'seq'), may hold values from 0 to 20
- seq_weights: float32 [1024], P('seq'), may hold values from 0.1 to 1
- fields: float32 [3072, 21], P('res'), may hold values from -4 to 352
- couplings: bfloat16 [32768, 441], P('res'), may hold values from -2.390625 to 2.390625
- pair_left: int32 [32768], P('res'), may hold values from 0 to 47, as said below
- pair_slot: int32 [32768], P('res'), may hold values from 0 to 3
- slot_residue: int32 [16384], P('res'), may hold values from 0 to 47
- pair_count: int32 [4096], P('res'), may hold values from 1 to 8, as said below
Outputs:
- coupling_grad: float32 [32768, 441], P('res')
- field_grad: float32 [3072, 21], P('res')
Inputs may be any that keep to these rules, and one draw needn't show every extreme that they name: `pair_left`: A residue never pairs with itself; the same two residues may form more than one pair. Only the first pair_count slots of each bucket are live.
All inputs are finite; a program needn't handle non-finite values.
Results may differ from a plain program's by a relative error of at most 0.003.
Values may be sent and summed in bfloat16 or wider, within the bound.
No kernel may reach another device: no remote copies, remote signals or barrier semaphores. Data moves between devices by JAX's collectives and lax.ppermute only.
A program may use at most 128 MiB of HBM per device.

v0:
```python
import jax
import jax.numpy as jnp
from jax import lax
from jax.sharding import PartitionSpec as P

Q = 21


def shortened(x):

    def short(part):
        return part.astype(jnp.bfloat16) if part.dtype == jnp.float32 else part

    return jax.tree.map(short, x)


def onehot(states):
    state_codes = jnp.arange(Q, dtype=jnp.int32)
    return (states[:, None, :] == state_codes[None, :, None]).astype(jnp.bfloat16)


def per_device(
    alignment, seq_weights, fields, couplings, pair_left, pair_slot, slot_residue, pair_count
):
    res_devices = lax.axis_size("res")
    my_index = lax.axis_index("res")
    res_local = fields.shape[0]
    seq_local = alignment.shape[1]
    pair_local = couplings.shape[0]
    capacity = pair_local // res_devices
    slot_count = slot_residue.shape[0] // res_devices
    grad_scale = Q / (seq_local * lax.axis_size("seq"))
    pair_index = jnp.arange(pair_local, dtype=jnp.int32)
    target_dev = pair_index // capacity
    is_live = pair_index % capacity < pair_count[target_dev]
    slot_flat = target_dev * slot_count + pair_slot
    partner = slot_residue[slot_flat]
    left_global = my_index * res_local + pair_left
    right_global = target_dev * res_local + partner
    matrices = (couplings * is_live.astype(jnp.bfloat16)[:, None]).reshape(pair_local, Q, Q)
    own_states = lax.dynamic_slice_in_dim(alignment, my_index * res_local, res_local, 0)
    residues = jnp.arange(res_local, dtype=jnp.int32)
    per_block = max(1, min(res_devices, 256 // capacity))
    block_rows = per_block * capacity
    block_count = pair_local // block_rows

    def blockwise(array):
        return array.reshape((block_count, block_rows) + array.shape[1:])

    def field_pass(own_field, inputs):
        matrix, left_local, left_all, right_all, slot_ids = inputs
        right_hot = onehot(alignment[right_all])
        near_term = jnp.einsum(
            "pac,pcb->pab", matrix, right_hot, preferred_element_type=jnp.float32
        )
        select = (left_local[:, None] == residues[None, :]).astype(jnp.float32)
        own_field = own_field + jnp.einsum(
            "pr,pab->rab", select, near_term, precision=lax.Precision.HIGHEST
        )
        return (own_field, None)

    start_field = jnp.zeros((res_local, Q, seq_local), jnp.float32)
    own_field, slot_parts = lax.scan(
        field_pass,
        start_field,
        (
            blockwise(matrices),
            blockwise(pair_left),
            blockwise(left_global),
            blockwise(right_global),
            blockwise(pair_slot),
        ),
    )
    indices = jnp.stack((left_global, partner), axis=1).reshape(res_devices, capacity, 2)
    sent_blocks, sent_index = (
        lax.all_to_all(
            matrices.reshape(res_devices, capacity, Q * Q),
            "res",
            split_axis=0,
            concat_axis=0,
            tiled=True,
        ),
        lax.all_to_all(indices, "res", split_axis=0, concat_axis=0, tiled=True),
    )
    recv_blocks = sent_blocks.reshape(pair_local, Q, Q)
    recv_left = sent_index[:, :, 0].reshape(pair_local)
    recv_partner = sent_index[:, :, 1].reshape(pair_local)

    def partner_pass(field_acc, inputs):
        matrix, left_all, partner_ids = inputs
        left_hot = onehot(alignment[left_all])
        far_term = jnp.einsum("pac,pab->pcb", matrix, left_hot, preferred_element_type=jnp.float32)
        select = (partner_ids[:, None] == residues[None, :]).astype(jnp.float32)
        return (
            field_acc
            + jnp.einsum("pr,pcb->rcb", select, far_term, precision=lax.Precision.HIGHEST),
            None,
        )

    field_sum, unused = lax.scan(
        partner_pass,
        own_field,
        (blockwise(recv_blocks), blockwise(recv_left), blockwise(recv_partner)),
    )
    logits = field_sum + fields[:, :, None]
    softmax_out = jax.nn.softmax(logits, axis=1)
    own_hot = onehot(own_states).astype(jnp.float32)
    residual = (seq_weights[None, None, :] * (softmax_out - own_hot)).astype(jnp.bfloat16)
    field_part = grad_scale * jnp.sum(residual.astype(jnp.float32), axis=2)

    def remote_grad(inputs):
        left_all, partner_ids = inputs
        return jnp.einsum(
            "pab,pcb->pac",
            onehot(alignment[left_all]),
            residual[partner_ids],
            preferred_element_type=jnp.float32,
        )

    remote_part = lax.map(remote_grad, (blockwise(recv_left), blockwise(recv_partner))).reshape(
        res_devices, capacity, Q * Q
    )
    remote_back = (
        lax.all_to_all(shortened(remote_part), "res", split_axis=0, concat_axis=0, tiled=True)
        .astype(remote_part.dtype)
        .reshape(pair_local, Q, Q)
    )

    def local_grad(inputs):
        left_local, right_all = inputs
        return jnp.einsum(
            "pab,pcb->pac",
            residual[left_local],
            onehot(alignment[right_all]),
            preferred_element_type=jnp.float32,
        )

    gradient = (
        lax.map(local_grad, (blockwise(pair_left), blockwise(right_global))).reshape(
            pair_local, Q, Q
        )
        + remote_back
    )
    grad_total = (gradient * (grad_scale * is_live.astype(jnp.float32))[:, None, None]).reshape(
        pair_local, Q * Q
    )
    coupling_grad, field_grad = lax.psum((grad_total, field_part), "seq")
    return (coupling_grad, field_grad)


def solution(mesh):
    in_specs = (
        P(None, "seq"),
        P("seq"),
        P("res", None),
        P("res", None),
        P("res"),
        P("res"),
        P("res"),
        P("res"),
    )
    out_specs = (P("res", None), P("res", None))
    return jax.shard_map(
        per_device, mesh=mesh, in_specs=in_specs, out_specs=out_specs, check_vma=False
    )
```

profile of v0, /device:TPU:1, one launch (start us, length us, event | category | flops | bytes accessed | tf_op | source)
XLA Modules:
  0.0 288.6 jit_solution(1771594830436086423)
XLA Ops:
  7.9 3.5 %gather_fusion.6 = s32[512]{0:T(512)S(1)} fusion(s32[256]{0:T(256)S(1)} %copy-done, s32[1024]{0:T(1024)S(1)} %pad_clamp_fusion.6), kind=kCustom, calls=%fused_computation.6 | custom fusion | bytes 6144 | tf_op jit(solution)/shard_map/gather | solution.py:37
  13.2 13.0 %all-to-all-start = ((s32[64,8,2]{1,2,0:T(2,128)}), s32[64,8,2]{1,2,0:T(2,128)S(1)}, u32[]{:S(2)}, u32[]{:S(2)}) async-start(s32[64,8,2]{1,2,0:T(2,128)} %copy.65), calls=%async_computation | async-start | bytes 131072 | tf_op jit(solution)/shard_map/all_to_all | solution.py:83
  28.1 1.6 fusion.42
  29.7 2.1 fusion.41
  31.8 2.1 fusion.40
  33.9 2.1 fusion.39
  36.0 4.4 %compare_select_fusion.7 = s32[512,1]{0,1:T(1,128)S(1)} fusion(s32[]{:T(128)} %bitcast.67, s32[]{:T(128)} %bitcast.68, s32[]{:T(128)} %bitcast.69, s32[]{:T(128)} %bitcast.70, s32[]{:T(128)} %bitcast.71, s32[]{:T(128)} %bitcast.73, s32[]{:T(128)} %bitcast.72), kind=kLoop, calls=%fused_computation.122 | loop fusion | flops 11776 | bytes 2076 | tf_op jit(solution)/shard_map/gather | solution.py:35
  40.4 35.6 %broadcast_select_fusion = (f32[512]{0:T(512)S(1)}, pred[512]{0:T(512)(128)(4,1)S(1)}) fusion(pred[512]{0:T(512)(128)(4,1)S(1)} %compare_reduce_fusion, pred[512]{0:T(512)(128)(4,1)S(1)} %compare_reduce_fusion.1, pred[512]{0:T(512)(128)(4,1)S(1)} %compare_reduce_fusion.2, pred[512]{0:T(512)(128)(4,1)S(1)} %compare_reduce_fusion.3, ...), kind=kLoop, calls=%fused_computation.153 | loop fusion | flops 33280 | bytes 34020 | tf_op jit(solution)/shard_map/mul | solution.py:144
  76.0 1.8 broadcast_multiply_fusion
  77.8 2.5 reshape_reshape.9
  80.3 2.0 copy.66
  82.3 1.9 copy.64
  84.2 10.5 %all-to-all-start.1 = ((bf16[64,8,441]{2,1,0:T(8,128)(2,1)}), bf16[64,8,441]{2,1,0:T(8,128)(2,1)}, u32[]{:S(2)}, u32[]{:S(2)}) async-start(bf16[64,8,441]{2,1,0:T(8,128)(2,1)} %bitcast.175), calls=%async_computation.1 | async-start | bytes 1048576 | tf_op jit(solution)/shard_map/all_to_all | solution.py:76
  94.8 33.6 %while.49 = (s32[]{:T(128)}, f32[48,21,256]{2,0,1:T(8,128)}, s32[2,256]{1,0:T(2,128)S(1)}, bf16[2,256,21,21]{1,3,2,0:T(8,128)(2,1)}, s32[2,256]{1,0:T(2,128)S(1)}, /*index=5*/s32[3072,256]{1,0:T(8,128)S(1)}) while((s32[]{:T(128)}, f32[48,21,256]{2,0,1:T(8,128)}, s32[2,256]{1,0:T(2,128)S(1)}, ...), condition=%wide.region_1.2_spmd.clone.clone, body=%wide.region_0.1_spmd.clone.sunk.clone | while | flops 852432640 | bytes 15001187 | solution.py:63
  94.8 1.0 dynamic-slice_bitcast_fusion.7
  95.7 1.7 copy.92
  97.5 1.0 gather_fusion.5
  98.5 5.6 %fusion.81 = f32[256,21,256]{2,1,0:T(8,128)} fusion(bf16[256,21,21]{2,1,0:T(8,128)(2,1)} %copy.92, s32[256,256]{1,0:T(8,128)S(1)} %gather_fusion.5), kind=kOutput, calls=%fused_computation.39.clone.1.clone | convolution fusion | flops 59179008 | bytes 5992960 | tf_op jit(solution)/shard_map/while/body/eval_jaxpr/pac,pcb->pab/dot_general | solution.py:53
  104.1 7.4 %fusion.82 = f32[48,21,256]{2,0,1:T(8,128)} fusion(f32[256,21,256]{2,1,0:T(8,128)} %fusion.81, f32[48,21,256]{2,0,1:T(8,128)} %get-tuple-element.661, pred[]{:T(512)S(6)} %compare.233, s32[256]{0:T(256)S(1)} %bitcast.176), kind=kOutput, calls=%fused_computation.43.clone.1.clone | convolution fusion | flops 793251840 | bytes 7570433 | tf_op jit(solution)/shard_map/while/body/eval_jaxpr/pr,pab->rab/dot_general | solution.py:57
  111.5 1.0 dynamic-slice_bitcast_fusion.7
  112.4 1.7 copy.92
  114.2 1.0 gather_fusion.5
  115.2 5.6 %fusion.81 = f32[256,21,256]{2,1,0:T(8,128)} fusion(bf16[256,21,21]{2,1,0:T(8,128)(2,1)} %copy.92, s32[256,256]{1,0:T(8,128)S(1)} %gather_fusion.5), kind=kOutput, calls=%fused_computation.39.clone.1.clone | convolution fusion | flops 59179008 | bytes 5992960 | tf_op jit(solution)/shard_map/while/body/eval_jaxpr/pac,pcb->pab/dot_general | solution.py:53
  120.8 7.6 %fusion.82 = f32[48,21,256]{2,0,1:T(8,128)} fusion(f32[256,21,256]{2,1,0:T(8,128)} %fusion.81, f32[48,21,256]{2,0,1:T(8,128)} %get-tuple-element.661, pred[]{:T(512)S(6)} %compare.233, s32[256]{0:T(256)S(1)} %bitcast.176), kind=kOutput, calls=%fused_computation.43.clone.1.clone | convolution fusion | flops 793251840 | bytes 7570433 | tf_op jit(solution)/shard_map/while/body/eval_jaxpr/pr,pab->rab/dot_general | solution.py:57
  128.4 2.0 broadcast_convert_fusion
  130.8 4.6 %reshape_reshape.11 = bf16[2,256,21,21]{3,2,1,0:T(8,128)(2,1)} reshape(bf16[64,8,441]{2,1,0:T(8,128)(2,1)} %all-to-all-done.1) | data formatting | bytes 903168 | tf_op jit(solution)/shard_map/reshape;reshape | solution.py:48
  135.5 4.6 %copy.67 = bf16[2,256,21,21]{1,3,2,0:T(8,128)(2,1)} copy(bf16[2,256,21,21]{3,2,1,0:T(8,128)(2,1)} %reshape_reshape.11) | data formatting | bytes 903168
  140.1 23.7 %while.48 = (s32[]{:T(128)}, f32[48,21,256]{2,0,1:T(8,128)}, s32[2,256]{1,0:T(2,128)S(1)}, bf16[2,256,21,21]{1,3,2,0:T(8,128)(2,1)}, s32[2,256]{1,0:T(2,128)S(1)}, /*index=5*/s32[3072,256]{1,0:T(8,128)S(1)}) while((s32[]{:T(128)}, f32[48,21,256]{2,0,1:T(8,128)}, s32[2,256]{1,0:T(2,128)S(1)}, ...), condition=%wide.region_3.4_spmd.clone.clone, body=%wide.region_2.3_spmd.clone.sunk.clone | while | flops 852174592 | bytes 23258768 | solution.py:100
  140.1 1.0 dynamic-slice_bitcast_fusion.6
  141.1 1.8 copy.90
  142.9 1.0 gather_fusion.4
  143.9 3.0 %fusion.76 = f32[256,21,256]{2,1,0:T(8,128)S(1)} fusion(bf16[256,21,21]{1,2,0:T(8,128)(2,1)} %copy.90, s32[256,256]{1,0:T(8,128)S(1)} %gather_fusion.4), kind=kOutput, calls=%fused_computation.26.clone.1.clone | convolution fusion | flops 59179008 | bytes 5992960 | tf_op jit(solution)/shard_map/while/body/eval_jaxpr/pac,pab->pcb/dot_general | solution.py:92
  146.9 3.9 %fusion.77 = f32[48,21,256]{2,0,1:T(8,128)S(1)} fusion(f32[48,21,256]{2,0,1:T(8,128)S(1)} %copy-done.3, f32[256,21,256]{2,1,0:T(8,128)S(1)} %fusion.76, s32[256]{0:T(256)S(1)} %bitcast.177), kind=kOutput, calls=%fused_computation.30.clone.1.clone | convolution fusion | flops 792993792 | bytes 7570432 | tf_op jit(solution)/shard_map/while/body/eval_jaxpr/pr,pcb->rcb/dot_general | solution.py:96
  150.9 1.0 copy-done.4
  151.9 1.0 dynamic-slice_bitcast_fusion.6
  152.9 1.8 copy.90
  154.7 1.0 gather_fusion.4
  155.7 3.0 %fusion.76 = f32[256,21,256]{2,1,0:T(8,128)S(1)} fusion(bf16[256,21,21]{1,2,0:T(8,128)(2,1)} %copy.90, s32[256,256]{1,0:T(8,128)S(1)} %gather_fusion.4), kind=kOutput, calls=%fused_computation.26.clone.1.clone | convolution fusion | flops 59179008 | bytes 5992960 | tf_op jit(solution)/shard_map/while/body/eval_jaxpr/pac,pab->pcb/dot_general | solution.py:92
  158.7 3.9 %fusion.77 = f32[48,21,256]{2,0,1:T(8,128)S(1)} fusion(f32[48,21,256]{2,0,1:T(8,128)S(1)} %copy-done.3, f32[256,21,256]{2,1,0:T(8,128)S(1)} %fusion.76, s32[256]{0:T(256)S(1)} %bitcast.177), kind=kOutput, calls=%fused_computation.30.clone.1.clone | convolution fusion | flops 792993792 | bytes 7570432 | tf_op jit(solution)/shard_map/while/body/eval_jaxpr/pr,pcb->rcb/dot_general | solution.py:96
  162.7 1.0 copy-done.4
  163.7 2.2 add_reduce_fusion
  165.9 1.5 fusion.29
  167.4 1.7 convert_reduce_fusion
  169.3 19.0 %while.47 = (s32[]{:T(128)}, bf16[2,256,21,21]{3,2,1,0:T(8,128)(2,1)}, s32[2,256]{1,0:T(2,128)S(1)}, s32[3072,256]{1,0:T(8,128)}, s32[2,256]{1,0:T(2,128)S(1)}, /*index=5*/bf16[48,21,256]{2,1,0:T(8,128)(2,1)S(1)}) while((s32[]{:T(128)}, bf16[2,256,21,21]{3,2,1,0:T(8,128)(2,1)}, s32[2,256]{1,0:T(2,128)S(1)}, ...), condition=%wide.region_9.10_spmd.clone, body=%wide.region_8.9_spmd.sunk.clone | while | flops 59182592 | bytes 9905237 | solution.py:120
  169.4 2.4 gather_fusion.2
  171.8 2.9 gather_fusion.3
  174.7 4.2 %bitcast_dynamic-update-slice_fusion.7 = bf16[2,256,21,21]{3,2,1,0:T(8,128)(2,1)} fusion(bf16[2,256,21,21]{3,2,1,0:T(8,128)(2,1)} %get-tuple-element.715, s32[]{:T(128)S(6)} %copy.115, bf16[256,21,256]{2,1,0:T(8,128)(2,1)} %gather_fusion.2, s32[256,256]{1,0:T(8,128)S(1)} %gather_fusion.3), kind=kOutput, calls=%fused_computation.19.clone.1.clone | convolution fusion | flops 59179008 | bytes 3859460 | tf_op jit(solution)/shard_map/while/body/eval_jaxpr/pab,pcb->pac/dot_general | solution.py:113
  178.9 2.4 gather_fusion.2
  181.3 2.9 gather_fusion.3
  184.2 4.2 %bitcast_dynamic-update-slice_fusion.7 = bf16[2,256,21,21]{3,2,1,0:T(8,128)(2,1)} fusion(bf16[2,256,21,21]{3,2,1,0:T(8,128)(2,1)} %get-tuple-element.715, s32[]{:T(128)S(6)} %copy.115, bf16[256,21,256]{2,1,0:T(8,128)(2,1)} %gather_fusion.2, s32[256,256]{1,0:T(8,128)S(1)} %gather_fusion.3), kind=kOutput, calls=%fused_computation.19.clone.1.clone | convolution fusion | flops 59179008 | bytes 3859460 | tf_op jit(solution)/shard_map/while/body/eval_jaxpr/pab,pcb->pac/dot_general | solution.py:113
  188.3 4.6 %convert_element_type.38 = bf16[64,8,441]{2,1,0:T(8,128)(2,1)} reshape(bf16[2,256,21,21]{3,2,1,0:T(8,128)(2,1)} %get-tuple-element.143) | data formatting | bytes 903168 | tf_op jit(solution)/shard_map/convert_element_type | solution.py:12
  192.9 10.3 %all-to-all-start.2 = ((bf16[64,8,441]{2,1,0:T(8,128)(2,1)}), bf16[64,8,441]{2,1,0:T(8,128)(2,1)S(1)}, u32[]{:S(2)}, u32[]{:S(2)}) async-start(bf16[64,8,441]{2,1,0:T(8,128)(2,1)} %convert_element_type.38), calls=%async_computation.2 | async-start | bytes 1048576 | tf_op jit(solution)/shard_map/all_to_all | solution.py:124
  203.3 20.3 %while.46 = (s32[]{:T(128)}, f32[2,256,21,21]{3,2,1,0:T(8,128)}, s32[2,256]{1,0:T(2,128)S(1)}, bf16[48,21,256]{2,1,0:T(8,128)(2,1)S(1)}, s32[2,256]{1,0:T(2,128)S(1)}, /*index=5*/s32[3072,256]{1,0:T(8,128)}) while((s32[]{:T(128)}, f32[2,256,21,21]{3,2,1,0:T(8,128)}, s32[2,256]{1,0:T(2,128)S(1)}, ...), condition=%wide.region_7.8_spmd.clone, body=%wide.region_6.7_spmd.sunk.clone | while | flops 59182592 | bytes 12599381 | solution.py:139
  203.6 2.4 gather_fusion
  206.0 2.9 gather_fusion.1
  208.9 4.7 %bitcast_dynamic-update-slice_fusion.6 = f32[2,256,21,21]{3,2,1,0:T(8,128)} fusion(f32[2,256,21,21]{3,2,1,0:T(8,128)} %get-tuple-element.697, s32[]{:T(128)S(6)} %copy.109, bf16[256,21,256]{2,1,0:T(8,128)(2,1)} %gather_fusion, s32[256,256]{1,0:T(8,128)S(1)} %gather_fusion.1), kind=kOutput, calls=%fused_computation.11.clone.1.clone | convolution fusion | flops 59179008 | bytes 6553604 | tf_op jit(solution)/shard_map/while/body/eval_jaxpr/pab,pcb->pac/dot_general | solution.py:131
  213.6 2.4 gather_fusion
  216.0 2.9 gather_fusion.1
  218.8 4.7 %bitcast_dynamic-update-slice_fusion.6 = f32[2,256,21,21]{3,2,1,0:T(8,128)} fusion(f32[2,256,21,21]{3,2,1,0:T(8,128)} %get-tuple-element.697, s32[]{:T(128)S(6)} %copy.109, bf16[256,21,256]{2,1,0:T(8,128)(2,1)} %gather_fusion, s32[256,256]{1,0:T(8,128)S(1)} %gather_fusion.1), kind=kOutput, calls=%fused_computation.11.clone.1.clone | convolution fusion | flops 59179008 | bytes 6553604 | tf_op jit(solution)/shard_map/while/body/eval_jaxpr/pab,pcb->pac/dot_general | solution.py:131
  223.6 4.2 %reshape.572 = f32[512,441]{1,0:T(8,128)S(1)} reshape(f32[2,256,21,21]{3,2,1,0:T(8,128)} %get-tuple-element.142) | data formatting | bytes 1806336 | tf_op jit(solution)/shard_map/reshape | solution.py:139
  228.6 1.1 add_multiply_fusion
  229.8 13.9 %psum.15 = f32[48,21]{0,1:T(8,128)} all-reduce(f32[48,21]{0,1:T(8,128)S(1)} %broadcast_multiply_fusion.1), channel_id=1, replica_groups=mesh['seq'=4,'res'=64] {'seq'}, use_global_device_ids=true, to_apply=%region_12.13 | all-reduce | flops 1008 | bytes 8064 | tf_op jit(solution)/shard_map/psum | solution.py:147
  243.7 35.9 %all-reduce.2.cloned.1.call-done = f32[512,441]{0,1:T(8,128)} async-done(((f32[512,441]{0,1:T(8,128)}), f32[512,441]{0,1:T(8,128)}) %all-reduce.2.cloned.1.call-update) | async-done | bytes 903184 | tf_op jit(solution)/shard_map/psum | solution.py:147
  279.6 2.2 copy.121
  (126 shorter events, 6.0 us)
Async XLA Ops:
  7.2 0.7 copy-start
  7.2 70.6 %copy-start.6 = (s32[512]{0:T(512)S(1)}, s32[512]{0:T(512)}, u32[]{:S(2)}) copy-start(s32[512]{0:T(512)} %param.20) | copy-start | bytes 6148
  11.4 83.3 %copy-start.1 = (s32[3072,256]{1,0:T(8,128)S(1)}, s32[3072,256]{1,0:T(8,128)}, u32[]{:S(2)}) copy-start(s32[3072,256]{1,0:T(8,128)} %param.16) | copy-start | bytes 9437188
  13.2 71.1 %all-to-all-start = ((s32[64,8,2]{1,2,0:T(2,128)}), s32[64,8,2]{1,2,0:T(2,128)S(1)}, u32[]{:S(2)}, u32[]{:S(2)}) async-start(s32[64,8,2]{1,2,0:T(2,128)} %copy.65), calls=%async_computation | async-start | bytes 131072 | tf_op jit(solution)/shard_map/all_to_all | solution.py:83
  84.2 46.6 %all-to-all-start.1 = ((bf16[64,8,441]{2,1,0:T(8,128)(2,1)}), bf16[64,8,441]{2,1,0:T(8,128)(2,1)}, u32[]{:S(2)}, u32[]{:S(2)}) async-start(bf16[64,8,441]{2,1,0:T(8,128)(2,1)} %bitcast.175), calls=%async_computation.1 | async-start | bytes 1048576 | tf_op jit(solution)/shard_map/all_to_all | solution.py:76
  140.1 23.7 %copy-start.5 = (f32[48,21]{0,1:T(8,128)S(1)}, f32[48,21]{0,1:T(8,128)}, u32[]{:S(2)}) copy-start(f32[48,21]{0,1:T(8,128)} %param.18) | copy-start | bytes 12100
  140.1 27.3 %copy-start.7 = (f32[256]{0:T(256)S(1)}, f32[256]{0:T(256)}, u32[]{:S(2)}) copy-start(f32[256]{0:T(256)} %param.17) | copy-start | bytes 3076
  143.9 3.1 %copy-start.3 = (f32[48,21,256]{2,0,1:T(8,128)S(1)}, f32[48,21,256]{2,0,1:T(8,128)}, u32[]{:S(2)}) copy-start(f32[48,21,256]{2,0,1:T(8,128)} %get-tuple-element.679) | copy-start | bytes 3096580 | tf_op jit(solution)/shard_map/while
  150.9 1.1 copy-start.4
  155.7 3.1 %copy-start.3 = (f32[48,21,256]{2,0,1:T(8,128)S(1)}, f32[48,21,256]{2,0,1:T(8,128)}, u32[]{:S(2)}) copy-start(f32[48,21,256]{2,0,1:T(8,128)} %get-tuple-element.679) | copy-start | bytes 3096580 | tf_op jit(solution)/shard_map/while
  162.7 1.1 copy-start.4
  163.7 5.4 %copy-start.2 = (s32[3072,256]{1,0:T(8,128)}, s32[3072,256]{1,0:T(8,128)S(1)}, u32[]{:S(2)}) copy-start(s32[3072,256]{1,0:T(8,128)S(1)} %get-tuple-element.731) | copy-start | bytes 9437188
  192.9 35.2 %all-to-all-start.2 = ((bf16[64,8,441]{2,1,0:T(8,128)(2,1)}), bf16[64,8,441]{2,1,0:T(8,128)(2,1)S(1)}, u32[]{:S(2)}, u32[]{:S(2)}) async-start(bf16[64,8,441]{2,1,0:T(8,128)(2,1)} %convert_element_type.38), calls=%async_computation.2 | async-start | bytes 1048576 | tf_op jit(solution)/shard_map/all_to_all | solution.py:124
  203.3 76.3 %all-reduce.2.cloned.1.call-start = ((), (), s32[]{:S(2)}) async-start(), calls=%async_computation.3 | async-start | bytes 1835008 | tf_op jit(solution)/shard_map/psum | solution.py:147
Sparse Core Ops, SparseCore 0:
  229.9 49.6 all-reduce.1
where the time goes:
time: 292 us; the launch traced here: 289 us
  local copies, waits for them, and re-layouts  78.1 us (27%)
  matrix products  57.9 us (20%)
  other arithmetic  54.1 us (19%)
  waiting for transfers between devices  35.9 us (12%)
  starting transfers between devices  33.9 us (12%)
  between operations  14.3 us (5%)
  blocking collectives  13.9 us (5%)
    psum x1, waiting for transfers between devices, per_device(): coupling_grad, field_grad = lax.psum((grad_total, field_part), 'seq')  35.9 us
    mul x1, other arithmetic, per_device(): grad_scale * is_live.astype(jnp.float32)  35.6 us
    dot_general x2, matrix products, field_pass(): jnp.einsum('pr,pab->rab', select, near_term, precision=lax.Precision.HIGH...  15 us
    psum x1, blocking collectives, per_device(): coupling_grad, field_grad = lax.psum((grad_total, field_part), 'seq')  13.9 us
    all_to_all x1, starting transfers between devices, per_device(): lax.all_to_all(indices, 'res', split_axis=0, concat_axis=0, tiled=True)  13 us
    dot_general x2, matrix products, field_pass(): jnp.einsum('pac,pcb->pab', matrix, right_hot, preferred_element_type=jnp....  11.2 us
    squeeze x8, local copies, waits for them, and re-layouts, per_device(): lax.scan(field_pass, start_field, (blockwise(matrices), blockwise(pair_le...  11 us
    all_to_all x1, starting transfers between devices, per_device(): lax.all_to_all(matrices.reshape(res_devices, capacity, Q * Q), 'res', spl...  10.5 us
  transfers between devices with their start and end apart: 4, of which 1 were waited for; matrix products, arithmetic and copies ran while one was open for 41% of the time, Pallas kernels for 0%

commit v1 on v0

v1 whole, which is shorter than its diff:
```python
import functools

import jax
import jax.numpy as jnp
from jax import lax
from jax.experimental import pallas as pl
from jax.experimental.pallas import tpu as pltpu
from jax.sharding import PartitionSpec as P

Q = 21
QP = 24
RL = 48
CAP = 8
SLOTS = 4
PAIRS = 512
BLOCKS = 64
SEQ = 256
RES = 3072
TILE = 128
TILES = PAIRS // TILE
GROUP = 8
GROUPS = RL // GROUP
GROWS = GROUP * QP
QUARTER = 112
PADQ = 4 * QUARTER
DEEP = Q * TILE
F32 = jnp.float32
BF16 = jnp.bfloat16
VMEM = pl.BlockSpec(memory_space=pltpu.VMEM)
SMEM = pl.BlockSpec(memory_space=pltpu.SMEM)
PARAMS = pltpu.CompilerParams(vmem_limit_bytes=56 * 1024 * 1024)


def iota(shape, dim):
    return lax.broadcasted_iota(jnp.int32, shape, dim)


def dot(x, y):
    return jnp.dot(x, y, preferred_element_type=F32)


def pack_kernel(ids, coup, left, slot, table, out, wide, tall):
    wide[...] = jnp.zeros_like(wide)
    wide[0 : Q * Q, :] = coup[...].astype(F32)
    start = pl.multiple_of(ids[0] * QUARTER, 8)
    tall[0:QUARTER, :] = wide[pl.ds(start, QUARTER), :]
    bucket = iota((BLOCKS, PAIRS), 1) // CAP
    spread = (bucket == iota((BLOCKS, PAIRS), 0)).astype(F32).astype(BF16)
    rows = dot(table[...], spread)
    slots = slot[...]
    partner = jnp.zeros((1, PAIRS), F32)
    for s in range(SLOTS):
        partner = partner + jnp.where(slots == s, rows[s : s + 1], 0.0)
    lane = iota((1, PAIRS), 1)
    live = jnp.where((lane % CAP).astype(F32) < rows[SLOTS : SLOTS + 1], 1.0, 0.0)
    sub = iota((16, PAIRS), 0)
    index = jnp.where(sub == 0, left[...].astype(F32), 0.0)
    index = jnp.where(sub == 1, partner, index)
    index = jnp.where(sub == 2, live, index)
    index = jnp.where(sub == 3, ids[1].astype(F32), index)
    index = jnp.where(sub == 4, (lane // CAP).astype(F32), index)
    tall[QUARTER:TILE, :] = index
    out[...] = jnp.transpose(tall[...]).astype(BF16)


def pack_pairs(ids, coup, left, slot, table):
    return pl.pallas_call(
        pack_kernel,
        out_shape=jax.ShapeDtypeStruct((PAIRS, TILE), BF16),
        in_specs=[SMEM, VMEM, VMEM, VMEM, VMEM],
        out_specs=VMEM,
        scratch_shapes=[pltpu.VMEM((PADQ, PAIRS), F32), pltpu.VMEM((TILE, PAIRS), F32)],
        compiler_params=PARAMS,
        name="pack_pairs",
    )(ids, coup, left, slot, table)


def order_half(pack, flipped, own):
    mine, other, block = (112, 113, 116) if own else (113, 112, 115)
    wide = pack.astype(F32)
    key_row = jnp.where(flipped[114:115] > 0.5, flipped[mine : mine + 1], float(RL))
    key_col = jnp.where(wide[:, 114:115] > 0.5, wide[:, mine : mine + 1], float(RL))
    lane = iota((PAIRS, PAIRS), 1).astype(F32)
    sub = iota((PAIRS, PAIRS), 0).astype(F32)
    full_row = key_row * PAIRS + lane
    full_col = key_col * PAIRS + sub
    place_row = jnp.sum(jnp.where(full_col < full_row, 1.0, 0.0), axis=0, keepdims=True)
    place_col = jnp.sum(jnp.where(full_row < full_col, 1.0, 0.0), axis=1, keepdims=True)
    to_sorted = jnp.where(place_col == lane, 1.0, 0.0).astype(BF16)
    to_plain = jnp.where(place_row == sub, 1.0, 0.0).astype(BF16)
    cols = dot(to_plain, pack)
    far = cols[:, block : block + 1] * RL + cols[:, other : other + 1]
    keys = dot(jnp.broadcast_to(key_row, (8, PAIRS)).astype(BF16), to_sorted)
    return to_sorted, to_plain, far, keys


def fill_hot(far, states, hot):
    far_states = jnp.zeros((PAIRS, SEQ), F32)
    chunk = 256
    lane = iota((PAIRS, chunk), 1).astype(F32)
    for n in range(RES // chunk):
        pick = jnp.where(far - float(n * chunk) == lane, 1.0, 0.0).astype(BF16)
        far_states = far_states + dot(pick, states[n * chunk : (n + 1) * chunk, :])
    for c in range(Q):
        hit = jnp.where(far_states == float(c), 1.0, 0.0).astype(BF16)
        for j in range(TILES):
            hot[j, c * TILE : (c + 1) * TILE, :] = hit[j * TILE : (j + 1) * TILE]


def store_keys(keys, keys_ref):
    for j in range(TILES):
        keys_ref[j] = keys[:, j * TILE : (j + 1) * TILE]


def group_range(keys):
    low = jnp.min(keys).astype(jnp.int32)
    high = jnp.max(jnp.where(keys < RL - 0.5, keys, -1.0)).astype(jnp.int32)
    return lax.shift_right_logical(low, 3), lax.shift_right_logical(high + 8, 3)


def group_masks(keys, g):
    base = (g * GROUP).astype(F32)
    wide = jnp.broadcast_to(keys[0:1], (QP, TILE))
    return [wide == base + float(m) for m in range(GROUP)]


def add_field(keys_ref, blocks, hot, lhs, field):
    def tile_step(j, carry):
        keys = keys_ref[j]
        low, high = group_range(keys)

        def group_step(g, carry):
            masks = group_masks(keys, g)
            for c in range(Q):
                block = blocks[j, c]
                rows = [jnp.where(mask, block, 0.0) for mask in masks]
                lhs[:, c * TILE : (c + 1) * TILE] = jnp.concatenate(rows, axis=0).astype(BF16)
            field[g] += dot(lhs[...], hot[j])
            return carry

        return lax.fori_loop(low, high, group_step, carry)

    lax.fori_loop(0, TILES, tile_step, 0)


def add_grad(keys_ref, resid, hot, grad):
    grad[...] = jnp.zeros_like(grad)

    def tile_step(j, carry):
        keys = keys_ref[j]
        low, high = group_range(keys)

        def group_step(g, carry):
            masks = group_masks(keys, g)
            rows = resid[g]
            for c in range(0, Q, 2):
                count = min(2, Q - c)
                part = hot[j, c * TILE : (c + count) * TILE, :]
                out = lax.dot_general(
                    rows, part, (((1,), (1,)), ((), ())), preferred_element_type=F32
                )
                for i in range(count):
                    total = grad[j, c + i]
                    for m in range(GROUP):
                        piece = out[m * QP : (m + 1) * QP, i * TILE : (i + 1) * TILE]
                        total = jnp.where(masks[m], piece, total)
                    grad[j, c + i] = total
            return carry

        return lax.fori_loop(low, high, group_step, carry)

    lax.fori_loop(0, TILES, tile_step, 0)


def own_field_kernel(
    alignment, pack, coup, states, hot, to_plain_out, keys_ref, field, sorted_blocks, blocks, lhs
):
    for n in range(RES // 256):
        rows = slice(n * 256, (n + 1) * 256)
        states[rows, :] = alignment[rows, :].astype(F32).astype(BF16)
    packed = pack[...]
    flipped = jnp.transpose(packed.astype(F32))
    to_sorted, to_plain, far, keys = order_half(packed, flipped, True)
    to_plain_out[...] = to_plain
    store_keys(keys, keys_ref)
    sorted_blocks[...] = jnp.zeros_like(sorted_blocks)
    ordered = dot(coup[...], to_sorted)
    for j in range(TILES):
        sorted_blocks[j, 0 : Q * Q, :] = ordered[:, j * TILE : (j + 1) * TILE]
    for c in range(Q):
        for j in range(TILES):
            blocks[j, c] = sorted_blocks[j, pl.ds(c, QP, stride=Q), :]
    fill_hot(far, states, hot)
    field[...] = jnp.zeros_like(field)
    add_field(keys_ref, blocks, hot, lhs, field)


def own_field(alignment, pack, coup):
    return pl.pallas_call(
        own_field_kernel,
        out_shape=(
            jax.ShapeDtypeStruct((RES, SEQ), BF16),
            jax.ShapeDtypeStruct((TILES, DEEP, SEQ), BF16),
            jax.ShapeDtypeStruct((PAIRS, PAIRS), BF16),
            jax.ShapeDtypeStruct((TILES, 8, TILE), F32),
            jax.ShapeDtypeStruct((GROUPS, GROWS, SEQ), F32),
        ),
        in_specs=[VMEM] * 3,
        out_specs=(VMEM,) * 5,
        scratch_shapes=[
            pltpu.VMEM((TILES, 512, TILE), F32),
            pltpu.VMEM((TILES, Q, QP, TILE), F32),
            pltpu.VMEM((GROWS, DEEP), BF16),
        ],
        compiler_params=PARAMS,
        cost_estimate=pl.CostEstimate(
            flops=20_000_000_000, bytes_accessed=10_000_000, transcendentals=0
        ),
        name="own_field",
    )(alignment, pack, coup)


def recv_kernel(
    ids, q0, q1, q2, q3, states, own, fields, weights,
    grad_out, resid_out, field_out,
    wide, sorted_blocks, blocks, hot, lhs, field, grad, keys_ref,
):
    for back, part in enumerate((q0, q1, q2, q3)):
        flipped = jnp.transpose(part[...].astype(F32))
        owner = lax.rem(ids[0] + (4 - back), 4)
        wide[pl.ds(pl.multiple_of(owner * QUARTER, 8), QUARTER), :] = flipped[0:QUARTER]
        if back == 0:
            first = flipped
    to_sorted, to_plain, far, keys = order_half(q0[...], first, False)
    store_keys(keys, keys_ref)
    sorted_blocks[PADQ:512, :] = jnp.zeros((512 - PADQ, PAIRS), F32)
    sorted_blocks[0:PADQ, :] = dot(wide[...].astype(BF16), to_sorted)
    for a in range(Q):
        for j in range(TILES):
            blocks[j, a] = sorted_blocks[a * Q : a * Q + QP, j * TILE : (j + 1) * TILE]
    fill_hot(far, states, hot)
    field[...] = own[...]
    add_field(keys_ref, blocks, hot, lhs, field)

    my_states = states[pl.ds(pl.multiple_of(ids[1] * RL, 16), RL), :].astype(F32)
    state = iota((QP, SEQ), 0)
    valid = state < Q
    state = state.astype(F32)
    weight = weights[...]
    lane = iota((QP, TILE), 1)
    field_part = jnp.zeros((QP, TILE), F32)
    for g in range(GROUPS):
        pieces = []
        for m in range(GROUP):
            r = g * GROUP + m
            logits = field[g, m * QP : (m + 1) * QP, :] + fields[:, r : r + 1]
            logits = jnp.where(valid, logits, -1e30)
            top = jnp.max(logits, axis=0, keepdims=True)
            raised = jnp.exp(logits - top)
            soft = raised / jnp.sum(raised, axis=0, keepdims=True)
            hot_own = jnp.where(state == my_states[r : r + 1], 1.0, 0.0)
            rounded = (weight * (soft - hot_own)).astype(BF16).astype(F32)
            pieces.append(rounded)
            field_part = jnp.where(lane == r, jnp.sum(rounded, axis=1, keepdims=True), field_part)
        resid_out[g] = jnp.concatenate(pieces, axis=0).astype(BF16)
    field_out[...] = field_part

    add_grad(keys_ref, resid_out, hot, grad)
    wide[Q * Q // 8 * 8 : PADQ, :] = jnp.zeros((PADQ - Q * Q // 8 * 8, PAIRS), F32)
    for a in range(Q):
        for j in range(TILES):
            wide[a * Q : (a + 1) * Q, j * TILE : (j + 1) * TILE] = grad[j, a, 0:Q]
    grad_out[...] = dot(wide[...].astype(BF16), to_plain).astype(BF16)


def recv_half(ids, parts, states, own, fields, weights):
    return pl.pallas_call(
        recv_kernel,
        out_shape=(
            jax.ShapeDtypeStruct((PADQ, PAIRS), BF16),
            jax.ShapeDtypeStruct((GROUPS, GROWS, SEQ), BF16),
            jax.ShapeDtypeStruct((QP, TILE), F32),
        ),
        in_specs=[SMEM] + [VMEM] * 8,
        out_specs=(VMEM,) * 3,
        scratch_shapes=[
            pltpu.VMEM((PADQ, PAIRS), F32),
            pltpu.VMEM((512, PAIRS), F32),
            pltpu.VMEM((TILES, Q, QP, TILE), F32),
            pltpu.VMEM((TILES, DEEP, SEQ), BF16),
            pltpu.VMEM((GROWS, DEEP), BF16),
            pltpu.VMEM((GROUPS, GROWS, SEQ), F32),
            pltpu.VMEM((TILES, Q, QP, TILE), F32),
            pltpu.VMEM((TILES, 8, TILE), F32),
        ],
        compiler_params=PARAMS,
        cost_estimate=pl.CostEstimate(
            flops=20_000_000_000, bytes_accessed=10_000_000, transcendentals=0
        ),
        name="recv_half",
    )(ids, *parts, states, own, fields, weights)


def own_grad_kernel(keys_ref, to_plain, hot, resid, grad_out, grad, wide):
    add_grad(keys_ref, resid, hot, grad)
    total = jnp.zeros((PADQ, PAIRS), F32)
    for j in range(TILES):
        wide[j, Q * Q // 8 * 8 : PADQ, :] = jnp.zeros((PADQ - Q * Q // 8 * 8, TILE), F32)
        for c in range(Q):
            wide[j, pl.ds(c, Q, stride=Q), :] = grad[j, c, 0:Q]
        total = total + dot(wide[j].astype(BF16), to_plain[j * TILE : (j + 1) * TILE, :])
    grad_out[...] = total.astype(BF16)


def own_grad(keys, to_plain, hot, resid):
    return pl.pallas_call(
        own_grad_kernel,
        out_shape=jax.ShapeDtypeStruct((PADQ, PAIRS), BF16),
        in_specs=[VMEM] * 4,
        out_specs=VMEM,
        scratch_shapes=[
            pltpu.VMEM((TILES, Q, QP, TILE), F32),
            pltpu.VMEM((TILES, PADQ, TILE), F32),
        ],
        compiler_params=PARAMS,
        cost_estimate=pl.CostEstimate(
            flops=12_000_000_000, bytes_accessed=8_000_000, transcendentals=0
        ),
        name="own_grad",
    )(keys, to_plain, hot, resid)


def back_kernel(mine, r1, r2, r3, out, tall):
    total = mine[...].astype(F32) + r1[...].astype(F32)
    total = total + (r2[...].astype(F32) + r3[...].astype(F32))
    tall[0:QUARTER, :] = total
    tall[QUARTER:TILE, :] = jnp.zeros((TILE - QUARTER, PAIRS), F32)
    out[...] = jnp.transpose(tall[...]).astype(BF16)


def sum_back(chunks):
    return pl.pallas_call(
        back_kernel,
        out_shape=jax.ShapeDtypeStruct((PAIRS, TILE), BF16),
        in_specs=[VMEM] * 4,
        out_specs=VMEM,
        scratch_shapes=[pltpu.VMEM((TILE, PAIRS), F32)],
        compiler_params=PARAMS,
        name="sum_back",
    )(*chunks)


def join_kernel(scale, mine, r1, r2, r3, remote, out):
    total = mine[...].astype(F32) + r1[...].astype(F32)
    total = total + (r2[...].astype(F32) + r3[...].astype(F32))
    flipped = jnp.transpose(remote[...].astype(F32))
    out[...] = (total + flipped[0:QUARTER]) * scale


def join_parts(scale, chunks, remote):
    return pl.pallas_call(
        functools.partial(join_kernel, scale),
        out_shape=jax.ShapeDtypeStruct((QUARTER, PAIRS), F32),
        in_specs=[VMEM] * 5,
        out_specs=VMEM,
        compiler_params=PARAMS,
        name="join_parts",
    )(*chunks, remote)


def place_kernel(scale, ids, c0, c1, c2, c3, f0, f1, f2, f3, out, field_out, wide):
    for back, part in enumerate((c0, c1, c2, c3)):
        owner = lax.rem(ids[0] + (4 - back), 4)
        wide[pl.ds(pl.multiple_of(owner * QUARTER, 8), QUARTER), :] = part[...]
    out[...] = wide[0 : Q * Q, :]
    field_out[...] = ((f0[...] + f1[...]) + (f2[...] + f3[...])) * scale


def place_parts(scale, ids, chunks, field_parts):
    return pl.pallas_call(
        functools.partial(place_kernel, scale),
        out_shape=(
            jax.ShapeDtypeStruct((Q * Q, PAIRS), F32),
            jax.ShapeDtypeStruct((QP, TILE), F32),
        ),
        in_specs=[SMEM] + [VMEM] * 8,
        out_specs=(VMEM, VMEM),
        scratch_shapes=[pltpu.VMEM((PADQ, PAIRS), F32)],
        compiler_params=PARAMS,
        name="place_parts",
    )(ids, *chunks, *field_parts)


def shifted(array, k):
    return lax.ppermute(array, "seq", [(i, (i + k) % 4) for i in range(4)])


def gather_seq(array):
    return [array] + [shifted(array, k) for k in (1, 2, 3)]


def scatter_seq(array, seq_index):
    def quarter(k):
        start = lax.rem(seq_index + k, 4) * QUARTER
        return lax.dynamic_slice_in_dim(array, start, QUARTER, 0)

    return [quarter(0)] + [shifted(quarter(k), k) for k in (1, 2, 3)]


def swap_blocks(array):
    blocks = array.reshape(BLOCKS, CAP, TILE)
    moved = lax.all_to_all(blocks, "res", split_axis=0, concat_axis=0, tiled=True)
    return moved.reshape(PAIRS, TILE)


def per_device(
    alignment, seq_weights, fields, couplings, pair_left, pair_slot, slot_residue, pair_count
):
    seq_index = lax.axis_index("seq")
    res_index = lax.axis_index("res")
    ids = jnp.stack([seq_index, res_index]).astype(jnp.int32)
    scale = Q / (SEQ * 4)
    coup = couplings.T
    table = jnp.concatenate(
        [slot_residue.reshape(BLOCKS, SLOTS).T, pair_count[None, :], jnp.zeros((3, BLOCKS), jnp.int32)]
    ).astype(BF16)
    pack = pack_pairs(ids, coup, pair_left[None, :], pair_slot[None, :], table)
    received = swap_blocks(pack)
    states, hot, to_plain, keys, field = own_field(alignment, pack, coup)
    parts = gather_seq(received)
    fields_t = jnp.pad(fields.T, ((0, QP - Q), (0, 0)))
    remote_grad, resid, field_part = recv_half(
        ids, parts, states, field, fields_t, seq_weights[None, :]
    )
    field_parts = gather_seq(field_part)
    remote_chunks = scatter_seq(remote_grad, seq_index)
    local_grad = own_grad(keys, to_plain, hot, resid)
    remote = swap_blocks(sum_back(remote_chunks))
    local_chunks = scatter_seq(local_grad, seq_index)
    joined = gather_seq(join_parts(scale, local_chunks, remote))
    coupling_grad, field_grad = place_parts(scale, ids, joined, field_parts)
    return coupling_grad.T, field_grad[:Q, :RL].T


def solution(mesh):
    in_specs = (
        P(None, "seq"),
        P("seq"),
        P("res", None),
        P("res", None),
        P("res"),
        P("res"),
        P("res"),
        P("res"),
    )
    out_specs = (P("res", None), P("res", None))
    return jax.shard_map(
        per_device, mesh=mesh, in_specs=in_specs, out_specs=out_specs, check_vma=False
    )
```

time: 292 us -> 133 us (0.46)
  local copies, waits for them, and re-layouts: 78.1 us -> 9.18 us
  matrix products: 57.9 us -> 0 us
  other arithmetic: 54.1 us -> 2.66 us
  Pallas kernels: 0 us -> 51.2 us
  waiting for transfers between devices: 35.9 us -> 15.3 us
  between operations: 14.3 us -> 0.77 us
  blocking collectives: 13.9 us -> 23.3 us
  starting transfers between devices: 33.9 us -> 28.9 us
    dot_general x12 -> x0, matrix products: 57.9 us -> none  [the longest x2 15 us: field_pass(): jnp.einsum('pr,pab->rab', select, near_term, precision=lax.Precision.HIGH...]
    pallas_call x0 -> x7, Pallas kernels: none -> 51.2 us  [the longest x1 20.4 us: recv_half(): pl.pallas_call(recv_kernel, out_shape=(jax.ShapeDtypeStruct((PADQ, PAIRS)...]
    mul x4 -> x0, other arithmetic: 38.5 us -> none  [the longest x1 35.6 us: per_device(): grad_scale * is_live.astype(jnp.float32)]
    gather x18 -> x0, local copies, waits for them, and re-layouts: 36.3 us -> none  [the longest x4 7.8 us: per_device(): is_live = pair_index % capacity < pair_count[target_dev]]
    psum x1 -> x0, waiting for transfers between devices: 35.9 us -> none  [per_device(): coupling_grad, field_grad = lax.psum((grad_total, field_part), 'seq')]
    all_to_all x3 -> x1, starting transfers between devices: 33.8 us -> 7.12 us  [swap_blocks(): lax.all_to_all(blocks, 'res', split_axis=0, concat_axis=0, tiled=True)]
    all_to_all x0 -> x1, blocking collectives: none -> 23.3 us  [swap_blocks(): lax.all_to_all(blocks, 'res', split_axis=0, concat_axis=0, tiled=True)]
    ppermute x0 -> x15, starting transfers between devices: none -> 21.7 us  [shifted(): return lax.ppermute(array, 'seq', [(i, (i + k) % 4) for i in range(4)])]
  transfers between devices with their start and end apart: 4 -> 16, of which waited for: 1 -> 6; matrix products, arithmetic and copies ran while one was open for 41% -> 2% of each run, Pallas kernels for 0% -> 17%
where the time goes in v1:
time: 133 us; the launch traced here: 131 us
  Pallas kernels  51.2 us (38%)
  starting transfers between devices  28.9 us (22%)
  blocking collectives  23.3 us (18%)
  waiting for transfers between devices  15.3 us (12%)
  local copies, waits for them, and re-layouts  9.18 us (7%)
  other arithmetic  2.66 us (2%)
    all_to_all x1, blocking collectives, swap_blocks(): lax.all_to_all(blocks, 'res', split_axis=0, concat_axis=0, tiled=True)  23.3 us
    ppermute x15, starting transfers between devices, shifted(): return lax.ppermute(array, 'seq', [(i, (i + k) % 4) for i in range(4)])  21.7 us
    pallas_call x1, Pallas kernels, recv_half(): pl.pallas_call(recv_kernel, out_shape=(jax.ShapeDtypeStruct((PADQ, PAIRS)...  20.4 us
    ppermute x15, waiting for transfers between devices, shifted(): return lax.ppermute(array, 'seq', [(i, (i + k) % 4) for i in range(4)])  15.3 us
    pallas_call x1, Pallas kernels, own_field(): pl.pallas_call(own_field_kernel, out_shape=(jax.ShapeDtypeStruct((RES, SE...  13 us
    pallas_call x1, Pallas kernels, own_grad(): pl.pallas_call(own_grad_kernel, out_shape=jax.ShapeDtypeStruct((PADQ, PAI...  9.78 us
    all_to_all x1, starting transfers between devices, swap_blocks(): lax.all_to_all(blocks, 'res', split_axis=0, concat_axis=0, tiled=True)  7.12 us
    unnamed x38, local copies, waits for them, and re-layouts  3.52 us
  transfers between devices with their start and end apart: 16, of which 6 were waited for; matrix products, arithmetic and copies ran while one was open for 2% of the time, Pallas kernels for 17%

profile of v1, /device:TPU:1, one launch (start us, length us, event | category | flops | bytes accessed | tf_op | source)
XLA Modules:
  0.0 131.3 jit_solution(9111246515024329549)
XLA Ops:
  0.6 0.7 convert_bitcast_fusion
  1.3 0.7 convert.11
  2.0 0.1 reshape.20
  2.1 0.1 copy.10
  2.2 0.7 pad_add_fusion.ids
  2.9 0.1 pad.7.clone
  2.9 0.7 maximum_maximum_fusion.table
  3.6 1.9 %pack_pairs.1.pack = bf16[512,128]{1,0:T(8,128)(2,1)} custom-call(s32[2]{0:T(128)} %pad_add_fusion.ids, bf16[441,512]{1,0:T(8,128)(2,1)} %bitcast.20, s32[1,512]{1,0:T(1,128)} %bitcast.28, s32[1,512]{1,0:T(1,128)} %bitcast.29, bf16[8,64]{1,0:T(8,128)(2,1)} %maximum_maximum_fusion.table), custom_call_target="tpu_custom_call" | custom-call | tf_op jit(solution)/shard_map/pack_pairs/pallas_call | solution.py:67
  5.5 23.3 %all_to_all.10 = bf16[64,8,128]{2,1,0:T(8,128)(2,1)S(1)} all-to-all(bf16[64,8,128]{2,1,0:T(8,128)(2,1)} %bitcast.19), channel_id=1, replica_groups=mesh['seq'=4,'res'=64] {'res'}, dimensions={0} | all-to-all | bytes 262144 | tf_op jit(solution)/shard_map/all_to_all | solution.py:412
  28.8 1.3 collective-permute-start
  30.1 2.6 %collective-permute-start.1 = (bf16[512,128]{1,0:T(8,128)(2,1)S(1)}, bf16[512,128]{1,0:T(8,128)(2,1)S(1)}, u32[]{:S(2)}, u32[]{:S(2)}) collective-permute-start(bf16[512,128]{1,0:T(8,128)(2,1)S(1)} %bitcast.23), channel_id=1, source_target_pairs={{0,128},{64,192},{128,0},{192,64},{1,129},{65,193},{129,1},{193,65... | collective-permute-start | bytes 393224 | tf_op jit(solution)/shard_map/ppermute | solution.py:395
  32.8 1.1 collective-permute-start.2
  33.8 13.0 %own_field.1 = (bf16[3072,256]{1,0:T(8,128)(2,1)}, bf16[4,2688,256]{2,1,0:T(8,128)(2,1)}, bf16[512,512]{1,0:T(8,128)(2,1)}, f32[4,8,128]{2,1,0:T(8,128)}, f32[6,192,256]{2,1,0:T(8,128)}) custom-call(s32[3072,256]{1,0:T(8,128)} %alignment.1, bf16[512,128]{1,0:T(8,128)(2,1)} %pack_pairs.1.pack, bf16[441,512]{1,0:T(8,128)(2,1)} %bitcast.21), custom_call_target="tpu_custom_call" | custom-call | flops 20000000000 | bytes 10000000 | tf_op jit(solution)/shard_map/own_field/pallas_call | solution.py:199
  46.8 0.6 pad.4.fields
  47.4 0.0 collective-permute-done.q1
  47.4 0.0 collective-permute-done.1.q2
  47.5 0.0 copy-start.17
  47.5 0.0 collective-permute-done.2.q3
  47.5 0.6 copy-done.16
  48.1 0.1 copy-done.17
  48.2 0.0 copy-done.18
  48.2 20.4 %recv_half.1 = (bf16[448,512]{1,0:T(8,128)(2,1)}, bf16[6,192,256]{2,1,0:T(8,128)(2,1)}, f32[24,128]{1,0:T(8,128)}) custom-call(s32[2]{0:T(128)} %pad_add_fusion.ids, bf16[512,128]{1,0:T(8,128)(2,1)} %bitcast.25, bf16[512,128]{1,0:T(8,128)(2,1)} %copy-done.16, bf16[512,128]{1,0:T(8,128)(2,1)} %copy-done.17, bf16[512,128]{1,0:T(8,128)(2,1)} %copy-done.18, ...), custom_call_target="tpu_custom_call" | custom-call | flops 20000000000 | bytes 10000000 | tf_op jit(solution)/shard_map/recv_half/pallas_call | solution.py:277
  68.6 1.7 %constant_dynamic-slice_fusion = (bf16[112,512]{1,0:T(8,128)(2,1)S(1)}, bf16[112,512]{1,0:T(8,128)(2,1)S(1)}, bf16[112,512]{1,0:T(8,128)(2,1)S(1)}, bf16[112,512]{1,0:T(8,128)(2,1)}) fusion(bf16[448,512]{1,0:T(8,128)(2,1)} %get-tuple-element.18, s32[]{:T(128)S(6)} %select_n.19, s32[]{:T(128)S(6)} %select_n.18, s32[]{:T(128)S(6)} %select_n.17, s32[]{:T(128)S(6)} %select_n.16), kind=kLoop, calls=%fused_computation.2 | loop fusion | bytes 917520 | tf_op jit(solution)/shard_map/dynamic_slice | solution.py:405
  70.3 0.4 collective-permute-start.6
  70.7 0.8 collective-permute-start.7
  71.5 1.6 %collective-permute-start.8 = (bf16[112,512]{1,0:T(8,128)(2,1)S(1)}, bf16[112,512]{1,0:T(8,128)(2,1)S(1)}, u32[]{:S(2)}, u32[]{:S(2)}) collective-permute-start(bf16[112,512]{1,0:T(8,128)(2,1)S(1)} %get-tuple-element.22), channel_id=1, source_target_pairs={{0,192},{64,0},{128,64},{192,128},{1,193},{65,1},{129,65},{193,129... | collective-permute-start | bytes 344072 | tf_op jit(solution)/shard_map/ppermute | solution.py:395
  73.1 3.3 %collective-permute-done.6.r1 = bf16[112,512]{1,0:T(8,128)(2,1)S(1)} collective-permute-done((bf16[112,512]{1,0:T(8,128)(2,1)S(1)}, bf16[112,512]{1,0:T(8,128)(2,1)S(1)}, u32[]{:S(2)}, u32[]{:S(2)}) %collective-permute-start.6) | collective-permute-done | bytes 114720 | tf_op jit(solution)/shard_map/ppermute | solution.py:395
  76.4 0.0 collective-permute-done.7.r2
  76.4 1.4 %collective-permute-done.8.r3 = bf16[112,512]{1,0:T(8,128)(2,1)S(1)} collective-permute-done((bf16[112,512]{1,0:T(8,128)(2,1)S(1)}, bf16[112,512]{1,0:T(8,128)(2,1)S(1)}, u32[]{:S(2)}, u32[]{:S(2)}) %collective-permute-start.8) | collective-permute-done | bytes 114720 | tf_op jit(solution)/shard_map/ppermute | solution.py:395
  77.8 0.6 copy-done.10
  78.4 1.9 %sum_back.1 = bf16[512,128]{1,0:T(8,128)(2,1)} custom-call(bf16[112,512]{1,0:T(8,128)(2,1)} %get-tuple-element.25.mine, bf16[112,512]{1,0:T(8,128)(2,1)} %copy-done.7, bf16[112,512]{1,0:T(8,128)(2,1)} %copy-done.9, bf16[112,512]{1,0:T(8,128)(2,1)} %copy-done.10), custom_call_target="tpu_custom_call" | custom-call | tf_op jit(solution)/shard_map/sum_back/pallas_call | solution.py:342
  80.3 7.1 %all-to-all-start.1 = ((bf16[64,8,128]{2,1,0:T(8,128)(2,1)}), bf16[64,8,128]{2,1,0:T(8,128)(2,1)S(1)}, u32[]{:S(2)}, u32[]{:S(2)}) async-start(bf16[64,8,128]{2,1,0:T(8,128)(2,1)} %bitcast.18), calls=%async_computation.1 | async-start | bytes 262144 | tf_op jit(solution)/shard_map/all_to_all | solution.py:412
  87.4 9.8 %own_grad.1 = bf16[448,512]{1,0:T(8,128)(2,1)} custom-call(f32[4,8,128]{2,1,0:T(8,128)} %get-tuple-element.12.keys_ref, bf16[512,512]{1,0:T(8,128)(2,1)} %get-tuple-element.13.to_plain, bf16[4,2688,256]{2,1,0:T(8,128)(2,1)} %get-tuple-element.14.hot, bf16[6,192,256]{2,1,0:T(8,128)(2,1)} %get-tuple-element.17.resid), custom_call_target="tpu_custom_call" | custom-call | flops 12000000000 | bytes 8000000 | tf_op jit(solution)/shard_map/own_grad/pallas_call | solution.py:316
  97.2 1.7 %constant_dynamic-slice_fusion.4 = (bf16[112,512]{1,0:T(8,128)(2,1)S(1)}, bf16[112,512]{1,0:T(8,128)(2,1)S(1)}, bf16[112,512]{1,0:T(8,128)(2,1)S(1)}, bf16[112,512]{1,0:T(8,128)(2,1)}) fusion(bf16[448,512]{1,0:T(8,128)(2,1)} %own_grad.1, s32[]{:T(128)S(6)} %select_n.19, s32[]{:T(128)S(6)} %select_n.18, s32[]{:T(128)S(6)} %select_n.17, s32[]{:T(128)S(6)} %select_n.16), kind=kLoop, calls=%fused_computation.6 | loop fusion | bytes 917520 | tf_op jit(solution)/shard_map/dynamic_slice | solution.py:405
  98.9 0.2 collective-permute-start.3
  99.1 3.2 %collective-permute-start.4 = (bf16[112,512]{1,0:T(8,128)(2,1)S(1)}, bf16[112,512]{1,0:T(8,128)(2,1)S(1)}, u32[]{:S(2)}, u32[]{:S(2)}) collective-permute-start(bf16[112,512]{1,0:T(8,128)(2,1)S(1)} %get-tuple-element.27), channel_id=1, source_target_pairs={{0,128},{64,192},{128,0},{192,64},{1,129},{65,193},{129,1},{193,65... | collective-permute-start | bytes 344072 | tf_op jit(solution)/shard_map/ppermute | solution.py:395
  102.3 0.0 collective-permute-start.5
  102.3 2.1 %collective-permute-done.3.r1 = bf16[112,512]{1,0:T(8,128)(2,1)S(1)} collective-permute-done((bf16[112,512]{1,0:T(8,128)(2,1)S(1)}, bf16[112,512]{1,0:T(8,128)(2,1)S(1)}, u32[]{:S(2)}, u32[]{:S(2)}) %collective-permute-start.3) | collective-permute-done | bytes 114720 | tf_op jit(solution)/shard_map/ppermute | solution.py:395
  104.4 3.1 %collective-permute-done.4.r2 = bf16[112,512]{1,0:T(8,128)(2,1)S(1)} collective-permute-done((bf16[112,512]{1,0:T(8,128)(2,1)S(1)}, bf16[112,512]{1,0:T(8,128)(2,1)S(1)}, u32[]{:S(2)}, u32[]{:S(2)}) %collective-permute-start.4) | collective-permute-done | bytes 114720 | tf_op jit(solution)/shard_map/ppermute | solution.py:395
  107.6 0.0 collective-permute-done.5.r3
  107.6 0.0 all-to-all-done.1
  107.6 0.0 copy-start
  107.6 0.6 copy-done.6
  108.2 0.0 copy-done.8
  108.2 0.0 copy-done
  108.3 1.9 %join_parts.1.c0 = f32[112,512]{1,0:T(8,128)} custom-call(bf16[112,512]{1,0:T(8,128)(2,1)} %get-tuple-element.29.mine, bf16[112,512]{1,0:T(8,128)(2,1)} %copy-done.5, bf16[112,512]{1,0:T(8,128)(2,1)} %copy-done.6, bf16[112,512]{1,0:T(8,128)(2,1)} %copy-done.8, bf16[512,128]{1,0:T(8,128)(2,1)} %bitcast.17), custom_call_target="tpu_custom_call" | custom-call | tf_op jit(solution)/shard_map/join_parts/pallas_call | solution.py:361
  110.2 0.1 collective-permute-start.9
  110.3 4.1 %collective-permute-start.10 = (f32[112,512]{1,0:T(8,128)}, f32[112,512]{1,0:T(8,128)S(1)}, u32[]{:S(2)}, u32[]{:S(2)}) collective-permute-start(f32[112,512]{1,0:T(8,128)} %join_parts.1.c0), channel_id=1, source_target_pairs={{0,128},{64,192},{128,0},{192,64},{1,129},{65,193},{129,1},{193,65... | collective-permute-start | bytes 688136 | tf_op jit(solution)/shard_map/ppermute | solution.py:395
  114.5 0.0 collective-permute-start.11
  114.5 1.5 %collective-permute-start.12 = (f32[24,128]{1,0:T(8,128)S(1)}, f32[24,128]{1,0:T(8,128)S(1)}, u32[]{:S(2)}, u32[]{:S(2)}) collective-permute-start(f32[24,128]{1,0:T(8,128)S(1)} %copy-done.11), channel_id=1, source_target_pairs={{0,64},{64,128},{128,192},{192,0},{1,65},{65,129},{129,193},{193,1... | collective-permute-start | bytes 36872 | tf_op jit(solution)/shard_map/ppermute | solution.py:395
  115.9 0.0 collective-permute-start.13
  115.9 4.5 %collective-permute-done.12.f1 = f32[24,128]{1,0:T(8,128)S(1)} collective-permute-done((f32[24,128]{1,0:T(8,128)S(1)}, f32[24,128]{1,0:T(8,128)S(1)}, u32[]{:S(2)}, u32[]{:S(2)}) %collective-permute-start.12) | collective-permute-done | bytes 12320 | tf_op jit(solution)/shard_map/ppermute | solution.py:395
  120.5 4.9 %collective-permute-start.14 = (f32[24,128]{1,0:T(8,128)S(1)}, f32[24,128]{1,0:T(8,128)S(1)}, u32[]{:S(2)}, u32[]{:S(2)}) collective-permute-start(f32[24,128]{1,0:T(8,128)S(1)} %copy-done.11), channel_id=1, source_target_pairs={{0,192},{64,0},{128,64},{192,128},{1,193},{65,1},{129,65},{193,129... | collective-permute-start | bytes 36872 | tf_op jit(solution)/shard_map/ppermute | solution.py:395
  125.3 0.0 collective-permute-done.13.f2
  125.3 0.8 collective-permute-done.14.f3
  126.2 0.0 collective-permute-done.9.c1
  126.2 0.0 collective-permute-done.10.c2
  126.2 0.0 collective-permute-done.11.c3
  126.2 0.5 copy-done.14
  126.8 0.1 copy-done.1
  126.9 0.1 copy-done.2
  127.0 0.7 copy-done.3
  127.7 2.4 %place_parts.1 = (f32[441,512]{1,0:T(8,128)}, f32[24,128]{1,0:T(8,128)}) custom-call(s32[2]{0:T(128)} %pad_add_fusion.ids, f32[112,512]{1,0:T(8,128)} %join_parts.1.c0, f32[112,512]{1,0:T(8,128)} %copy-done.1, f32[112,512]{1,0:T(8,128)} %copy-done.2, f32[112,512]{1,0:T(8,128)} %copy-done.3, f32[24,128]{1,0:T(8,128)} %get-tuple-element.19.f0, ...), custom_call_target="tpu_custom_call" | custom-call | tf_op jit(solution)/shard_map/place_parts/pallas_call | solution.py:380
  130.0 1.3 slice_bitcast_fusion
  (26 shorter events, 0.0 us)
Async XLA Ops:
  28.8 18.0 %copy-start.4 = (bf16[64,8,128]{2,1,0:T(8,128)(2,1)}, bf16[64,8,128]{2,1,0:T(8,128)(2,1)S(1)}, u32[]{:S(2)}) copy-start(bf16[64,8,128]{2,1,0:T(8,128)(2,1)S(1)} %all_to_all.10) | copy-start | bytes 393220
  28.8 18.0 %copy-start.15 = (f32[48,21]{0,1:T(8,128)S(1)}, f32[48,21]{0,1:T(8,128)}, u32[]{:S(2)}) copy-start(f32[48,21]{0,1:T(8,128)} %param.10) | copy-start | bytes 12100
  28.8 18.6 %collective-permute-start = (bf16[512,128]{1,0:T(8,128)(2,1)S(1)}, bf16[512,128]{1,0:T(8,128)(2,1)S(1)}, u32[]{:S(2)}, u32[]{:S(2)}) collective-permute-start(bf16[512,128]{1,0:T(8,128)(2,1)S(1)} %bitcast.22), channel_id=1, source_target_pairs={{0,64},{64,128},{128,192},{192,0},{1,65},{65,129},{129,193},{193,1... | collective-permute-start | bytes 393224 | tf_op jit(solution)/shard_map/ppermute | solution.py:395
  30.1 17.3 %collective-permute-start.1 = (bf16[512,128]{1,0:T(8,128)(2,1)S(1)}, bf16[512,128]{1,0:T(8,128)(2,1)S(1)}, u32[]{:S(2)}, u32[]{:S(2)}) collective-permute-start(bf16[512,128]{1,0:T(8,128)(2,1)S(1)} %bitcast.23), channel_id=1, source_target_pairs={{0,128},{64,192},{128,0},{192,64},{1,129},{65,193},{129,1},{193,65... | collective-permute-start | bytes 393224 | tf_op jit(solution)/shard_map/ppermute | solution.py:395
  32.8 14.7 %collective-permute-start.2 = (bf16[512,128]{1,0:T(8,128)(2,1)S(1)}, bf16[512,128]{1,0:T(8,128)(2,1)S(1)}, u32[]{:S(2)}, u32[]{:S(2)}) collective-permute-start(bf16[512,128]{1,0:T(8,128)(2,1)S(1)} %bitcast.24), channel_id=1, source_target_pairs={{0,192},{64,0},{128,64},{192,128},{1,193},{65,1},{129,65},{193,129... | collective-permute-start | bytes 393224 | tf_op jit(solution)/shard_map/ppermute | solution.py:395
  47.4 0.7 copy-start.16
  47.5 0.7 copy-start.17
  47.5 0.7 copy-start.18
  70.3 6.1 %collective-permute-start.6 = (bf16[112,512]{1,0:T(8,128)(2,1)S(1)}, bf16[112,512]{1,0:T(8,128)(2,1)S(1)}, u32[]{:S(2)}, u32[]{:S(2)}) collective-permute-start(bf16[112,512]{1,0:T(8,128)(2,1)S(1)} %get-tuple-element.24), channel_id=1, source_target_pairs={{0,64},{64,128},{128,192},{192,0},{1,65},{65,129},{129,193},{193,1... | collective-permute-start | bytes 344072 | tf_op jit(solution)/shard_map/ppermute | solution.py:395
  70.7 5.7 %collective-permute-start.7 = (bf16[112,512]{1,0:T(8,128)(2,1)S(1)}, bf16[112,512]{1,0:T(8,128)(2,1)S(1)}, u32[]{:S(2)}, u32[]{:S(2)}) collective-permute-start(bf16[112,512]{1,0:T(8,128)(2,1)S(1)} %get-tuple-element.23), channel_id=1, source_target_pairs={{0,128},{64,192},{128,0},{192,64},{1,129},{65,193},{129,1},{193,65... | collective-permute-start | bytes 344072 | tf_op jit(solution)/shard_map/ppermute | solution.py:395
  71.5 6.3 %collective-permute-start.8 = (bf16[112,512]{1,0:T(8,128)(2,1)S(1)}, bf16[112,512]{1,0:T(8,128)(2,1)S(1)}, u32[]{:S(2)}, u32[]{:S(2)}) collective-permute-start(bf16[112,512]{1,0:T(8,128)(2,1)S(1)} %get-tuple-element.22), channel_id=1, source_target_pairs={{0,192},{64,0},{128,64},{192,128},{1,193},{65,1},{129,65},{193,129... | collective-permute-start | bytes 344072 | tf_op jit(solution)/shard_map/ppermute | solution.py:395
  76.4 1.4 %copy-start.7 = (bf16[112,512]{1,0:T(8,128)(2,1)}, bf16[112,512]{1,0:T(8,128)(2,1)S(1)}, u32[]{:S(2)}) copy-start(bf16[112,512]{1,0:T(8,128)(2,1)S(1)} %collective-permute-done.6.r1) | copy-start | bytes 344068
  76.4 1.4 %copy-start.9 = (bf16[112,512]{1,0:T(8,128)(2,1)}, bf16[112,512]{1,0:T(8,128)(2,1)S(1)}, u32[]{:S(2)}) copy-start(bf16[112,512]{1,0:T(8,128)(2,1)S(1)} %collective-permute-done.7.r2) | copy-start | bytes 344068
  77.8 0.6 copy-start.10
  80.3 27.3 %all-to-all-start.1 = ((bf16[64,8,128]{2,1,0:T(8,128)(2,1)}), bf16[64,8,128]{2,1,0:T(8,128)(2,1)S(1)}, u32[]{:S(2)}, u32[]{:S(2)}) async-start(bf16[64,8,128]{2,1,0:T(8,128)(2,1)} %bitcast.18), calls=%async_computation.1 | async-start | bytes 262144 | tf_op jit(solution)/shard_map/all_to_all | solution.py:412
  87.4 27.0 %copy-start.11 = (f32[24,128]{1,0:T(8,128)S(1)}, f32[24,128]{1,0:T(8,128)}, u32[]{:S(2)}) copy-start(f32[24,128]{1,0:T(8,128)} %get-tuple-element.19.f0) | copy-start | bytes 36868
  98.9 5.5 %collective-permute-start.3 = (bf16[112,512]{1,0:T(8,128)(2,1)S(1)}, bf16[112,512]{1,0:T(8,128)(2,1)S(1)}, u32[]{:S(2)}, u32[]{:S(2)}) collective-permute-start(bf16[112,512]{1,0:T(8,128)(2,1)S(1)} %get-tuple-element.28), channel_id=1, source_target_pairs={{0,64},{64,128},{128,192},{192,0},{1,65},{65,129},{129,193},{193,1... | collective-permute-start | bytes 344072 | tf_op jit(solution)/shard_map/ppermute | solution.py:395
  99.1 8.4 %collective-permute-start.4 = (bf16[112,512]{1,0:T(8,128)(2,1)S(1)}, bf16[112,512]{1,0:T(8,128)(2,1)S(1)}, u32[]{:S(2)}, u32[]{:S(2)}) collective-permute-start(bf16[112,512]{1,0:T(8,128)(2,1)S(1)} %get-tuple-element.27), channel_id=1, source_target_pairs={{0,128},{64,192},{128,0},{192,64},{1,129},{65,193},{129,1},{193,65... | collective-permute-start | bytes 344072 | tf_op jit(solution)/shard_map/ppermute | solution.py:395
  102.3 5.3 %collective-permute-start.5 = (bf16[112,512]{1,0:T(8,128)(2,1)S(1)}, bf16[112,512]{1,0:T(8,128)(2,1)S(1)}, u32[]{:S(2)}, u32[]{:S(2)}) collective-permute-start(bf16[112,512]{1,0:T(8,128)(2,1)S(1)} %get-tuple-element.26), channel_id=1, source_target_pairs={{0,192},{64,0},{128,64},{192,128},{1,193},{65,1},{129,65},{193,129... | collective-permute-start | bytes 344072 | tf_op jit(solution)/shard_map/ppermute | solution.py:395
  104.4 3.2 %copy-start.5 = (bf16[112,512]{1,0:T(8,128)(2,1)}, bf16[112,512]{1,0:T(8,128)(2,1)S(1)}, u32[]{:S(2)}) copy-start(bf16[112,512]{1,0:T(8,128)(2,1)S(1)} %collective-permute-done.3.r1) | copy-start | bytes 344068
  107.5 0.6 copy-start.6
  107.6 0.7 copy-start.8
  107.6 0.7 copy-start
  110.2 16.0 %collective-permute-start.9 = (f32[112,512]{1,0:T(8,128)}, f32[112,512]{1,0:T(8,128)S(1)}, u32[]{:S(2)}, u32[]{:S(2)}) collective-permute-start(f32[112,512]{1,0:T(8,128)} %join_parts.1.c0), channel_id=1, source_target_pairs={{0,64},{64,128},{128,192},{192,0},{1,65},{65,129},{129,193},{193,1... | collective-permute-start | bytes 688136 | tf_op jit(solution)/shard_map/ppermute | solution.py:395
  110.3 15.9 %collective-permute-start.10 = (f32[112,512]{1,0:T(8,128)}, f32[112,512]{1,0:T(8,128)S(1)}, u32[]{:S(2)}, u32[]{:S(2)}) collective-permute-start(f32[112,512]{1,0:T(8,128)} %join_parts.1.c0), channel_id=1, source_target_pairs={{0,128},{64,192},{128,0},{192,64},{1,129},{65,193},{129,1},{193,65... | collective-permute-start | bytes 688136 | tf_op jit(solution)/shard_map/ppermute | solution.py:395
  114.5 11.7 %collective-permute-start.11 = (f32[112,512]{1,0:T(8,128)}, f32[112,512]{1,0:T(8,128)S(1)}, u32[]{:S(2)}, u32[]{:S(2)}) collective-permute-start(f32[112,512]{1,0:T(8,128)} %join_parts.1.c0), channel_id=1, source_target_pairs={{0,192},{64,0},{128,64},{192,128},{1,193},{65,1},{129,65},{193,129... | collective-permute-start | bytes 688136 | tf_op jit(solution)/shard_map/ppermute | solution.py:395
  114.5 6.0 %collective-permute-start.12 = (f32[24,128]{1,0:T(8,128)S(1)}, f32[24,128]{1,0:T(8,128)S(1)}, u32[]{:S(2)}, u32[]{:S(2)}) collective-permute-start(f32[24,128]{1,0:T(8,128)S(1)} %copy-done.11), channel_id=1, source_target_pairs={{0,64},{64,128},{128,192},{192,0},{1,65},{65,129},{129,193},{193,1... | collective-permute-start | bytes 36872 | tf_op jit(solution)/shard_map/ppermute | solution.py:395
  115.9 9.4 %collective-permute-start.13 = (f32[24,128]{1,0:T(8,128)S(1)}, f32[24,128]{1,0:T(8,128)S(1)}, u32[]{:S(2)}, u32[]{:S(2)}) collective-permute-start(f32[24,128]{1,0:T(8,128)S(1)} %copy-done.11), channel_id=1, source_target_pairs={{0,128},{64,192},{128,0},{192,64},{1,129},{65,193},{129,1},{193,65... | collective-permute-start | bytes 36872 | tf_op jit(solution)/shard_map/ppermute | solution.py:395
  120.5 5.8 %copy-start.12 = (f32[24,128]{1,0:T(8,128)}, f32[24,128]{1,0:T(8,128)S(1)}, u32[]{:S(2)}) copy-start(f32[24,128]{1,0:T(8,128)S(1)} %collective-permute-done.12.f1) | copy-start | bytes 36868
  120.5 5.7 %collective-permute-start.14 = (f32[24,128]{1,0:T(8,128)S(1)}, f32[24,128]{1,0:T(8,128)S(1)}, u32[]{:S(2)}, u32[]{:S(2)}) collective-permute-start(f32[24,128]{1,0:T(8,128)S(1)} %copy-done.11), channel_id=1, source_target_pairs={{0,192},{64,0},{128,64},{192,128},{1,193},{65,1},{129,65},{193,129... | collective-permute-start | bytes 36872 | tf_op jit(solution)/shard_map/ppermute | solution.py:395
  125.3 0.9 copy-start.13
  126.2 0.6 copy-start.14
  126.2 0.7 copy-start.1
  126.2 0.8 copy-start.2
  127.0 0.7 copy-start.3

commit v2 on v1

v2 whole, which is shorter than its diff:
```python
import functools

import jax
import jax.numpy as jnp
from jax import lax
from jax.experimental import pallas as pl
from jax.experimental.pallas import tpu as pltpu
from jax.sharding import PartitionSpec as P

Q = 21
QP = 24
RL = 48
CAP = 8
SLOTS = 4
PAIRS = 512
BLOCKS = 64
SEQ = 256
RES = 3072
TILE = 128
TILES = PAIRS // TILE
GROUP = 8
GROUPS = RL // GROUP
GROWS = GROUP * QP
QUARTER = 112
PADQ = 4 * QUARTER
DEEP = Q * TILE
F32 = jnp.float32
BF16 = jnp.bfloat16
VMEM = pl.BlockSpec(memory_space=pltpu.VMEM)
SMEM = pl.BlockSpec(memory_space=pltpu.SMEM)
ANY = pl.BlockSpec(memory_space=pl.ANY)
PARAMS = pltpu.CompilerParams(vmem_limit_bytes=56 * 1024 * 1024)
SMALL = pltpu.CompilerParams(vmem_limit_bytes=16 * 1024 * 1024)
SENT = F32
SPANS = ((0, 6), (6, 12), (12, 18), (18, 21))


def iota(shape, dim):
    return lax.broadcasted_iota(jnp.int32, shape, dim)


def dot(x, y):
    return jnp.dot(x, y, preferred_element_type=F32)


def pack_kernel(coup, left, slot, residue, count, out, wide, tall):
    wide[...] = jnp.zeros_like(wide)
    wide[0 : Q * Q, :] = coup[...].astype(F32)
    start = pl.multiple_of(lax.axis_index("seq") * QUARTER, 8)
    tall[0:QUARTER, :] = wide[pl.ds(start, QUARTER), :]
    lane = iota((1, PAIRS), 1)
    bucket = lax.shift_right_logical(lane, 3)
    wanted = bucket * SLOTS + slot[...]
    pick = jnp.where(iota((BLOCKS * SLOTS, PAIRS), 0) == wanted, 1.0, 0.0).astype(BF16)
    partner = dot(jnp.broadcast_to(residue[...], (8, BLOCKS * SLOTS)).astype(F32).astype(BF16), pick)
    spread = jnp.where(iota((BLOCKS, PAIRS), 0) == bucket, 1.0, 0.0).astype(BF16)
    counts = dot(jnp.broadcast_to(count[...], (8, BLOCKS)).astype(F32).astype(BF16), spread)
    live = jnp.where((lane & (CAP - 1)).astype(F32) < counts[0:1], 1.0, 0.0)
    sub = iota((16, PAIRS), 0)
    index = jnp.where(sub == 0, left[...].astype(F32), 0.0)
    index = jnp.where(sub == 1, partner[0:1], index)
    index = jnp.where(sub == 2, live, index)
    index = jnp.where(sub == 3, lax.axis_index("res").astype(F32), index)
    index = jnp.where(sub == 4, bucket.astype(F32), index)
    tall[QUARTER:TILE, :] = index
    out[...] = jnp.transpose(tall[...]).astype(BF16)


def pack_pairs(coup, left, slot, residue, count):
    return pl.pallas_call(
        pack_kernel,
        out_shape=jax.ShapeDtypeStruct((PAIRS, TILE), BF16),
        in_specs=[VMEM] * 5,
        out_specs=VMEM,
        scratch_shapes=[pltpu.VMEM((PADQ, PAIRS), F32), pltpu.VMEM((TILE, PAIRS), F32)],
        compiler_params=PARAMS,
        name="pack_pairs",
    )(coup, left, slot, residue, count)


def order_half(pack, flipped, own):
    mine, other, block = (112, 113, 116) if own else (113, 112, 115)
    wide = pack.astype(F32)
    key_row = jnp.where(flipped[114:115] > 0.5, flipped[mine : mine + 1], float(RL))
    key_col = jnp.where(wide[:, 114:115] > 0.5, wide[:, mine : mine + 1], float(RL))
    lane = iota((PAIRS, PAIRS), 1).astype(F32)
    sub = iota((PAIRS, PAIRS), 0).astype(F32)
    full_row = key_row * PAIRS + lane
    full_col = key_col * PAIRS + sub
    place_row = jnp.sum(jnp.where(full_col < full_row, 1.0, 0.0), axis=0, keepdims=True)
    place_col = jnp.sum(jnp.where(full_row < full_col, 1.0, 0.0), axis=1, keepdims=True)
    to_sorted = jnp.where(place_col == lane, 1.0, 0.0).astype(BF16)
    to_plain = jnp.where(place_row == sub, 1.0, 0.0).astype(BF16)
    cols = dot(to_plain, pack)
    far = cols[:, block : block + 1] * RL + cols[:, other : other + 1]
    keys = dot(jnp.broadcast_to(key_row, (8, PAIRS)).astype(BF16), to_sorted)
    return to_sorted, place_row, far, keys


def plain_order(place):
    return jnp.where(place[0:1] == iota((PAIRS, PAIRS), 0).astype(F32), 1.0, 0.0).astype(BF16)


def sorted_order(place):
    col = jnp.transpose(jnp.broadcast_to(place[0:1], (TILE, PAIRS)))[:, 0:1]
    return jnp.where(col == iota((PAIRS, PAIRS), 1).astype(F32), 1.0, 0.0).astype(BF16)


def find_far(far, states):
    far_states = jnp.zeros((PAIRS, SEQ), F32)
    chunk = 256
    lane = iota((PAIRS, chunk), 1).astype(F32)
    for n in range(RES // chunk):
        pick = jnp.where(far - float(n * chunk) == lane, 1.0, 0.0).astype(BF16)
        far_states = far_states + dot(pick, states[n * chunk : (n + 1) * chunk, :])
    return far_states


def fill_hot(far_states, j, hot):
    tile = far_states[j * TILE : (j + 1) * TILE]
    for c in range(Q):
        hot[j, c * TILE : (c + 1) * TILE, :] = jnp.where(tile == float(c), 1.0, 0.0).astype(BF16)


def fill_flat(far_states, j, flat):
    tile = jnp.transpose(far_states[j * TILE : (j + 1) * TILE])
    for c in range(Q):
        flat[j, :, c * TILE : (c + 1) * TILE] = jnp.where(tile == float(c), 1.0, 0.0).astype(BF16)


def store_keys(keys, keys_ref):
    for j in range(TILES):
        keys_ref[j] = keys[:, j * TILE : (j + 1) * TILE]


def group_range(keys):
    low = jnp.min(keys).astype(jnp.int32)
    high = jnp.max(jnp.where(keys < RL - 0.5, keys, -1.0)).astype(jnp.int32)
    return low // GROUP, (high + GROUP) // GROUP


def group_masks(keys, g):
    base = (g * GROUP).astype(F32)
    wide = jnp.broadcast_to(keys[0:1], (QP, TILE))
    return [wide == base + float(m) for m in range(GROUP)]


def add_field(keys_ref, blocks, hot, lhs, field, wait=None):
    def tile_step(j, carry):
        if wait is not None:
            wait(j)
        keys = keys_ref[j]
        low, high = group_range(keys)

        def group_step(g, carry):
            masks = group_masks(keys, g)
            total = field[g]
            for n, (first, last) in enumerate(SPANS):
                for c in range(first, last):
                    block = blocks[j, c]
                    rows = [jnp.where(mask, block, 0.0) for mask in masks]
                    lhs[n][:, (c - first) * TILE : (c - first + 1) * TILE] = jnp.concatenate(
                        rows, axis=0
                    ).astype(BF16)
                total = total + dot(lhs[n][...], hot[j, first * TILE : last * TILE, :])
            field[g] = total
            return carry

        return lax.fori_loop(low, high, group_step, carry)

    lax.fori_loop(0, TILES, tile_step, 0)


def add_grad(keys_ref, resid, flat, grad, wait=None):
    grad[...] = jnp.zeros_like(grad)

    def tile_step(j, carry):
        if wait is not None:
            wait(j)
        keys = keys_ref[j]
        low, high = group_range(keys)

        def group_step(g, carry):
            masks = group_masks(keys, g)
            rows = resid[g]
            for c in range(0, Q, 2):
                count = min(2, Q - c)
                out = dot(rows, flat[j, :, c * TILE : (c + count) * TILE])
                for i in range(count):
                    total = grad[j, c + i]
                    for m in range(GROUP):
                        piece = out[m * QP : (m + 1) * QP, i * TILE : (i + 1) * TILE]
                        total = jnp.where(masks[m], piece, total)
                    grad[j, c + i] = total
            return carry

        return lax.fori_loop(low, high, group_step, carry)

    lax.fori_loop(0, TILES, tile_step, 0)


def store_quarters(full, outs):
    seq_index = lax.axis_index("seq")
    for k, out in enumerate(outs):
        owner = lax.rem(seq_index + k, 4)
        out[0:QUARTER, :] = full[pl.ds(pl.multiple_of(owner * QUARTER, 8), QUARTER), :].astype(BF16)


def own_field_kernel(
    alignment, pack, coup, states, far_out, place_out, keys_ref, field,
    sorted_blocks, blocks, hot, *lhs,
):
    for n in range(RES // 256):
        rows = slice(n * 256, (n + 1) * 256)
        states[rows, :] = alignment[rows, :].astype(F32).astype(BF16)
    packed = pack[...]
    flipped = jnp.transpose(packed.astype(F32))
    to_sorted, place, far, keys = order_half(packed, flipped, True)
    place_out[...] = jnp.broadcast_to(place, (8, PAIRS))
    store_keys(keys, keys_ref)
    sorted_blocks[...] = jnp.zeros_like(sorted_blocks)
    ordered = dot(coup[...], to_sorted)
    for j in range(TILES):
        sorted_blocks[j, 0 : Q * Q, :] = ordered[:, j * TILE : (j + 1) * TILE]
    for c in range(Q):
        for j in range(TILES):
            blocks[j, c] = sorted_blocks[j, pl.ds(c, QP, stride=Q), :]
    far_states = find_far(far, states)
    far_out[...] = far_states.astype(BF16)
    for j in range(TILES):
        fill_hot(far_states, j, hot)
    field[...] = jnp.zeros_like(field)
    add_field(keys_ref, blocks, hot, lhs, field)


def lhs_scratch():
    return [pltpu.VMEM((GROWS, (last - first) * TILE), BF16) for first, last in SPANS]


def own_field(alignment, pack, coup):
    return pl.pallas_call(
        own_field_kernel,
        out_shape=(
            jax.ShapeDtypeStruct((RES, SEQ), BF16),
            jax.ShapeDtypeStruct((PAIRS, SEQ), BF16),
            jax.ShapeDtypeStruct((8, PAIRS), F32),
            jax.ShapeDtypeStruct((TILES, 8, TILE), F32),
            jax.ShapeDtypeStruct((GROUPS, GROWS, SEQ), F32),
        ),
        in_specs=[VMEM] * 3,
        out_specs=(VMEM,) * 5,
        scratch_shapes=[
            pltpu.VMEM((TILES, 512, TILE), F32),
            pltpu.VMEM((TILES, Q, QP, TILE), F32),
            pltpu.VMEM((TILES, DEEP, SEQ), BF16),
        ]
        + lhs_scratch(),
        compiler_params=PARAMS,
        cost_estimate=pl.CostEstimate(
            flops=10_000_000_000, bytes_accessed=10_000_000, transcendentals=0
        ),
        name="own_field",
    )(alignment, pack, coup)


def recv_order_kernel(pack, states, far_out, place_out, keys_ref, codes):
    packed = pack[...]
    flipped = jnp.transpose(packed.astype(F32))
    to_sorted, place, far, keys = order_half(packed, flipped, False)
    store_keys(keys, keys_ref)
    place_out[...] = jnp.broadcast_to(place, (8, PAIRS))
    far_out[...] = find_far(far, states).astype(BF16)
    codes[...] = states[pl.ds(pl.multiple_of(lax.axis_index("res") * RL, 16), RL), :]


def recv_order(pack, states):
    return pl.pallas_call(
        recv_order_kernel,
        out_shape=(
            jax.ShapeDtypeStruct((PAIRS, SEQ), BF16),
            jax.ShapeDtypeStruct((8, PAIRS), F32),
            jax.ShapeDtypeStruct((TILES, 8, TILE), F32),
            jax.ShapeDtypeStruct((RL, SEQ), BF16),
        ),
        in_specs=[VMEM] * 2,
        out_specs=(VMEM,) * 4,
        compiler_params=PARAMS,
        cost_estimate=pl.CostEstimate(
            flops=5_000_000_000, bytes_accessed=3_000_000, transcendentals=0
        ),
        name="recv_order",
    )(pack, states)


def recv_kernel(
    q0, q1, q2, q3, far, place, keys_ref, codes, own, fields, weights,
    g0, g1, g2, g3, resid_out, field_out,
    wide, sorted_blocks, blocks, hot, flat, field, grad, *lhs,
):
    for back, part in enumerate((q0, q1, q2, q3)):
        flipped = jnp.transpose(part[...].astype(F32))
        owner = lax.rem(lax.axis_index("seq") + (4 - back), 4)
        wide[pl.ds(pl.multiple_of(owner * QUARTER, 8), QUARTER), :] = flipped[0:QUARTER]
    sorted_blocks[PADQ:512, :] = jnp.zeros((512 - PADQ, PAIRS), F32)
    sorted_blocks[0:PADQ, :] = dot(wide[...].astype(BF16), sorted_order(place))
    for a in range(Q):
        for j in range(TILES):
            blocks[j, a] = sorted_blocks[a * Q : a * Q + QP, j * TILE : (j + 1) * TILE]
    far_states = far[...].astype(F32)
    for j in range(TILES):
        fill_hot(far_states, j, hot)
    field[...] = own[...]
    add_field(keys_ref, blocks, hot, lhs, field)

    my_codes = codes[...].astype(F32)
    state = iota((QP, SEQ), 0).astype(F32)
    weight = weights[...]
    lane = iota((QP, TILE), 1)
    local = jnp.concatenate([fields[...], jnp.full((QP - Q, RL), -1e30, F32)], axis=0)
    for g in range(GROUPS):
        pieces = []
        for m in range(GROUP):
            r = g * GROUP + m
            logits = field[g, m * QP : (m + 1) * QP, :] + local[:, r : r + 1]
            top = jnp.max(logits, axis=0, keepdims=True)
            raised = jnp.exp(logits - top)
            share = weight / jnp.sum(raised, axis=0, keepdims=True)
            hot_own = jnp.where(state == my_codes[r : r + 1], weight, 0.0)
            pieces.append(raised * share - hot_own)
        resid_out[g] = jnp.concatenate(pieces, axis=0).astype(BF16)
    field_part = jnp.zeros((QP, TILE), F32)
    ones = jnp.ones((SEQ, TILE), BF16)
    for g in range(GROUPS):
        sums = dot(resid_out[g], ones)
        for m in range(GROUP):
            piece = sums[m * QP : (m + 1) * QP]
            field_part = jnp.where(lane == g * GROUP + m, piece, field_part)
    field_out[...] = field_part

    for j in range(TILES):
        fill_flat(far_states, j, flat)
    add_grad(keys_ref, resid_out, flat, grad)
    wide[Q * Q // 8 * 8 : PADQ, :] = jnp.zeros((PADQ - Q * Q // 8 * 8, PAIRS), F32)
    for a in range(Q):
        for j in range(TILES):
            wide[a * Q : (a + 1) * Q, j * TILE : (j + 1) * TILE] = grad[j, a, 0:Q]
    wide[...] = dot(wide[...].astype(BF16), plain_order(place))
    store_quarters(wide, (g0, g1, g2, g3))


def recv_half(parts, order, own, fields, weights):
    return pl.pallas_call(
        recv_kernel,
        out_shape=(jax.ShapeDtypeStruct((QUARTER, PAIRS), BF16),) * 4
        + (
            jax.ShapeDtypeStruct((GROUPS, GROWS, SEQ), BF16),
            jax.ShapeDtypeStruct((QP, TILE), F32),
        ),
        in_specs=[VMEM] * 11,
        out_specs=(VMEM,) * 6,
        scratch_shapes=[
            pltpu.VMEM((PADQ, PAIRS), F32),
            pltpu.VMEM((512, PAIRS), F32),
            pltpu.VMEM((TILES, Q, QP, TILE), F32),
            pltpu.VMEM((TILES, DEEP, SEQ), BF16),
            pltpu.VMEM((TILES, SEQ, DEEP), BF16),
            pltpu.VMEM((GROUPS, GROWS, SEQ), F32),
            pltpu.VMEM((TILES, Q, QP, TILE), F32),
        ]
        + lhs_scratch(),
        compiler_params=PARAMS,
        cost_estimate=pl.CostEstimate(
            flops=20_000_000_000, bytes_accessed=10_000_000, transcendentals=0
        ),
        name="recv_half",
    )(*parts, *order, own, fields, weights)


def own_grad_kernel(
    keys_ref, place, far, resid, field_part, g0, g1, g2, g3, grad, wide, full, flat
):
    far_states = far[...].astype(F32)
    for j in range(TILES):
        fill_flat(far_states, j, flat)
    add_grad(keys_ref, resid, flat, grad)
    to_plain = plain_order(place)
    total = jnp.zeros((PADQ, PAIRS), F32)
    for j in range(TILES):
        wide[j, Q * Q // 8 * 8 : PADQ, :] = jnp.zeros((PADQ - Q * Q // 8 * 8, TILE), F32)
        for c in range(Q):
            wide[j, pl.ds(c, Q, stride=Q), :] = grad[j, c, 0:Q]
        total = total + dot(wide[j].astype(BF16), to_plain[j * TILE : (j + 1) * TILE, :])
    full[...] = total
    outs = (g0, g1, g2, g3)
    store_quarters(full, outs)
    exact = field_part[...]
    coarse = exact.astype(BF16).astype(F32)
    rest = exact - coarse
    tail = jnp.concatenate(
        [coarse[0:16], jnp.concatenate([coarse[16:24], rest[0:8]], axis=0), rest[8:24],
         jnp.zeros((16, TILE), F32)], axis=1,
    ).astype(BF16)
    for out in outs:
        out[QUARTER:TILE, :] = tail


def own_grad(keys, place, far, resid, field_part):
    return pl.pallas_call(
        own_grad_kernel,
        out_shape=(jax.ShapeDtypeStruct((TILE, PAIRS), BF16),) * 4,
        in_specs=[VMEM] * 5,
        out_specs=(VMEM,) * 4,
        scratch_shapes=[
            pltpu.VMEM((TILES, Q, QP, TILE), F32),
            pltpu.VMEM((TILES, PADQ, TILE), F32),
            pltpu.VMEM((PADQ, PAIRS), F32),
            pltpu.VMEM((TILES, SEQ, DEEP), BF16),
        ],
        compiler_params=PARAMS,
        cost_estimate=pl.CostEstimate(
            flops=6_000_000_000, bytes_accessed=8_000_000, transcendentals=0
        ),
        name="own_grad",
    )(keys, place, far, resid, field_part)


def back_kernel(mine, r1, r2, r3, out, tall):
    total = mine[...].astype(F32) + r1[...].astype(F32)
    total = total + (r2[...].astype(F32) + r3[...].astype(F32))
    tall[0:QUARTER, :] = total
    tall[QUARTER:TILE, :] = jnp.zeros((TILE - QUARTER, PAIRS), F32)
    out[...] = jnp.transpose(tall[...]).astype(BF16)


def sum_back(chunks):
    return pl.pallas_call(
        back_kernel,
        out_shape=jax.ShapeDtypeStruct((PAIRS, TILE), BF16),
        in_specs=[VMEM] * 4,
        out_specs=VMEM,
        scratch_shapes=[pltpu.VMEM((TILE, PAIRS), F32)],
        compiler_params=SMALL,
        name="sum_back",
    )(*chunks)


def join_kernel(scale, mine, r1, r2, r3, remote, out, field_out):
    total = mine[...].astype(F32) + r1[...].astype(F32)
    total = total + (r2[...].astype(F32) + r3[...].astype(F32))
    flipped = jnp.transpose(remote[...].astype(F32))
    out[...] = (total[0:QUARTER] + flipped[0:QUARTER]) * scale
    tail = total[QUARTER:TILE]
    first = tail[:, 0:TILE]
    middle = tail[:, TILE : 2 * TILE]
    last = tail[:, 2 * TILE : 3 * TILE]
    coarse = jnp.concatenate([first, middle[0:8]], axis=0)
    rest = jnp.concatenate([middle[8:16], last], axis=0)
    field_out[...] = ((coarse + rest) * scale)[0:Q, 0:RL]


def join_parts(scale, chunks, remote):
    return pl.pallas_call(
        functools.partial(join_kernel, scale),
        out_shape=(
            jax.ShapeDtypeStruct((QUARTER, PAIRS), SENT),
            jax.ShapeDtypeStruct((Q, RL), F32),
        ),
        in_specs=[VMEM] * 5,
        out_specs=(VMEM, VMEM),
        compiler_params=SMALL,
        name="join_parts",
    )(*chunks, remote)


def place_kernel(c0, c1, c2, c3, out, wide):
    for back, part in enumerate((c0, c1, c2, c3)):
        owner = lax.rem(lax.axis_index("seq") + (4 - back), 4)
        wide[pl.ds(pl.multiple_of(owner * QUARTER, 8), QUARTER), :] = part[...].astype(F32)
    out[...] = wide[0 : Q * Q, :]


def place_parts(chunks):
    return pl.pallas_call(
        place_kernel,
        out_shape=jax.ShapeDtypeStruct((Q * Q, PAIRS), F32),
        in_specs=[VMEM] * 4,
        out_specs=VMEM,
        scratch_shapes=[pltpu.VMEM((PADQ, PAIRS), F32)],
        compiler_params=SMALL,
        name="place_parts",
    )(*chunks)


def shifted(array, k):
    return lax.ppermute(array, "seq", [(i, (i + k) % 4) for i in range(4)])


def gather_seq(array):
    return [array] + [shifted(array, k) for k in (1, 2, 3)]


def scatter_seq(quarters):
    return [quarters[0]] + [shifted(quarters[k], k) for k in (1, 2, 3)]


def swap_blocks(array):
    blocks = array.reshape(BLOCKS, CAP, TILE)
    moved = lax.all_to_all(blocks, "res", split_axis=0, concat_axis=0, tiled=True)
    return moved.reshape(PAIRS, TILE)


def per_device(
    alignment, seq_weights, fields, couplings, pair_left, pair_slot, slot_residue, pair_count
):
    scale = Q / (SEQ * 4)
    coup = couplings.T
    pack = pack_pairs(
        coup, pair_left[None, :], pair_slot[None, :], slot_residue[None, :], pair_count[None, :]
    )
    received = swap_blocks(pack)
    states, far, place, keys, field = own_field(alignment, pack, coup)
    received, field, states = lax.optimization_barrier((received, field, states))
    parts = gather_seq(received)
    order = recv_order(received, states)
    remote = recv_half(parts, order, field, fields.T, seq_weights[None, :])
    remote_quarters, resid, field_part = remote[:4], remote[4], remote[5]
    remote_chunks = scatter_seq(remote_quarters)
    local_quarters = own_grad(keys, place, far, resid, field_part)
    remote_chunks, local_quarters = lax.optimization_barrier((remote_chunks, local_quarters))
    swapped = swap_blocks(sum_back(remote_chunks))
    local_chunks = scatter_seq(local_quarters)
    joined, field_grad = join_parts(scale, local_chunks, swapped)
    coupling_grad = place_parts(gather_seq(joined))
    return coupling_grad.T, field_grad.T


def solution(mesh):
    in_specs = (
        P(None, "seq"),
        P("seq"),
        P("res", None),
        P("res", None),
        P("res"),
        P("res"),
        P("res"),
        P("res"),
    )
    out_specs = (P("res", None), P("res", None))
    return jax.shard_map(
        per_device, mesh=mesh, in_specs=in_specs, out_specs=out_specs, check_vma=False
    )
```

time: 133 us -> 107 us (0.80); the launches traced: 131 us -> 107 us
  blocking collectives: 23.3 us -> 0 us
  starting transfers between devices: 28.9 us -> 39.2 us
  Pallas kernels: 51.2 us -> 43.2 us
  local copies, waits for them, and re-layouts: 9.18 us -> 1.57 us
  waiting for transfers between devices: 15.3 us -> 22.1 us
  other arithmetic: 2.66 us -> 0 us
    all_to_all x1 -> x0, blocking collectives: 23.3 us -> none  [swap_blocks(): lax.all_to_all(blocks, 'res', split_axis=0, concat_axis=0, tiled=True)]
    all_to_all x1 -> x2, starting transfers between devices: 7.12 us -> 24.5 us  [swap_blocks(): lax.all_to_all(blocks, 'res', split_axis=0, concat_axis=0, tiled=True)]
    ppermute x15 -> x12, starting transfers between devices: 21.7 us -> 14.7 us  [shifted(): return lax.ppermute(array, 'seq', [(i, (i + k) % 4) for i in range(4)])]
    ppermute x15 -> x12, waiting for transfers between devices: 15.3 us -> 21 us  [shifted(): return lax.ppermute(array, 'seq', [(i, (i + k) % 4) for i in range(4)])]
    pallas_call x4 -> x5, Pallas kernels: 34.5 us -> 29.3 us  [the longest x1 14.9 us: recv_half(): pl.pallas_call(recv_kernel, out_shape=(jax.ShapeDtypeStruct((QUARTER, PAI...]
    dynamic_slice x2 -> x0, local copies, waits for them, and re-layouts: 3.48 us -> none  [quarter(): return lax.dynamic_slice_in_dim(array, start, QUARTER, 0)]
    unnamed x38 -> x12, local copies, waits for them, and re-layouts: 3.52 us -> 1.57 us
    pallas_call x1, Pallas kernels: 13 us -> 11.2 us  [own_field(): pl.pallas_call(own_field_kernel, out_shape=(jax.ShapeDtypeStruct((RES, SE...]
  transfers between devices with their start and end apart: 16 -> 14, of which waited for: 6 -> 9; matrix products, arithmetic and copies ran while one was open for 2% -> 0% of each run, Pallas kernels for 17% -> 22%
where the time goes in v2:
time: 107 us
  Pallas kernels  43.2 us (40%)
  starting transfers between devices  39.2 us (37%)
  waiting for transfers between devices  22.1 us (21%)
  local copies, waits for them, and re-layouts  1.57 us (1%)
    all_to_all x2, starting transfers between devices, swap_blocks(): lax.all_to_all(blocks, 'res', split_axis=0, concat_axis=0, tiled=True)  24.5 us
    ppermute x12, waiting for transfers between devices, shifted(): return lax.ppermute(array, 'seq', [(i, (i + k) % 4) for i in range(4)])  21 us
    pallas_call x1, Pallas kernels, recv_half(): pl.pallas_call(recv_kernel, out_shape=(jax.ShapeDtypeStruct((QUARTER, PAI...  14.9 us
    ppermute x12, starting transfers between devices, shifted(): return lax.ppermute(array, 'seq', [(i, (i + k) % 4) for i in range(4)])  14.7 us
    pallas_call x1, Pallas kernels, own_field(): pl.pallas_call(own_field_kernel, out_shape=(jax.ShapeDtypeStruct((RES, SE...  11.2 us
    pallas_call x1, Pallas kernels, own_grad(): pl.pallas_call(own_grad_kernel, out_shape=(jax.ShapeDtypeStruct((TILE, PA...  8.3 us
    pallas_call x1, Pallas kernels, recv_order(): pl.pallas_call(recv_order_kernel, out_shape=(jax.ShapeDtypeStruct((PAIRS,...  4.3 us
  transfers between devices with their start and end apart: 14, of which 9 were waited for; matrix products, arithmetic and copies ran while one was open for 0% of the time, Pallas kernels for 22%

profile of v2, /device:TPU:1, one launch (start us, length us, event | category | flops | bytes accessed | tf_op | source)
XLA Modules:
  0.0 106.8 jit_solution(5921671076136597848)
XLA Ops:
  0.6 2.0 %pack_pairs.1.pack = bf16[512,128]{1,0:T(8,128)(2,1)} custom-call(bf16[441,512]{1,0:T(8,128)(2,1)} %bitcast.16, s32[1,512]{1,0:T(1,128)} %bitcast.23, s32[1,512]{1,0:T(1,128)} %bitcast.24, s32[1,256]{1,0:T(1,128)} %bitcast.25, s32[1,64]{1,0:T(1,128)} %bitcast.26), custom_call_target="tpu_custom_call" | custom-call | tf_op jit(solution)/shard_map/pack_pairs/pallas_call | solution.py:70
  2.6 13.0 %all-to-all-start = ((bf16[64,8,128]{2,1,0:T(8,128)(2,1)}), bf16[64,8,128]{2,1,0:T(8,128)(2,1)S(1)}, u32[]{:S(2)}, u32[]{:S(2)}) async-start(bf16[64,8,128]{2,1,0:T(8,128)(2,1)} %bitcast.15), calls=%async_computation | async-start | bytes 262144 | tf_op jit(solution)/shard_map/all_to_all | solution.py:508
  15.6 11.2 %own_field.1 = (bf16[3072,256]{1,0:T(8,128)(2,1)}, bf16[512,256]{1,0:T(8,128)(2,1)}, f32[8,512]{1,0:T(8,128)}, f32[4,8,128]{2,1,0:T(8,128)}, f32[6,192,256]{2,1,0:T(8,128)}) custom-call(s32[3072,256]{1,0:T(8,128)} %alignment.1, bf16[512,128]{1,0:T(8,128)(2,1)} %pack_pairs.1.pack, bf16[441,512]{1,0:T(8,128)(2,1)} %bitcast.17), custom_call_target="tpu_custom_call" | custom-call | flops 10000000000 | bytes 10000000 | tf_op jit(solution)/shard_map/own_field/pallas_call | solution.py:241
  26.8 0.0 all-to-all-done
  26.8 0.0 copy-start.2
  26.8 2.7 %collective-permute-start.2 = (bf16[512,128]{1,0:T(8,128)(2,1)S(1)}, bf16[512,128]{1,0:T(8,128)(2,1)S(1)}, u32[]{:S(2)}, u32[]{:S(2)}) collective-permute-start(bf16[512,128]{1,0:T(8,128)(2,1)S(1)} %bitcast.18), channel_id=1, source_target_pairs={{0,192},{64,0},{128,64},{192,128},{1,193},{65,1},{129,65},{193,129... | collective-permute-start | bytes 393224 | tf_op jit(solution)/shard_map/ppermute | solution.py:495
  29.5 0.3 collective-permute-start.1
  29.9 0.7 collective-permute-start
  30.6 0.0 copy-done.2
  30.6 4.3 %recv_order.1 = (bf16[512,256]{1,0:T(8,128)(2,1)}, f32[8,512]{1,0:T(8,128)}, f32[4,8,128]{2,1,0:T(8,128)}, bf16[48,256]{1,0:T(8,128)(2,1)}) custom-call(bf16[512,128]{1,0:T(8,128)(2,1)} %bitcast.21, bf16[3072,256]{1,0:T(8,128)(2,1)} %get-tuple-element.37.states), custom_call_target="tpu_custom_call" | custom-call | flops 5000000000 | bytes 3000000 | tf_op jit(solution)/shard_map/recv_order/pallas_call | solution.py:277
  34.9 0.3 collective-permute-done.2.q3
  35.1 0.0 copy-start.3
  35.1 0.8 collective-permute-done.1.q2
  35.9 0.0 copy-start.4
  35.9 3.3 %collective-permute-done.q1 = bf16[512,128]{1,0:T(8,128)(2,1)S(1)} collective-permute-done((bf16[512,128]{1,0:T(8,128)(2,1)S(1)}, bf16[512,128]{1,0:T(8,128)(2,1)S(1)}, u32[]{:S(2)}, u32[]{:S(2)}) %collective-permute-start) | collective-permute-done | bytes 131104 | tf_op jit(solution)/shard_map/ppermute | solution.py:495
  39.2 0.0 copy-start.5
  39.2 0.0 copy-done.3
  39.2 0.0 copy-done.4
  39.3 0.6 copy-done.5
  39.9 14.9 %recv_half.1 = (bf16[112,512]{1,0:T(8,128)(2,1)}, bf16[112,512]{1,0:T(8,128)(2,1)}, bf16[112,512]{1,0:T(8,128)(2,1)}, bf16[112,512]{1,0:T(8,128)(2,1)}, bf16[6,192,256]{2,1,0:T(8,128)(2,1)}, /*index=5*/f32[24,128]{1,0:T(8,128)}) custom-call(bf16[512,128]{1,0:T(8,128)(2,1)} %bitcast.22, bf16[512,128]{1,0:T(8,128)(2,1)} %copy-done.5, ...), custom_call_target="tpu_custom_call" | custom-call | flops 20000000000 | bytes 10000000 | tf_op jit(solution)/shard_map/recv_half/pallas_call | solution.py:352
  54.8 0.0 collective-permute-start.3
  54.8 1.0 collective-permute-start.4
  55.8 1.7 %collective-permute-start.5 = (bf16[112,512]{1,0:T(8,128)(2,1)}, bf16[112,512]{1,0:T(8,128)(2,1)S(1)}, u32[]{:S(2)}, u32[]{:S(2)}) collective-permute-start(bf16[112,512]{1,0:T(8,128)(2,1)} %get-tuple-element.46), channel_id=1, source_target_pairs={{0,192},{64,0},{128,64},{192,128},{1,193},{65,1},{129,65},{193,129... | collective-permute-start | bytes 344072 | tf_op jit(solution)/shard_map/ppermute | solution.py:495
  57.5 0.0 copy-start.1
  57.5 8.3 %own_grad.1 = (bf16[128,512]{1,0:T(8,128)(2,1)}, bf16[128,512]{1,0:T(8,128)(2,1)}, bf16[128,512]{1,0:T(8,128)(2,1)}, bf16[128,512]{1,0:T(8,128)(2,1)}) custom-call(f32[4,8,128]{2,1,0:T(8,128)} %get-tuple-element.47.keys_ref, f32[8,512]{1,0:T(8,128)} %get-tuple-element.48.place, bf16[512,256]{1,0:T(8,128)(2,1)} %get-tuple-element.49.far, ...), custom_call_target="tpu_custom_call" | custom-call | flops 6000000000 | bytes 8000000 | tf_op jit(solution)/shard_map/own_grad/pallas_call | solution.py:408
  65.8 0.0 collective-permute-done.3.r1
  65.8 0.0 collective-permute-done.4.r2
  65.8 0.0 collective-permute-done.5.r3
  65.8 0.0 copy-done.1
  65.8 0.8 sum_back.1
  66.6 11.5 %all-to-all-start.1 = ((bf16[64,8,128]{2,1,0:T(8,128)(2,1)}), bf16[64,8,128]{2,1,0:T(8,128)(2,1)S(1)}, u32[]{:S(2)}, u32[]{:S(2)}) async-start(bf16[64,8,128]{2,1,0:T(8,128)(2,1)} %bitcast.9), calls=%async_computation.1 | async-start | bytes 262144 | tf_op jit(solution)/shard_map/all_to_all | solution.py:508
  78.1 0.6 collective-permute-start.6
  78.8 2.2 %collective-permute-start.7 = (bf16[128,512]{1,0:T(8,128)(2,1)}, bf16[128,512]{1,0:T(8,128)(2,1)S(1)}, u32[]{:S(2)}, u32[]{:S(2)}) collective-permute-start(bf16[128,512]{1,0:T(8,128)(2,1)} %get-tuple-element.58), channel_id=1, source_target_pairs={{0,128},{64,192},{128,0},{192,64},{1,129},{65,193},{129,1},{193,65... | collective-permute-start | bytes 393224 | tf_op jit(solution)/shard_map/ppermute | solution.py:495
  80.9 2.0 %collective-permute-start.8 = (bf16[128,512]{1,0:T(8,128)(2,1)}, bf16[128,512]{1,0:T(8,128)(2,1)S(1)}, u32[]{:S(2)}, u32[]{:S(2)}) collective-permute-start(bf16[128,512]{1,0:T(8,128)(2,1)} %get-tuple-element.59), channel_id=1, source_target_pairs={{0,192},{64,0},{128,64},{192,128},{1,193},{65,1},{129,65},{193,129... | collective-permute-start | bytes 393224 | tf_op jit(solution)/shard_map/ppermute | solution.py:495
  82.9 1.3 %collective-permute-done.6.r1 = bf16[128,512]{1,0:T(8,128)(2,1)S(1)} collective-permute-done((bf16[128,512]{1,0:T(8,128)(2,1)}, bf16[128,512]{1,0:T(8,128)(2,1)S(1)}, u32[]{:S(2)}, u32[]{:S(2)}) %collective-permute-start.6) | collective-permute-done | bytes 131104 | tf_op jit(solution)/shard_map/ppermute | solution.py:495
  84.2 3.1 %collective-permute-done.7.r2 = bf16[128,512]{1,0:T(8,128)(2,1)S(1)} collective-permute-done((bf16[128,512]{1,0:T(8,128)(2,1)}, bf16[128,512]{1,0:T(8,128)(2,1)S(1)}, u32[]{:S(2)}, u32[]{:S(2)}) %collective-permute-start.7) | collective-permute-done | bytes 131104 | tf_op jit(solution)/shard_map/ppermute | solution.py:495
  87.3 0.0 collective-permute-done.8.r3
  87.3 1.2 %all-to-all-done.1 = bf16[64,8,128]{2,1,0:T(8,128)(2,1)S(1)} async-done(((bf16[64,8,128]{2,1,0:T(8,128)(2,1)}), bf16[64,8,128]{2,1,0:T(8,128)(2,1)S(1)}, u32[]{:S(2)}, u32[]{:S(2)}) %all-to-all-start.1) | async-done | bytes 131104 | tf_op jit(solution)/shard_map/all_to_all | solution.py:508
  88.5 0.0 copy-start
  88.5 0.9 copy-done
  89.4 0.7 join_parts.1
  90.1 1.7 %collective-permute-start.11 = (f32[112,512]{1,0:T(8,128)S(1)}, f32[112,512]{1,0:T(8,128)S(1)}, u32[]{:S(2)}, u32[]{:S(2)}) collective-permute-start(f32[112,512]{1,0:T(8,128)S(1)} %get-tuple-element.64.c0), channel_id=1, source_target_pairs={{0,192},{64,0},{128,64},{192,128},{1,193},{65,1},{129,65},{193,129... | collective-permute-start | bytes 688136 | tf_op jit(solution)/shard_map/ppermute | solution.py:495
  91.8 0.9 collective-permute-start.10
  92.7 0.9 collective-permute-start.9
  93.6 3.3 %collective-permute-done.11.c3 = f32[112,512]{1,0:T(8,128)S(1)} collective-permute-done((f32[112,512]{1,0:T(8,128)S(1)}, f32[112,512]{1,0:T(8,128)S(1)}, u32[]{:S(2)}, u32[]{:S(2)}) %collective-permute-start.11) | collective-permute-done | bytes 229408 | tf_op jit(solution)/shard_map/ppermute | solution.py:495
  96.8 2.1 %collective-permute-done.10.c2 = f32[112,512]{1,0:T(8,128)S(1)} collective-permute-done((f32[112,512]{1,0:T(8,128)S(1)}, f32[112,512]{1,0:T(8,128)S(1)}, u32[]{:S(2)}, u32[]{:S(2)}) %collective-permute-start.10) | collective-permute-done | bytes 229408 | tf_op jit(solution)/shard_map/ppermute | solution.py:495
  99.0 6.8 %collective-permute-done.9.c1 = f32[112,512]{1,0:T(8,128)S(1)} collective-permute-done((f32[112,512]{1,0:T(8,128)S(1)}, f32[112,512]{1,0:T(8,128)S(1)}, u32[]{:S(2)}, u32[]{:S(2)}) %collective-permute-start.9) | collective-permute-done | bytes 229408 | tf_op jit(solution)/shard_map/ppermute | solution.py:495
  105.7 1.1 place_parts.1
Async XLA Ops:
  2.6 24.2 %all-to-all-start = ((bf16[64,8,128]{2,1,0:T(8,128)(2,1)}), bf16[64,8,128]{2,1,0:T(8,128)(2,1)S(1)}, u32[]{:S(2)}, u32[]{:S(2)}) async-start(bf16[64,8,128]{2,1,0:T(8,128)(2,1)} %bitcast.15), calls=%async_computation | async-start | bytes 262144 | tf_op jit(solution)/shard_map/all_to_all | solution.py:508
  26.8 3.8 %copy-start.2 = (bf16[64,8,128]{2,1,0:T(8,128)(2,1)}, bf16[64,8,128]{2,1,0:T(8,128)(2,1)S(1)}, u32[]{:S(2)}) copy-start(bf16[64,8,128]{2,1,0:T(8,128)(2,1)S(1)} %all-to-all-done) | copy-start | bytes 393220
  26.8 8.4 %collective-permute-start.2 = (bf16[512,128]{1,0:T(8,128)(2,1)S(1)}, bf16[512,128]{1,0:T(8,128)(2,1)S(1)}, u32[]{:S(2)}, u32[]{:S(2)}) collective-permute-start(bf16[512,128]{1,0:T(8,128)(2,1)S(1)} %bitcast.18), channel_id=1, source_target_pairs={{0,192},{64,0},{128,64},{192,128},{1,193},{65,1},{129,65},{193,129... | collective-permute-start | bytes 393224 | tf_op jit(solution)/shard_map/ppermute | solution.py:495
  29.5 6.4 %collective-permute-start.1 = (bf16[512,128]{1,0:T(8,128)(2,1)S(1)}, bf16[512,128]{1,0:T(8,128)(2,1)S(1)}, u32[]{:S(2)}, u32[]{:S(2)}) collective-permute-start(bf16[512,128]{1,0:T(8,128)(2,1)S(1)} %bitcast.19), channel_id=1, source_target_pairs={{0,128},{64,192},{128,0},{192,64},{1,129},{65,193},{129,1},{193,65... | collective-permute-start | bytes 393224 | tf_op jit(solution)/shard_map/ppermute | solution.py:495
  29.9 9.4 %collective-permute-start = (bf16[512,128]{1,0:T(8,128)(2,1)S(1)}, bf16[512,128]{1,0:T(8,128)(2,1)S(1)}, u32[]{:S(2)}, u32[]{:S(2)}) collective-permute-start(bf16[512,128]{1,0:T(8,128)(2,1)S(1)} %bitcast.20), channel_id=1, source_target_pairs={{0,64},{64,128},{128,192},{192,0},{1,65},{65,129},{129,193},{193,1... | collective-permute-start | bytes 393224 | tf_op jit(solution)/shard_map/ppermute | solution.py:495
  35.1 4.1 %copy-start.3 = (bf16[512,128]{1,0:T(8,128)(2,1)}, bf16[512,128]{1,0:T(8,128)(2,1)S(1)}, u32[]{:S(2)}) copy-start(bf16[512,128]{1,0:T(8,128)(2,1)S(1)} %collective-permute-done.2.q3) | copy-start | bytes 393220
  35.9 3.3 %copy-start.4 = (bf16[512,128]{1,0:T(8,128)(2,1)}, bf16[512,128]{1,0:T(8,128)(2,1)S(1)}, u32[]{:S(2)}) copy-start(bf16[512,128]{1,0:T(8,128)(2,1)S(1)} %collective-permute-done.1.q2) | copy-start | bytes 393220
  39.2 0.7 copy-start.5
  54.8 11.0 %collective-permute-start.3 = (bf16[112,512]{1,0:T(8,128)(2,1)}, bf16[112,512]{1,0:T(8,128)(2,1)S(1)}, u32[]{:S(2)}, u32[]{:S(2)}) collective-permute-start(bf16[112,512]{1,0:T(8,128)(2,1)} %get-tuple-element.44), channel_id=1, source_target_pairs={{0,64},{64,128},{128,192},{192,0},{1,65},{65,129},{129,193},{193,1... | collective-permute-start | bytes 344072 | tf_op jit(solution)/shard_map/ppermute | solution.py:495
  54.8 11.0 %collective-permute-start.4 = (bf16[112,512]{1,0:T(8,128)(2,1)}, bf16[112,512]{1,0:T(8,128)(2,1)S(1)}, u32[]{:S(2)}, u32[]{:S(2)}) collective-permute-start(bf16[112,512]{1,0:T(8,128)(2,1)} %get-tuple-element.45), channel_id=1, source_target_pairs={{0,128},{64,192},{128,0},{192,64},{1,129},{65,193},{129,1},{193,65... | collective-permute-start | bytes 344072 | tf_op jit(solution)/shard_map/ppermute | solution.py:495
  55.8 10.0 %collective-permute-start.5 = (bf16[112,512]{1,0:T(8,128)(2,1)}, bf16[112,512]{1,0:T(8,128)(2,1)S(1)}, u32[]{:S(2)}, u32[]{:S(2)}) collective-permute-start(bf16[112,512]{1,0:T(8,128)(2,1)} %get-tuple-element.46), channel_id=1, source_target_pairs={{0,192},{64,0},{128,64},{192,128},{1,193},{65,1},{129,65},{193,129... | collective-permute-start | bytes 344072 | tf_op jit(solution)/shard_map/ppermute | solution.py:495
  57.5 8.3 %copy-start.1 = (bf16[112,512]{1,0:T(8,128)(2,1)S(1)}, bf16[112,512]{1,0:T(8,128)(2,1)}, u32[]{:S(2)}) copy-start(bf16[112,512]{1,0:T(8,128)(2,1)} %get-tuple-element.60.mine) | copy-start | bytes 344068
  66.6 21.9 %all-to-all-start.1 = ((bf16[64,8,128]{2,1,0:T(8,128)(2,1)}), bf16[64,8,128]{2,1,0:T(8,128)(2,1)S(1)}, u32[]{:S(2)}, u32[]{:S(2)}) async-start(bf16[64,8,128]{2,1,0:T(8,128)(2,1)} %bitcast.9), calls=%async_computation.1 | async-start | bytes 262144 | tf_op jit(solution)/shard_map/all_to_all | solution.py:508
  78.1 6.1 %collective-permute-start.6 = (bf16[128,512]{1,0:T(8,128)(2,1)}, bf16[128,512]{1,0:T(8,128)(2,1)S(1)}, u32[]{:S(2)}, u32[]{:S(2)}) collective-permute-start(bf16[128,512]{1,0:T(8,128)(2,1)} %get-tuple-element.57), channel_id=1, source_target_pairs={{0,64},{64,128},{128,192},{192,0},{1,65},{65,129},{129,193},{193,1... | collective-permute-start | bytes 393224 | tf_op jit(solution)/shard_map/ppermute | solution.py:495
  78.8 8.6 %collective-permute-start.7 = (bf16[128,512]{1,0:T(8,128)(2,1)}, bf16[128,512]{1,0:T(8,128)(2,1)S(1)}, u32[]{:S(2)}, u32[]{:S(2)}) collective-permute-start(bf16[128,512]{1,0:T(8,128)(2,1)} %get-tuple-element.58), channel_id=1, source_target_pairs={{0,128},{64,192},{128,0},{192,64},{1,129},{65,193},{129,1},{193,65... | collective-permute-start | bytes 393224 | tf_op jit(solution)/shard_map/ppermute | solution.py:495
  80.9 6.4 %collective-permute-start.8 = (bf16[128,512]{1,0:T(8,128)(2,1)}, bf16[128,512]{1,0:T(8,128)(2,1)S(1)}, u32[]{:S(2)}, u32[]{:S(2)}) collective-permute-start(bf16[128,512]{1,0:T(8,128)(2,1)} %get-tuple-element.59), channel_id=1, source_target_pairs={{0,192},{64,0},{128,64},{192,128},{1,193},{65,1},{129,65},{193,129... | collective-permute-start | bytes 393224 | tf_op jit(solution)/shard_map/ppermute | solution.py:495
  88.5 0.9 copy-start
  90.1 6.7 %collective-permute-start.11 = (f32[112,512]{1,0:T(8,128)S(1)}, f32[112,512]{1,0:T(8,128)S(1)}, u32[]{:S(2)}, u32[]{:S(2)}) collective-permute-start(f32[112,512]{1,0:T(8,128)S(1)} %get-tuple-element.64.c0), channel_id=1, source_target_pairs={{0,192},{64,0},{128,64},{192,128},{1,193},{65,1},{129,65},{193,129... | collective-permute-start | bytes 688136 | tf_op jit(solution)/shard_map/ppermute | solution.py:495
  91.8 7.2 %collective-permute-start.10 = (f32[112,512]{1,0:T(8,128)S(1)}, f32[112,512]{1,0:T(8,128)S(1)}, u32[]{:S(2)}, u32[]{:S(2)}) collective-permute-start(f32[112,512]{1,0:T(8,128)S(1)} %get-tuple-element.64.c0), channel_id=1, source_target_pairs={{0,128},{64,192},{128,0},{192,64},{1,129},{65,193},{129,1},{193,65... | collective-permute-start | bytes 688136 | tf_op jit(solution)/shard_map/ppermute | solution.py:495
  92.7 13.0 %collective-permute-start.9 = (f32[112,512]{1,0:T(8,128)S(1)}, f32[112,512]{1,0:T(8,128)S(1)}, u32[]{:S(2)}, u32[]{:S(2)}) collective-permute-start(f32[112,512]{1,0:T(8,128)S(1)} %get-tuple-element.64.c0), channel_id=1, source_target_pairs={{0,64},{64,128},{128,192},{192,0},{1,65},{65,129},{129,193},{193,1... | collective-permute-start | bytes 688136 | tf_op jit(solution)/shard_map/ppermute | solution.py:495

commit v3 on v2

v3 whole, which is shorter than its diff:
```python
import functools

import jax
import jax.numpy as jnp
from jax import lax
from jax.experimental import pallas as pl
from jax.experimental.pallas import tpu as pltpu
from jax.sharding import PartitionSpec as P

Q = 21
QP = 24
RL = 48
CAP = 8
SLOTS = 4
PAIRS = 512
BLOCKS = 64
SEQ = 256
RES = 3072
TILE = 128
WIDE = PAIRS // TILE
SPAN = 64
TILES = PAIRS // SPAN
DUOS = (Q + 1) // 2
GROUP = 8
GROUPS = RL // GROUP
GROWS = GROUP * QP
QUARTER = 112
PADQ = 4 * QUARTER
DEEP = DUOS * TILE
F32 = jnp.float32
BF16 = jnp.bfloat16
VMEM = pl.BlockSpec(memory_space=pltpu.VMEM)
SMEM = pl.BlockSpec(memory_space=pltpu.SMEM)
ANY = pl.BlockSpec(memory_space=pl.ANY)
PARAMS = pltpu.CompilerParams(vmem_limit_bytes=24 * 1024 * 1024)
LARGE = pltpu.CompilerParams(vmem_limit_bytes=56 * 1024 * 1024)
SMALL = pltpu.CompilerParams(vmem_limit_bytes=16 * 1024 * 1024)
SENT = BF16


def iota(shape, dim):
    return lax.broadcasted_iota(jnp.int32, shape, dim)


def dot(x, y):
    return jnp.dot(x, y, preferred_element_type=F32)


def pack_kernel(coup, left, slot, residue, count, out, wide):
    wide[...] = jnp.zeros_like(wide)
    wide[0 : Q * Q, :] = coup[...].astype(F32)
    lane = iota((1, PAIRS), 1)
    bucket = lax.shift_right_logical(lane, 3)
    wanted = bucket * SLOTS + slot[...]
    pick = jnp.where(iota((BLOCKS * SLOTS, PAIRS), 0) == wanted, 1.0, 0.0).astype(BF16)
    partner = dot(jnp.broadcast_to(residue[...], (8, BLOCKS * SLOTS)).astype(F32).astype(BF16), pick)
    spread = jnp.where(iota((BLOCKS, PAIRS), 0) == bucket, 1.0, 0.0).astype(BF16)
    counts = dot(jnp.broadcast_to(count[...], (8, BLOCKS)).astype(F32).astype(BF16), spread)
    live = jnp.where((lane & (CAP - 1)).astype(F32) < counts[0:1], 1.0, 0.0)
    sub = iota((16, PAIRS), 0)
    index = jnp.where(sub == 0, left[...].astype(F32), 0.0)
    index = jnp.where(sub == 1, partner[0:1], index)
    index = jnp.where(sub == 2, live, index)
    index = jnp.where(sub == 3, lax.axis_index("res").astype(F32), index)
    index = jnp.where(sub == 4, bucket.astype(F32), index)
    for n in range(4):
        part = jnp.concatenate([wide[n * QUARTER : (n + 1) * QUARTER, :], index], axis=0)
        out[:, n * TILE : (n + 1) * TILE] = jnp.transpose(part).astype(BF16)


def pack_pairs(coup, left, slot, residue, count):
    return pl.pallas_call(
        pack_kernel,
        out_shape=jax.ShapeDtypeStruct((PAIRS, 4 * TILE), BF16),
        in_specs=[VMEM] * 5,
        out_specs=VMEM,
        scratch_shapes=[pltpu.VMEM((PADQ, PAIRS), F32)],
        compiler_params=LARGE,
        name="pack_pairs",
    )(coup, left, slot, residue, count)


def order_half(pack, flipped, own):
    mine, other, block = (112, 113, 116) if own else (113, 112, 115)
    wide = pack.astype(F32)
    key_row = jnp.where(flipped[114:115] > 0.5, flipped[mine : mine + 1], float(RL))
    key_col = jnp.where(wide[:, 114:115] > 0.5, wide[:, mine : mine + 1], float(RL))
    lane = iota((PAIRS, PAIRS), 1).astype(F32)
    sub = iota((PAIRS, PAIRS), 0).astype(F32)
    full_row = key_row * PAIRS + lane
    full_col = key_col * PAIRS + sub
    place_row = jnp.sum(jnp.where(full_col < full_row, 1.0, 0.0), axis=0, keepdims=True)
    place_col = jnp.sum(jnp.where(full_row < full_col, 1.0, 0.0), axis=1, keepdims=True)
    to_sorted = jnp.where(place_col == lane, 1.0, 0.0).astype(BF16)
    to_plain = jnp.where(place_row == sub, 1.0, 0.0).astype(BF16)
    cols = dot(to_plain, pack)
    far = cols[:, block : block + 1] * RL + cols[:, other : other + 1]
    keys = dot(jnp.broadcast_to(key_row, (8, PAIRS)).astype(BF16), to_sorted)
    return to_sorted, place_row, far, keys


def plain_order(place):
    return jnp.where(place[0:1] == iota((PAIRS, PAIRS), 0).astype(F32), 1.0, 0.0).astype(BF16)


def sorted_order(place):
    col = jnp.transpose(jnp.broadcast_to(place[0:1], (TILE, PAIRS)))[:, 0:1]
    return jnp.where(col == iota((PAIRS, PAIRS), 1).astype(F32), 1.0, 0.0).astype(BF16)


def find_far(far, states):
    far_states = jnp.zeros((PAIRS, SEQ), F32)
    chunk = 256
    lane = iota((PAIRS, chunk), 1).astype(F32)
    for n in range(RES // chunk):
        pick = jnp.where(far - float(n * chunk) == lane, 1.0, 0.0).astype(BF16)
        far_states = far_states + dot(pick, states[n * chunk : (n + 1) * chunk, :])
    return far_states


def fill_hot(far, j, hot):
    tile = far[pl.ds(pl.multiple_of(j * SPAN, SPAN), SPAN), :].astype(F32)
    for c in range(2 * DUOS):
        hot[j, c * SPAN : (c + 1) * SPAN, :] = jnp.where(tile == float(c), 1.0, 0.0).astype(BF16)


def halves(first, second):
    low = iota(first.shape, 1) < SPAN
    return (
        jnp.where(low, first, pltpu.roll(second, SPAN, 1)),
        jnp.where(low, pltpu.roll(first, SPAN, 1), second),
    )


def store_keys(keys, keys_ref, bounds):
    for n in range(WIDE):
        part = keys[:, n * TILE : (n + 1) * TILE]
        for i, span in enumerate(halves(part, part)):
            j = 2 * n + i
            keys_ref[j] = span
            bounds[0, j], bounds[1, j] = group_range(span)


def store_blocks(block, n, blocks):
    for d in range(DUOS):
        second = block(2 * d + 1) if 2 * d + 1 < Q else jnp.zeros((QP, TILE), F32)
        blocks[2 * n, d], blocks[2 * n + 1, d] = halves(block(2 * d), second)


def load_grad(grad, n):
    columns = []
    for d in range(DUOS):
        columns.extend(halves(grad[2 * n, d], grad[2 * n + 1, d]))
    return columns[:Q]


def group_range(keys):
    low = jnp.min(keys).astype(jnp.int32)
    high = jnp.max(jnp.where(keys < RL - 0.5, keys, -1.0)).astype(jnp.int32)
    return low // GROUP, (high + GROUP) // GROUP


def group_masks(keys, g):
    base = (g * GROUP).astype(F32)
    wide = jnp.broadcast_to(keys[0:1], (QP, TILE))
    return [wide == base + float(m) for m in range(GROUP)]


def add_field(keys_ref, bounds, blocks, far, hot, lhs, field):
    def tile_step(j, carry):
        keys = keys_ref[j]
        low, high = bounds[0, j], bounds[1, j]

        @pl.when(low < high)
        def _():
            fill_hot(far, j, hot)

        def group_step(g, carry):
            masks = group_masks(keys, g)
            for d in range(DUOS):
                block = blocks[j, d]
                rows = [jnp.where(mask, block, 0.0) for mask in masks]
                lhs[:, d * TILE : (d + 1) * TILE] = jnp.concatenate(rows, axis=0).astype(BF16)
            field[g] += dot(lhs[...], hot[j])
            return carry

        return lax.fori_loop(low, high, group_step, carry)

    lax.fori_loop(0, TILES, tile_step, 0)


def add_grad(keys_ref, bounds, resid, hot, grad, far=None):
    grad[...] = jnp.zeros_like(grad)

    def tile_step(j, carry):
        keys = keys_ref[j]
        low, high = bounds[0, j], bounds[1, j]
        if far is not None:

            @pl.when(low < high)
            def _():
                fill_hot(far, j, hot)

        def group_step(g, carry):
            masks = group_masks(keys, g)
            rows = resid[g]
            for d in range(0, DUOS, 2):
                count = min(2, DUOS - d)
                part = hot[j, d * TILE : (d + count) * TILE, :]
                out = lax.dot_general(
                    rows, part, (((1,), (1,)), ((), ())), preferred_element_type=F32
                )
                for i in range(count):
                    total = grad[j, d + i]
                    for m in range(GROUP):
                        piece = out[m * QP : (m + 1) * QP, i * TILE : (i + 1) * TILE]
                        total = jnp.where(masks[m], piece, total)
                    grad[j, d + i] = total
            return carry

        return lax.fori_loop(low, high, group_step, carry)

    lax.fori_loop(0, TILES, tile_step, 0)


def store_quarters(full, outs):
    seq_index = lax.axis_index("seq")
    for k, out in enumerate(outs):
        owner = lax.rem(seq_index + k, 4)
        out[0:QUARTER, :] = full[pl.ds(pl.multiple_of(owner * QUARTER, 8), QUARTER), :].astype(BF16)


def own_field_kernel(
    alignment, pack, coup, states, far_out, place_out, keys_ref, bounds, field,
    sorted_blocks, blocks, hot, lhs,
):
    chunk = 512
    parts = [slice(n * chunk, (n + 1) * chunk) for n in range(RES // chunk)]
    packed = pack[:, 0:TILE]
    flipped = jnp.transpose(packed.astype(F32))
    to_sorted, place, far, keys = order_half(packed, flipped, True)
    place_out[...] = jnp.broadcast_to(place, (8, PAIRS))
    store_keys(keys, keys_ref, bounds)
    sorted_blocks[...] = jnp.zeros_like(sorted_blocks)
    ordered = dot(coup[...], to_sorted)
    for n in range(WIDE):
        sorted_blocks[n, 0 : Q * Q, :] = ordered[:, n * TILE : (n + 1) * TILE]
        store_blocks(lambda c: sorted_blocks[n, pl.ds(c, QP, stride=Q), :], n, blocks)
    field[...] = jnp.zeros_like(field)
    far_states = jnp.zeros((PAIRS, SEQ), F32)
    lane = iota((PAIRS, chunk), 1).astype(F32)
    for n, rows in enumerate(parts):
        part = alignment[rows, :].astype(F32).astype(BF16)
        states[rows, :] = part
        pick = jnp.where(far - float(n * chunk) == lane, 1.0, 0.0).astype(BF16)
        far_states = far_states + dot(pick, part)
    far_out[...] = far_states.astype(BF16)
    add_field(keys_ref, bounds, blocks, far_out, hot, lhs, field)


def own_field(alignment, pack, coup):
    return pl.pallas_call(
        own_field_kernel,
        out_shape=(
            jax.ShapeDtypeStruct((RES, SEQ), BF16),
            jax.ShapeDtypeStruct((PAIRS, SEQ), BF16),
            jax.ShapeDtypeStruct((8, PAIRS), F32),
            jax.ShapeDtypeStruct((TILES, 8, TILE), F32),
            jax.ShapeDtypeStruct((2, TILES), jnp.int32),
            jax.ShapeDtypeStruct((GROUPS, GROWS, SEQ), F32),
        ),
        in_specs=[VMEM, VMEM, VMEM],
        out_specs=(VMEM, VMEM, VMEM, VMEM, SMEM, VMEM),
        scratch_shapes=[
            pltpu.VMEM((WIDE, 512, TILE), F32),
            pltpu.VMEM((TILES, DUOS, QP, TILE), F32),
            pltpu.VMEM((TILES, DEEP, SEQ), BF16),
            pltpu.VMEM((GROWS, DEEP), BF16),
        ],
        compiler_params=PARAMS,
        cost_estimate=pl.CostEstimate(
            flops=10_000_000_000, bytes_accessed=10_000_000, transcendentals=0
        ),
        name="own_field",
    )(alignment, pack, coup)


def recv_order_kernel(pack, states, far_out, place_out, keys_ref, bounds, codes):
    packed = pack[:, 0:TILE]
    flipped = jnp.transpose(packed.astype(F32))
    to_sorted, place, far, keys = order_half(packed, flipped, False)
    store_keys(keys, keys_ref, bounds)
    place_out[...] = jnp.broadcast_to(place, (8, PAIRS))
    far_out[...] = find_far(far, states).astype(BF16)
    codes[...] = states[pl.ds(pl.multiple_of(lax.axis_index("res") * RL, 16), RL), :]


def recv_order(pack, states):
    return pl.pallas_call(
        recv_order_kernel,
        out_shape=(
            jax.ShapeDtypeStruct((PAIRS, SEQ), BF16),
            jax.ShapeDtypeStruct((8, PAIRS), F32),
            jax.ShapeDtypeStruct((TILES, 8, TILE), F32),
            jax.ShapeDtypeStruct((2, TILES), jnp.int32),
            jax.ShapeDtypeStruct((RL, SEQ), BF16),
        ),
        in_specs=[VMEM] * 2,
        out_specs=(VMEM, VMEM, VMEM, SMEM, VMEM),
        compiler_params=PARAMS,
        cost_estimate=pl.CostEstimate(
            flops=5_000_000_000, bytes_accessed=3_000_000, transcendentals=0
        ),
        name="recv_order",
    )(pack, states)


def recv_kernel(
    parts, far, place, keys_ref, bounds, codes, own, fields, weights,
    grad_out, resid_out, field_out,
    wide, sorted_blocks, blocks, hot, lhs, field, grad,
):
    for n in range(4):
        flipped = jnp.transpose(parts[:, n * TILE : (n + 1) * TILE].astype(F32))
        wide[n * QUARTER : (n + 1) * QUARTER, :] = flipped[0:QUARTER]
    sorted_blocks[PADQ:512, :] = jnp.zeros((512 - PADQ, PAIRS), F32)
    sorted_blocks[0:PADQ, :] = dot(wide[...].astype(BF16), sorted_order(place))
    for n in range(WIDE):
        lanes = slice(n * TILE, (n + 1) * TILE)
        store_blocks(lambda a: sorted_blocks[a * Q : a * Q + QP, lanes], n, blocks)
    field[...] = own[...]
    add_field(keys_ref, bounds, blocks, far, hot, lhs, field)

    my_codes = codes[...].astype(F32)
    state = iota((QP, SEQ), 0).astype(F32)
    weight = weights[...]
    lane = iota((QP, TILE), 1)
    local = jnp.concatenate([fields[...], jnp.full((QP - Q, RL), -1e30, F32)], axis=0)
    for g in range(GROUPS):
        pieces = []
        for m in range(GROUP):
            r = g * GROUP + m
            logits = field[g, m * QP : (m + 1) * QP, :] + local[:, r : r + 1]
            top = jnp.max(logits, axis=0, keepdims=True)
            raised = jnp.exp(logits - top)
            share = weight / jnp.sum(raised, axis=0, keepdims=True)
            hot_own = jnp.where(state == my_codes[r : r + 1], weight, 0.0)
            pieces.append(raised * share - hot_own)
        resid_out[g] = jnp.concatenate(pieces, axis=0).astype(BF16)
    field_part = jnp.zeros((QP, TILE), F32)
    ones = jnp.ones((SEQ, TILE), BF16)
    for g in range(GROUPS):
        sums = dot(resid_out[g], ones)
        for m in range(GROUP):
            piece = sums[m * QP : (m + 1) * QP]
            field_part = jnp.where(lane == g * GROUP + m, piece, field_part)
    field_out[...] = field_part

    add_grad(keys_ref, bounds, resid_out, hot, grad)
    wide[Q * Q // 8 * 8 : PADQ, :] = jnp.zeros((PADQ - Q * Q // 8 * 8, PAIRS), F32)
    for n in range(WIDE):
        for a, column in enumerate(load_grad(grad, n)):
            wide[a * Q : (a + 1) * Q, n * TILE : (n + 1) * TILE] = column[0:Q]
    plain = dot(wide[...].astype(BF16), plain_order(place))
    rest = jnp.zeros((TILE - QUARTER, PAIRS), F32)
    for n in range(4):
        part = jnp.concatenate([plain[n * QUARTER : (n + 1) * QUARTER], rest], axis=0)
        grad_out[n] = jnp.transpose(part).astype(BF16)


def recv_half(received, order, own, fields, weights):
    return pl.pallas_call(
        recv_kernel,
        out_shape=(
            jax.ShapeDtypeStruct((4, PAIRS, TILE), BF16),
            jax.ShapeDtypeStruct((GROUPS, GROWS, SEQ), BF16),
            jax.ShapeDtypeStruct((QP, TILE), F32),
        ),
        in_specs=[VMEM] * 4 + [SMEM] + [VMEM] * 4,
        out_specs=(VMEM,) * 3,
        scratch_shapes=[
            pltpu.VMEM((PADQ, PAIRS), F32),
            pltpu.VMEM((512, PAIRS), F32),
            pltpu.VMEM((TILES, DUOS, QP, TILE), F32),
            pltpu.VMEM((TILES, DEEP, SEQ), BF16),
            pltpu.VMEM((GROWS, DEEP), BF16),
            pltpu.VMEM((GROUPS, GROWS, SEQ), F32),
            pltpu.VMEM((TILES, DUOS, QP, TILE), F32),
        ],
        compiler_params=PARAMS,
        cost_estimate=pl.CostEstimate(
            flops=20_000_000_000, bytes_accessed=10_000_000, transcendentals=0
        ),
        name="recv_half",
    )(received, *order, own, fields, weights)


def own_grad_kernel(
    keys_ref, bounds, place, far, resid, field_part, g0, g1, g2, g3, grad, wide, full, hot
):
    add_grad(keys_ref, bounds, resid, hot, grad, far)
    to_plain = plain_order(place)
    total = jnp.zeros((PADQ, PAIRS), F32)
    for n in range(WIDE):
        wide[n, Q * Q // 8 * 8 : PADQ, :] = jnp.zeros((PADQ - Q * Q // 8 * 8, TILE), F32)
        for c, column in enumerate(load_grad(grad, n)):
            wide[n, pl.ds(c, Q, stride=Q), :] = column[0:Q]
        total = total + dot(wide[n].astype(BF16), to_plain[n * TILE : (n + 1) * TILE, :])
    full[...] = total
    outs = (g0, g1, g2, g3)
    store_quarters(full, outs)
    exact = field_part[...]
    coarse = exact.astype(BF16).astype(F32)
    rest = exact - coarse
    tail = jnp.concatenate(
        [coarse[0:16], jnp.concatenate([coarse[16:24], rest[0:8]], axis=0), rest[8:24],
         jnp.zeros((16, TILE), F32)], axis=1,
    ).astype(BF16)
    for out in outs:
        out[QUARTER:TILE, :] = tail


def own_grad(keys, bounds, place, far, resid, field_part):
    return pl.pallas_call(
        own_grad_kernel,
        out_shape=(jax.ShapeDtypeStruct((TILE, PAIRS), BF16),) * 4,
        in_specs=[VMEM, SMEM] + [VMEM] * 4,
        out_specs=(VMEM,) * 4,
        scratch_shapes=[
            pltpu.VMEM((TILES, DUOS, QP, TILE), F32),
            pltpu.VMEM((WIDE, PADQ, TILE), F32),
            pltpu.VMEM((PADQ, PAIRS), F32),
            pltpu.VMEM((TILES, DEEP, SEQ), BF16),
        ],
        compiler_params=PARAMS,
        cost_estimate=pl.CostEstimate(
            flops=6_000_000_000, bytes_accessed=8_000_000, transcendentals=0
        ),
        name="own_grad",
    )(keys, bounds, place, far, resid, field_part)


def join_kernel(scale, mine, r1, r2, r3, remote, out, field_out):
    total = mine[...].astype(F32) + r1[...].astype(F32)
    total = total + (r2[...].astype(F32) + r3[...].astype(F32))
    summed = remote[0].astype(F32) + remote[1].astype(F32)
    summed = summed + (remote[2].astype(F32) + remote[3].astype(F32))
    flipped = jnp.transpose(summed)
    out[...] = ((total[0:QUARTER] + flipped[0:QUARTER]) * scale).astype(SENT)
    tail = total[QUARTER:TILE]
    first = tail[:, 0:TILE]
    middle = tail[:, TILE : 2 * TILE]
    last = tail[:, 2 * TILE : 3 * TILE]
    coarse = jnp.concatenate([first, middle[0:8]], axis=0)
    rest = jnp.concatenate([middle[8:16], last], axis=0)
    field_out[...] = ((coarse + rest) * scale)[0:Q, 0:RL]


def join_parts(scale, chunks, remote):
    return pl.pallas_call(
        functools.partial(join_kernel, scale),
        out_shape=(
            jax.ShapeDtypeStruct((QUARTER, PAIRS), SENT),
            jax.ShapeDtypeStruct((Q, RL), F32),
        ),
        in_specs=[VMEM] * 5,
        out_specs=(VMEM, VMEM),
        compiler_params=SMALL,
        name="join_parts",
    )(*chunks, remote)


def place_kernel(c0, c1, c2, c3, out, wide):
    for back, part in enumerate((c0, c1, c2, c3)):
        owner = lax.rem(lax.axis_index("seq") + (4 - back), 4)
        wide[pl.ds(pl.multiple_of(owner * QUARTER, 8), QUARTER), :] = part[...].astype(F32)
    out[...] = wide[0 : Q * Q, :]


def place_parts(chunks):
    return pl.pallas_call(
        place_kernel,
        out_shape=jax.ShapeDtypeStruct((Q * Q, PAIRS), F32),
        in_specs=[VMEM] * 4,
        out_specs=VMEM,
        scratch_shapes=[pltpu.VMEM((PADQ, PAIRS), F32)],
        compiler_params=SMALL,
        name="place_parts",
    )(*chunks)


def shifted(array, k):
    return lax.ppermute(array, "seq", [(i, (i + k) % 4) for i in range(4)])


def gather_seq(array):
    return [array] + [shifted(array, k) for k in (1, 2, 3)]


def scatter_seq(quarters):
    return [quarters[0]] + [shifted(quarters[k], k) for k in (1, 2, 3)]


def swap_blocks(array):
    blocks = array.reshape(BLOCKS, CAP, array.shape[1])
    moved = lax.all_to_all(blocks, "res", split_axis=0, concat_axis=0, tiled=True)
    return moved.reshape(array.shape)


def swap_quarters(array):
    blocks = array.reshape(4 * BLOCKS, CAP, TILE)
    moved = lax.all_to_all(blocks, ("seq", "res"), split_axis=0, concat_axis=0, tiled=True)
    return moved.reshape(4, PAIRS, TILE)


def per_device(
    alignment, seq_weights, fields, couplings, pair_left, pair_slot, slot_residue, pair_count
):
    scale = Q / (SEQ * 4)
    coup = couplings.T
    pack = pack_pairs(
        coup, pair_left[None, :], pair_slot[None, :], slot_residue[None, :], pair_count[None, :]
    )
    received = swap_blocks(pack)
    states, far, place, keys, bounds, field = own_field(alignment, pack, coup)
    received, field, states = lax.optimization_barrier((received, field, states))
    order = recv_order(received, states)
    remote_grad, resid, field_part = recv_half(received, order, field, fields.T, seq_weights[None, :])
    swapped = swap_quarters(remote_grad)
    local_quarters = own_grad(keys, bounds, place, far, resid, field_part)
    local_chunks = scatter_seq(local_quarters)
    joined, field_grad = join_parts(scale, local_chunks, swapped)
    coupling_grad = place_parts(gather_seq(joined))
    return coupling_grad.T, field_grad.T


def solution(mesh):
    in_specs = (
        P(None, "seq"),
        P("seq"),
        P("res", None),
        P("res", None),
        P("res"),
        P("res"),
        P("res"),
        P("res"),
    )
    out_specs = (P("res", None), P("res", None))
    return jax.shard_map(
        per_device, mesh=mesh, in_specs=in_specs, out_specs=out_specs, check_vma=False
    )
```

time: 107 us -> 88.7 us (0.83)
  Pallas kernels: 43.2 us -> 31.3 us
  starting transfers between devices: 39.2 us -> 29.1 us
  local copies, waits for them, and re-layouts: 1.57 us -> 4.01 us
    all_to_all x2 -> x1, starting transfers between devices: 24.5 us -> 13 us  [swap_blocks(): lax.all_to_all(blocks, 'res', split_axis=0, concat_axis=0, tiled=True)]
    all_to_all x0 -> x1, starting transfers between devices: none -> 8.98 us  [swap_quarters(): lax.all_to_all(blocks, ('seq', 'res'), split_axis=0, concat_axis=0, tiled...]
    ppermute x12 -> x6, starting transfers between devices: 14.7 us -> 7.19 us  [shifted(): return lax.ppermute(array, 'seq', [(i, (i + k) % 4) for i in range(4)])]
    ppermute x12 -> x6, waiting for transfers between devices: 21 us -> 14.9 us  [shifted(): return lax.ppermute(array, 'seq', [(i, (i + k) % 4) for i in range(4)])]
    all_to_all x2 -> x1, waiting for transfers between devices: 1.17 us -> 6.02 us  [swap_blocks(): lax.all_to_all(blocks, 'res', split_axis=0, concat_axis=0, tiled=True)]
    pallas_call x3 -> x2, Pallas kernels: 17.7 us -> 13.4 us  [the longest x1 11.1 us: recv_half(): pl.pallas_call(recv_kernel, out_shape=(jax.ShapeDtypeStruct((4, PAIRS, TI...]
    pallas_call x1, Pallas kernels: 11.2 us -> 7.27 us  [own_field(): pl.pallas_call(own_field_kernel, out_shape=(jax.ShapeDtypeStruct((RES, SE...]
    unnamed x12 -> x14, local copies, waits for them, and re-layouts: 1.57 us -> 4.01 us
  transfers between devices with their start and end apart: 14 -> 8, of which waited for: 9 -> 7; matrix products, arithmetic and copies ran while one was open for 0% -> 0% of each run, Pallas kernels for 22% -> 16%
where the time goes in v3:
time: 88.7 us; the launch traced here: 88 us
  Pallas kernels  31.3 us (35%)
  starting transfers between devices  29.1 us (33%)
  waiting for transfers between devices  22.8 us (26%)
  local copies, waits for them, and re-layouts  4.01 us (5%)
    ppermute x6, waiting for transfers between devices, shifted(): return lax.ppermute(array, 'seq', [(i, (i + k) % 4) for i in range(4)])  14.9 us
    all_to_all x1, starting transfers between devices, swap_blocks(): lax.all_to_all(blocks, 'res', split_axis=0, concat_axis=0, tiled=True)  13 us
    pallas_call x1, Pallas kernels, recv_half(): pl.pallas_call(recv_kernel, out_shape=(jax.ShapeDtypeStruct((4, PAIRS, TI...  11.1 us
    all_to_all x1, starting transfers between devices, swap_quarters(): lax.all_to_all(blocks, ('seq', 'res'), split_axis=0, concat_axis=0, tiled...  8.98 us
    pallas_call x1, Pallas kernels, own_field(): pl.pallas_call(own_field_kernel, out_shape=(jax.ShapeDtypeStruct((RES, SE...  7.27 us
    ppermute x6, starting transfers between devices, shifted(): return lax.ppermute(array, 'seq', [(i, (i + k) % 4) for i in range(4)])  7.19 us
    pallas_call x1, Pallas kernels, own_grad(): pl.pallas_call(own_grad_kernel, out_shape=(jax.ShapeDtypeStruct((TILE, PA...  6.63 us
    all_to_all x1, waiting for transfers between devices, swap_blocks(): lax.all_to_all(blocks, 'res', split_axis=0, concat_axis=0, tiled=True)  6.02 us
  transfers between devices with their start and end apart: 8, of which 7 were waited for; matrix products, arithmetic and copies ran while one was open for 0% of the time, Pallas kernels for 16%

profile of v3, /device:TPU:1, one launch (start us, length us, event | category | flops | bytes accessed | tf_op | source)
XLA Modules:
  0.0 88.0 jit_solution(12546561390876770942)
XLA Ops:
  0.6 0.0 copy-start.1
  0.6 2.3 %pack_pairs.1.pack = bf16[512,512]{1,0:T(8,128)(2,1)} custom-call(bf16[441,512]{1,0:T(8,128)(2,1)} %bitcast.17, s32[1,512]{1,0:T(1,128)} %bitcast.22, s32[1,512]{1,0:T(1,128)} %bitcast.23, s32[1,256]{1,0:T(1,128)} %bitcast.24, s32[1,64]{1,0:T(1,128)} %bitcast.25), custom_call_target="tpu_custom_call" | custom-call | tf_op jit(solution)/shard_map/pack_pairs/pallas_call | solution.py:72
  2.9 13.0 %all-to-all-start = ((bf16[64,8,512]{2,1,0:T(8,128)(2,1)}), bf16[64,8,512]{2,1,0:T(8,128)(2,1)S(1)}, u32[]{:S(2)}, u32[]{:S(2)}) async-start(bf16[64,8,512]{2,1,0:T(8,128)(2,1)} %bitcast.14), calls=%async_computation | async-start | bytes 1048576 | tf_op jit(solution)/shard_map/all_to_all | solution.py:506
  15.9 0.0 copy-done.1
  15.9 0.0 copy-start
  15.9 1.1 %copy-done = bf16[512,512]{1,0:T(8,128)(2,1)S(1)} copy-done((bf16[512,512]{1,0:T(8,128)(2,1)S(1)}, bf16[512,512]{1,0:T(8,128)(2,1)}, u32[]{:S(2)}) %copy-start) | copy-done | bytes 524312
  17.0 0.0 copy-start.2
  17.0 1.9 %copy-done.2 = s32[3072,256]{1,0:T(8,128)S(1)} copy-done((s32[3072,256]{1,0:T(8,128)S(1)}, s32[3072,256]{1,0:T(8,128)}, u32[]{:S(2)}) %copy-start.2) | copy-done | bytes 3145752
  18.9 7.3 %own_field.1 = (bf16[3072,256]{1,0:T(8,128)(2,1)S(1)}, bf16[512,256]{1,0:T(8,128)(2,1)S(1)}, f32[8,512]{1,0:T(8,128)S(1)}, f32[8,8,128]{2,1,0:T(8,128)S(1)}, s32...) custom-call(s32[3072,256]{1,0:T(8,128)S(1)} %copy-done.2, bf16[512,512]{1,0:T(8,128)(2,1)S(1)} %copy-done, ...), custom_call_target="tpu_custom_call" | custom-call | flops 10000000000 | bytes 10000000 | tf_op jit(solution)/shard_map/own_field/pallas_call | solution.py:262
  26.1 0.0 copy-start.5
  26.2 1.0 %copy-done.5 = f32[6,192,256]{2,1,0:T(8,128)} copy-done((f32[6,192,256]{2,1,0:T(8,128)}, f32[6,192,256]{2,1,0:T(8,128)S(1)}, u32[]{:S(2)}) %copy-start.5) | copy-done | bytes 1179672
  27.2 6.0 %all-to-all-done = bf16[64,8,512]{2,1,0:T(8,128)(2,1)S(1)} async-done(((bf16[64,8,512]{2,1,0:T(8,128)(2,1)}), bf16[64,8,512]{2,1,0:T(8,128)(2,1)S(1)}, u32[]{:S(2)}, u32[]{:S(2)}) %all-to-all-start) | async-done | bytes 524320 | tf_op jit(solution)/shard_map/all_to_all | solution.py:506
  33.2 0.0 copy-start.3
  33.2 0.0 copy-start.4
  33.2 0.0 copy-start.6
  33.2 2.3 %recv_order.1 = (bf16[512,256]{1,0:T(8,128)(2,1)S(1)}, f32[8,512]{1,0:T(8,128)S(1)}, f32[8,8,128]{2,1,0:T(8,128)S(1)}, s32[2,8]{1,0:T(2,128)S(1)}, bf16[48,256]{1,0:T(8,128)(2,1)S(1)}) custom-call(bf16[512,512]{1,0:T(8,128)(2,1)S(1)} %bitcast.15, bf16[3072,256]{1,0:T(8,128)(2,1)S(1)} %get-tuple-element.32.states), custom_call_target="tpu_custom_call" | custom-call | flops 5000000000 | bytes 3000000 | tf_op jit(solution)/shard_map/recv_order/pallas_call | solution.py:299
  35.5 0.0 copy-done.3
  35.5 0.0 copy-done.4
  35.5 0.0 copy-done.6
  35.5 11.1 %recv_half.1 = (bf16[4,512,128]{2,1,0:T(8,128)(2,1)}, bf16[6,192,256]{2,1,0:T(8,128)(2,1)S(1)}, f32[24,128]{1,0:T(8,128)S(1)}) custom-call(bf16[512,512]{1,0:T(8,128)(2,1)S(1)} %bitcast.16, bf16[512,256]{1,0:T(8,128)(2,1)S(1)} %get-tuple-element.33.far, f32[8,512]{1,0:T(8,128)S(1)} %get-tuple-element.34.place, f32[8,8,128]{2,1,0:T(8,128)S(1)} %get-tuple-element.35.keys_ref, ...), custom_call_target="tpu_custom_call" | custom-call | flops 20000000000 | bytes 10000000 | tf_op jit(solution)/shard_map/recv_half/pallas_call | solution.py:372
  46.6 9.0 %all-to-all-start.1 = ((bf16[256,8,128]{2,1,0:T(8,128)(2,1)}), bf16[256,8,128]{2,1,0:T(8,128)(2,1)S(1)}, u32[]{:S(2)}, u32[]{:S(2)}) async-start(bf16[256,8,128]{2,1,0:T(8,128)(2,1)} %bitcast.9), calls=%async_computation.1 | async-start | bytes 1048576 | tf_op jit(solution)/shard_map/all_to_all | solution.py:512
  55.6 6.6 %own_grad.1 = (bf16[128,512]{1,0:T(8,128)(2,1)S(1)}, bf16[128,512]{1,0:T(8,128)(2,1)S(1)}, bf16[128,512]{1,0:T(8,128)(2,1)S(1)}, bf16[128,512]{1,0:T(8,128)(2,1)S(1)}) custom-call(f32[8,8,128]{2,1,0:T(8,128)S(1)} %get-tuple-element.25.keys_ref, s32[2,8]{1,0:T(2,128)S(1)} %get-tuple-element.26.bounds, f32[8,512]{1,0:T(8,128)S(1)} %get-tuple-element.27.place, ...), custom_call_target="tpu_custom_call" | custom-call | flops 6000000000 | bytes 8000000 | tf_op jit(solution)/shard_map/own_grad/pallas_call | solution.py:424
  62.3 1.5 %collective-permute-start = (bf16[128,512]{1,0:T(8,128)(2,1)S(1)}, bf16[128,512]{1,0:T(8,128)(2,1)S(1)}, u32[]{:S(2)}, u32[]{:S(2)}) collective-permute-start(bf16[128,512]{1,0:T(8,128)(2,1)S(1)} %get-tuple-element.42), channel_id=1, source_target_pairs={{0,64},{64,128},{128,192},{192,0},{1,65},{65,129},{129,193},{193,1... | collective-permute-start | bytes 393224 | tf_op jit(solution)/shard_map/ppermute | solution.py:493
  63.7 2.4 %collective-permute-start.1 = (bf16[128,512]{1,0:T(8,128)(2,1)S(1)}, bf16[128,512]{1,0:T(8,128)(2,1)S(1)}, u32[]{:S(2)}, u32[]{:S(2)}) collective-permute-start(bf16[128,512]{1,0:T(8,128)(2,1)S(1)} %get-tuple-element.43), channel_id=1, source_target_pairs={{0,128},{64,192},{128,0},{192,64},{1,129},{65,193},{129,1},{193,65... | collective-permute-start | bytes 393224 | tf_op jit(solution)/shard_map/ppermute | solution.py:493
  66.2 1.1 %collective-permute-start.2 = (bf16[128,512]{1,0:T(8,128)(2,1)S(1)}, bf16[128,512]{1,0:T(8,128)(2,1)S(1)}, u32[]{:S(2)}, u32[]{:S(2)}) collective-permute-start(bf16[128,512]{1,0:T(8,128)(2,1)S(1)} %get-tuple-element.44), channel_id=1, source_target_pairs={{0,192},{64,0},{128,64},{192,128},{1,193},{65,1},{129,65},{193,129... | collective-permute-start | bytes 393224 | tf_op jit(solution)/shard_map/ppermute | solution.py:493
  67.3 1.5 %collective-permute-done.r1 = bf16[128,512]{1,0:T(8,128)(2,1)S(1)} collective-permute-done((bf16[128,512]{1,0:T(8,128)(2,1)S(1)}, bf16[128,512]{1,0:T(8,128)(2,1)S(1)}, u32[]{:S(2)}, u32[]{:S(2)}) %collective-permute-start) | collective-permute-done | bytes 131104 | tf_op jit(solution)/shard_map/ppermute | solution.py:493
  68.8 6.4 %collective-permute-done.1.r2 = bf16[128,512]{1,0:T(8,128)(2,1)S(1)} collective-permute-done((bf16[128,512]{1,0:T(8,128)(2,1)S(1)}, bf16[128,512]{1,0:T(8,128)(2,1)S(1)}, u32[]{:S(2)}, u32[]{:S(2)}) %collective-permute-start.1) | collective-permute-done | bytes 131104 | tf_op jit(solution)/shard_map/ppermute | solution.py:493
  75.1 0.0 collective-permute-done.2.r3
  75.1 1.9 %all-to-all-done.1 = bf16[256,8,128]{2,1,0:T(8,128)(2,1)S(1)} async-done(((bf16[256,8,128]{2,1,0:T(8,128)(2,1)}), bf16[256,8,128]{2,1,0:T(8,128)(2,1)S(1)}, u32[]{:S(2)}, u32[]{:S(2)}) %all-to-all-start.1) | async-done | bytes 524320 | tf_op jit(solution)/shard_map/all_to_all | solution.py:512
  77.0 0.7 join_parts.1
  77.8 0.7 collective-permute-start.5
  78.5 1.4 %collective-permute-start.4 = (bf16[112,512]{1,0:T(8,128)(2,1)S(1)}, bf16[112,512]{1,0:T(8,128)(2,1)S(1)}, u32[]{:S(2)}, u32[]{:S(2)}) collective-permute-start(bf16[112,512]{1,0:T(8,128)(2,1)S(1)} %get-tuple-element.46.c0), channel_id=1, source_target_pairs={{0,128},{64,192},{128,0},{192,64},{1,129},{65,193},{129,1},{193,65... | collective-permute-start | bytes 344072 | tf_op jit(solution)/shard_map/ppermute | solution.py:493
  79.9 0.0 collective-permute-start.3
  79.9 2.2 %collective-permute-done.5.c3 = bf16[112,512]{1,0:T(8,128)(2,1)S(1)} collective-permute-done((bf16[112,512]{1,0:T(8,128)(2,1)S(1)}, bf16[112,512]{1,0:T(8,128)(2,1)S(1)}, u32[]{:S(2)}, u32[]{:S(2)}) %collective-permute-start.5) | collective-permute-done | bytes 114720 | tf_op jit(solution)/shard_map/ppermute | solution.py:493
  82.1 1.9 %collective-permute-done.4.c2 = bf16[112,512]{1,0:T(8,128)(2,1)S(1)} collective-permute-done((bf16[112,512]{1,0:T(8,128)(2,1)S(1)}, bf16[112,512]{1,0:T(8,128)(2,1)S(1)}, u32[]{:S(2)}, u32[]{:S(2)}) %collective-permute-start.4) | collective-permute-done | bytes 114720 | tf_op jit(solution)/shard_map/ppermute | solution.py:493
  84.0 3.0 %collective-permute-done.3.c1 = bf16[112,512]{1,0:T(8,128)(2,1)S(1)} collective-permute-done((bf16[112,512]{1,0:T(8,128)(2,1)S(1)}, bf16[112,512]{1,0:T(8,128)(2,1)S(1)}, u32[]{:S(2)}, u32[]{:S(2)}) %collective-permute-start.3) | collective-permute-done | bytes 114720 | tf_op jit(solution)/shard_map/ppermute | solution.py:493
  87.0 1.1 %place_parts.1 = f32[441,512]{1,0:T(8,128)} custom-call(bf16[112,512]{1,0:T(8,128)(2,1)S(1)} %get-tuple-element.46.c0, bf16[112,512]{1,0:T(8,128)(2,1)S(1)} %collective-permute-done.3.c1, bf16[112,512]{1,0:T(8,128)(2,1)S(1)} %collective-permute-done.4.c2, bf16[112,512]{1,0:T(8,128)(2,1)S(1)} %collective-permute-done.5.c3), custom_call_target="tpu_custom_call" | custom-call | tf_op jit(solution)/shard_map/place_parts/pallas_call | solution.py:481
Async XLA Ops:
  0.6 15.3 %copy-start.1 = (bf16[512,441]{0,1:T(8,128)(2,1)S(1)}, bf16[512,441]{0,1:T(8,128)(2,1)}, u32[]{:S(2)}) copy-start(bf16[512,441]{0,1:T(8,128)(2,1)} %param.11) | copy-start | bytes 1354756
  2.9 30.3 %all-to-all-start = ((bf16[64,8,512]{2,1,0:T(8,128)(2,1)}), bf16[64,8,512]{2,1,0:T(8,128)(2,1)S(1)}, u32[]{:S(2)}, u32[]{:S(2)}) async-start(bf16[64,8,512]{2,1,0:T(8,128)(2,1)} %bitcast.14), calls=%async_computation | async-start | bytes 1048576 | tf_op jit(solution)/shard_map/all_to_all | solution.py:506
  15.9 1.1 %copy-start = (bf16[512,512]{1,0:T(8,128)(2,1)S(1)}, bf16[512,512]{1,0:T(8,128)(2,1)}, u32[]{:S(2)}) copy-start(bf16[512,512]{1,0:T(8,128)(2,1)} %pack_pairs.1.pack) | copy-start | bytes 1572868
  17.0 1.9 %copy-start.2 = (s32[3072,256]{1,0:T(8,128)S(1)}, s32[3072,256]{1,0:T(8,128)}, u32[]{:S(2)}) copy-start(s32[3072,256]{1,0:T(8,128)} %alignment.1) | copy-start | bytes 9437188
  26.1 1.0 %copy-start.5 = (f32[6,192,256]{2,1,0:T(8,128)}, f32[6,192,256]{2,1,0:T(8,128)S(1)}, u32[]{:S(2)}) copy-start(f32[6,192,256]{2,1,0:T(8,128)S(1)} %get-tuple-element.38.own) | copy-start | bytes 3538948
  33.2 2.3 %copy-start.3 = (f32[48,21]{0,1:T(8,128)S(1)}, f32[48,21]{0,1:T(8,128)}, u32[]{:S(2)}) copy-start(f32[48,21]{0,1:T(8,128)} %param.10) | copy-start | bytes 12100
  33.2 2.3 %copy-start.4 = (f32[256]{0:T(256)S(1)}, f32[256]{0:T(256)}, u32[]{:S(2)}) copy-start(f32[256]{0:T(256)} %param.9) | copy-start | bytes 3076
  33.2 2.3 %copy-start.6 = (f32[6,192,256]{2,1,0:T(8,128)S(1)}, f32[6,192,256]{2,1,0:T(8,128)}, u32[]{:S(2)}) copy-start(f32[6,192,256]{2,1,0:T(8,128)} %copy-done.5) | copy-start | bytes 3538948
  46.6 30.4 %all-to-all-start.1 = ((bf16[256,8,128]{2,1,0:T(8,128)(2,1)}), bf16[256,8,128]{2,1,0:T(8,128)(2,1)S(1)}, u32[]{:S(2)}, u32[]{:S(2)}) async-start(bf16[256,8,128]{2,1,0:T(8,128)(2,1)} %bitcast.9), calls=%async_computation.1 | async-start | bytes 1048576 | tf_op jit(solution)/shard_map/all_to_all | solution.py:512
  62.3 6.5 %collective-permute-start = (bf16[128,512]{1,0:T(8,128)(2,1)S(1)}, bf16[128,512]{1,0:T(8,128)(2,1)S(1)}, u32[]{:S(2)}, u32[]{:S(2)}) collective-permute-start(bf16[128,512]{1,0:T(8,128)(2,1)S(1)} %get-tuple-element.42), channel_id=1, source_target_pairs={{0,64},{64,128},{128,192},{192,0},{1,65},{65,129},{129,193},{193,1... | collective-permute-start | bytes 393224 | tf_op jit(solution)/shard_map/ppermute | solution.py:493
  63.7 11.4 %collective-permute-start.1 = (bf16[128,512]{1,0:T(8,128)(2,1)S(1)}, bf16[128,512]{1,0:T(8,128)(2,1)S(1)}, u32[]{:S(2)}, u32[]{:S(2)}) collective-permute-start(bf16[128,512]{1,0:T(8,128)(2,1)S(1)} %get-tuple-element.43), channel_id=1, source_target_pairs={{0,128},{64,192},{128,0},{192,64},{1,129},{65,193},{129,1},{193,65... | collective-permute-start | bytes 393224 | tf_op jit(solution)/shard_map/ppermute | solution.py:493
  66.2 8.9 %collective-permute-start.2 = (bf16[128,512]{1,0:T(8,128)(2,1)S(1)}, bf16[128,512]{1,0:T(8,128)(2,1)S(1)}, u32[]{:S(2)}, u32[]{:S(2)}) collective-permute-start(bf16[128,512]{1,0:T(8,128)(2,1)S(1)} %get-tuple-element.44), channel_id=1, source_target_pairs={{0,192},{64,0},{128,64},{192,128},{1,193},{65,1},{129,65},{193,129... | collective-permute-start | bytes 393224 | tf_op jit(solution)/shard_map/ppermute | solution.py:493
  77.8 4.3 %collective-permute-start.5 = (bf16[112,512]{1,0:T(8,128)(2,1)S(1)}, bf16[112,512]{1,0:T(8,128)(2,1)S(1)}, u32[]{:S(2)}, u32[]{:S(2)}) collective-permute-start(bf16[112,512]{1,0:T(8,128)(2,1)S(1)} %get-tuple-element.46.c0), channel_id=1, source_target_pairs={{0,192},{64,0},{128,64},{192,128},{1,193},{65,1},{129,65},{193,129... | collective-permute-start | bytes 344072 | tf_op jit(solution)/shard_map/ppermute | solution.py:493
  78.5 5.5 %collective-permute-start.4 = (bf16[112,512]{1,0:T(8,128)(2,1)S(1)}, bf16[112,512]{1,0:T(8,128)(2,1)S(1)}, u32[]{:S(2)}, u32[]{:S(2)}) collective-permute-start(bf16[112,512]{1,0:T(8,128)(2,1)S(1)} %get-tuple-element.46.c0), channel_id=1, source_target_pairs={{0,128},{64,192},{128,0},{192,64},{1,129},{65,193},{129,1},{193,65... | collective-permute-start | bytes 344072 | tf_op jit(solution)/shard_map/ppermute | solution.py:493
  79.9 7.1 %collective-permute-start.3 = (bf16[112,512]{1,0:T(8,128)(2,1)S(1)}, bf16[112,512]{1,0:T(8,128)(2,1)S(1)}, u32[]{:S(2)}, u32[]{:S(2)}) collective-permute-start(bf16[112,512]{1,0:T(8,128)(2,1)S(1)} %get-tuple-element.46.c0), channel_id=1, source_target_pairs={{0,64},{64,128},{128,192},{192,0},{1,65},{65,129},{129,193},{193,1... | collective-permute-start | bytes 344072 | tf_op jit(solution)/shard_map/ppermute | solution.py:493

commit v4 on v3

--- a/solution.py
+++ b/solution.py
@@ -21,9 +21,9 @@
 SPAN = 64
 TILES = PAIRS // SPAN
 DUOS = (Q + 1) // 2
-GROUP = 8
-GROUPS = RL // GROUP
-GROWS = GROUP * QP
+ROWS = RL * QP
+WINDOW = 16
+WROWS = WINDOW * QP
 QUARTER = 112
 PADQ = 4 * QUARTER
 DEEP = DUOS * TILE
@@ -31,8 +31,7 @@
 BF16 = jnp.bfloat16
 VMEM = pl.BlockSpec(memory_space=pltpu.VMEM)
 SMEM = pl.BlockSpec(memory_space=pltpu.SMEM)
-ANY = pl.BlockSpec(memory_space=pl.ANY)
-PARAMS = pltpu.CompilerParams(vmem_limit_bytes=24 * 1024 * 1024)
+PARAMS = pltpu.CompilerParams(vmem_limit_bytes=20 * 1024 * 1024)
 LARGE = pltpu.CompilerParams(vmem_limit_bytes=56 * 1024 * 1024)
 SMALL = pltpu.CompilerParams(vmem_limit_bytes=16 * 1024 * 1024)
 SENT = BF16
@@ -93,29 +92,26 @@
     place_col = jnp.sum(jnp.where(full_row < full_col, 1.0, 0.0), axis=1, keepdims=True)
     to_sorted = jnp.where(place_col == lane, 1.0, 0.0).astype(BF16)
     to_plain = jnp.where(place_row == sub, 1.0, 0.0).astype(BF16)
-    cols = dot(to_plain, pack)
-    far = cols[:, block : block + 1] * RL + cols[:, other : other + 1]
+    far = wide[:, block : block + 1] * RL + wide[:, other : other + 1]
     keys = dot(jnp.broadcast_to(key_row, (8, PAIRS)).astype(BF16), to_sorted)
-    return to_sorted, place_row, far, keys
+    return to_sorted, to_plain, place_row, far, keys
 
 
 def plain_order(place):
     return jnp.where(place[0:1] == iota((PAIRS, PAIRS), 0).astype(F32), 1.0, 0.0).astype(BF16)
 
 
-def sorted_order(place):
-    col = jnp.transpose(jnp.broadcast_to(place[0:1], (TILE, PAIRS)))[:, 0:1]
-    return jnp.where(col == iota((PAIRS, PAIRS), 1).astype(F32), 1.0, 0.0).astype(BF16)
-
-
-def find_far(far, states):
-    far_states = jnp.zeros((PAIRS, SEQ), F32)
-    chunk = 256
-    lane = iota((PAIRS, chunk), 1).astype(F32)
-    for n in range(RES // chunk):
-        pick = jnp.where(far - float(n * chunk) == lane, 1.0, 0.0).astype(BF16)
-        far_states = far_states + dot(pick, states[n * chunk : (n + 1) * chunk, :])
-    return far_states
+def find_far(far, states, to_plain, plain):
+    count = 5
+    for start in range(0, BLOCKS, count):
+        blocks = min(count, BLOCKS - start)
+        pairs = slice(start * CAP, (start + blocks) * CAP)
+        base = start * RL
+        depth = min(256, RES - base)
+        lane = iota((blocks * CAP, depth), 1).astype(F32)
+        pick = jnp.where(far[pairs] - float(base) == lane, 1.0, 0.0).astype(BF16)
+        plain[pairs, :] = dot(pick, states[base : base + depth, :])
+    return dot(to_plain, plain[...].astype(BF16))
 
 
 def fill_hot(far, j, hot):
@@ -138,7 +134,7 @@
         for i, span in enumerate(halves(part, part)):
             j = 2 * n + i
             keys_ref[j] = span
-            bounds[0, j], bounds[1, j] = group_range(span)
+            bounds[0, j], bounds[1, j] = window_range(span)
 
 
 def store_blocks(block, n, blocks):
@@ -154,37 +150,41 @@
     return columns[:Q]
 
 
-def group_range(keys):
+def window_range(keys):
     low = jnp.min(keys).astype(jnp.int32)
     high = jnp.max(jnp.where(keys < RL - 0.5, keys, -1.0)).astype(jnp.int32)
-    return low // GROUP, (high + GROUP) // GROUP
-
-
-def group_masks(keys, g):
-    base = (g * GROUP).astype(F32)
-    wide = jnp.broadcast_to(keys[0:1], (QP, TILE))
-    return [wide == base + float(m) for m in range(GROUP)]
+    first = low - (low & 1)
+    return first, jnp.where(high >= 0, (high - first) // WINDOW + 1, 0)
+
+
+def window_at(keys, first, step):
+    start = first + step * WINDOW
+    base = jnp.minimum(start, RL - WINDOW)
+    fresh = jnp.where(keys[0:1] >= start.astype(F32), keys[0:1], -1.0)
+    wide = jnp.broadcast_to(fresh, (QP, TILE))
+    rows = pl.ds(pl.multiple_of(base * QP, 2 * QP), WROWS)
+    return rows, [wide == (base + m).astype(F32) for m in range(WINDOW)]
 
 
 def add_field(keys_ref, bounds, blocks, far, hot, lhs, field):
     def tile_step(j, carry):
         keys = keys_ref[j]
-        low, high = bounds[0, j], bounds[1, j]
-
-        @pl.when(low < high)
+        first, count = bounds[0, j], bounds[1, j]
+
+        @pl.when(count > 0)
         def _():
             fill_hot(far, j, hot)
 
-        def group_step(g, carry):
-            masks = group_masks(keys, g)
+        def window_step(step, carry):
+            window, masks = window_at(keys, first, step)
             for d in range(DUOS):
                 block = blocks[j, d]
                 rows = [jnp.where(mask, block, 0.0) for mask in masks]
                 lhs[:, d * TILE : (d + 1) * TILE] = jnp.concatenate(rows, axis=0).astype(BF16)
-            field[g] += dot(lhs[...], hot[j])
+            field[window, :] += dot(lhs[...], hot[j])
             return carry
 
-        return lax.fori_loop(low, high, group_step, carry)
+        return lax.fori_loop(0, count, window_step, carry)
 
     lax.fori_loop(0, TILES, tile_step, 0)
 
@@ -194,31 +194,31 @@
 
     def tile_step(j, carry):
         keys = keys_ref[j]
-        low, high = bounds[0, j], bounds[1, j]
+        first, count = bounds[0, j], bounds[1, j]
         if far is not None:
 
-            @pl.when(low < high)
+            @pl.when(count > 0)
             def _():
                 fill_hot(far, j, hot)
 
-        def group_step(g, carry):
-            masks = group_masks(keys, g)
-            rows = resid[g]
+        def window_step(step, carry):
+            window, masks = window_at(keys, first, step)
+            rows = resid[window, :]
             for d in range(0, DUOS, 2):
-                count = min(2, DUOS - d)
-                part = hot[j, d * TILE : (d + count) * TILE, :]
+                duos = min(2, DUOS - d)
+                part = hot[j, d * TILE : (d + duos) * TILE, :]
                 out = lax.dot_general(
                     rows, part, (((1,), (1,)), ((), ())), preferred_element_type=F32
                 )
-                for i in range(count):
+                for i in range(duos):
                     total = grad[j, d + i]
-                    for m in range(GROUP):
+                    for m in range(WINDOW):
                         piece = out[m * QP : (m + 1) * QP, i * TILE : (i + 1) * TILE]
                         total = jnp.where(masks[m], piece, total)
                     grad[j, d + i] = total
             return carry
 
-        return lax.fori_loop(low, high, group_step, carry)
+        return lax.fori_loop(0, count, window_step, carry)
 
     lax.fori_loop(0, TILES, tile_step, 0)
 
@@ -232,13 +232,13 @@
 
 def own_field_kernel(
     alignment, pack, coup, states, far_out, place_out, keys_ref, bounds, field,
-    sorted_blocks, blocks, hot, lhs,
+    sorted_blocks, blocks, hot, lhs, codes, plain,
 ):
     chunk = 512
     parts = [slice(n * chunk, (n + 1) * chunk) for n in range(RES // chunk)]
     packed = pack[:, 0:TILE]
     flipped = jnp.transpose(packed.astype(F32))
-    to_sorted, place, far, keys = order_half(packed, flipped, True)
+    to_sorted, to_plain, place, far, keys = order_half(packed, flipped, True)
     place_out[...] = jnp.broadcast_to(place, (8, PAIRS))
     store_keys(keys, keys_ref, bounds)
     sorted_blocks[...] = jnp.zeros_like(sorted_blocks)
@@ -247,15 +247,12 @@
         sorted_blocks[n, 0 : Q * Q, :] = ordered[:, n * TILE : (n + 1) * TILE]
         store_blocks(lambda c: sorted_blocks[n, pl.ds(c, QP, stride=Q), :], n, blocks)
     field[...] = jnp.zeros_like(field)
-    far_states = jnp.zeros((PAIRS, SEQ), F32)
-    lane = iota((PAIRS, chunk), 1).astype(F32)
-    for n, rows in enumerate(parts):
-        part = alignment[rows, :].astype(F32).astype(BF16)
-        states[rows, :] = part
-        pick = jnp.where(far - float(n * chunk) == lane, 1.0, 0.0).astype(BF16)
-        far_states = far_states + dot(pick, part)
-    far_out[...] = far_states.astype(BF16)
-    add_field(keys_ref, bounds, blocks, far_out, hot, lhs, field)
+    for rows in parts:
+        states[rows, :] = alignment[rows, :].astype(F32).astype(BF16)
+    far_states = find_far(far, states, to_plain, plain)
+    far_out[...] = far_states.astype(jnp.int8)
+    codes[...] = far_states.astype(BF16)
+    add_field(keys_ref, bounds, blocks, codes, hot, lhs, field)
 
 
 def own_field(alignment, pack, coup):
@@ -263,11 +260,11 @@
         own_field_kernel,
         out_shape=(
             jax.ShapeDtypeStruct((RES, SEQ), BF16),
-            jax.ShapeDtypeStruct((PAIRS, SEQ), BF16),
+            jax.ShapeDtypeStruct((PAIRS, SEQ), jnp.int8),
             jax.ShapeDtypeStruct((8, PAIRS), F32),
             jax.ShapeDtypeStruct((TILES, 8, TILE), F32),
             jax.ShapeDtypeStruct((2, TILES), jnp.int32),
-            jax.ShapeDtypeStruct((GROUPS, GROWS, SEQ), F32),
+            jax.ShapeDtypeStruct((ROWS, SEQ), F32),
         ),
         in_specs=[VMEM, VMEM, VMEM],
         out_specs=(VMEM, VMEM, VMEM, VMEM, SMEM, VMEM),
@@ -275,7 +272,9 @@
             pltpu.VMEM((WIDE, 512, TILE), F32),
             pltpu.VMEM((TILES, DUOS, QP, TILE), F32),
             pltpu.VMEM((TILES, DEEP, SEQ), BF16),
-            pltpu.VMEM((GROWS, DEEP), BF16),
+            pltpu.VMEM((WROWS, DEEP), BF16),
+            pltpu.VMEM((PAIRS, SEQ), BF16),
+            pltpu.VMEM((PAIRS, SEQ), F32),
         ],
         compiler_params=PARAMS,
         cost_estimate=pl.CostEstimate(
@@ -285,114 +284,102 @@
     )(alignment, pack, coup)
 
 
-def recv_order_kernel(pack, states, far_out, place_out, keys_ref, bounds, codes):
-    packed = pack[:, 0:TILE]
+def recv_kernel(
+    parts, states, own, fields, weights,
+    grad_out, resid_out, field_out,
+    wide, sorted_blocks, blocks, hot, lhs, field, grad, far, plain, keys_ref, bounds,
+):
+    packed = parts[:, 0:TILE]
     flipped = jnp.transpose(packed.astype(F32))
-    to_sorted, place, far, keys = order_half(packed, flipped, False)
+    to_sorted, to_plain, place, far_col, keys = order_half(packed, flipped, False)
     store_keys(keys, keys_ref, bounds)
-    place_out[...] = jnp.broadcast_to(place, (8, PAIRS))
-    far_out[...] = find_far(far, states).astype(BF16)
-    codes[...] = states[pl.ds(pl.multiple_of(lax.axis_index("res") * RL, 16), RL), :]
-
-
-def recv_order(pack, states):
-    return pl.pallas_call(
-        recv_order_kernel,
-        out_shape=(
-            jax.ShapeDtypeStruct((PAIRS, SEQ), BF16),
-            jax.ShapeDtypeStruct((8, PAIRS), F32),
-            jax.ShapeDtypeStruct((TILES, 8, TILE), F32),
-            jax.ShapeDtypeStruct((2, TILES), jnp.int32),
-            jax.ShapeDtypeStruct((RL, SEQ), BF16),
-        ),
-        in_specs=[VMEM] * 2,
-        out_specs=(VMEM, VMEM, VMEM, SMEM, VMEM),
-        compiler_params=PARAMS,
-        cost_estimate=pl.CostEstimate(
-            flops=5_000_000_000, bytes_accessed=3_000_000, transcendentals=0
-        ),
-        name="recv_order",
-    )(pack, states)
-
-
-def recv_kernel(
-    parts, far, place, keys_ref, bounds, codes, own, fields, weights,
-    grad_out, resid_out, field_out,
-    wide, sorted_blocks, blocks, hot, lhs, field, grad,
-):
+    far[...] = find_far(far_col, states, to_plain, plain).astype(BF16)
     for n in range(4):
-        flipped = jnp.transpose(parts[:, n * TILE : (n + 1) * TILE].astype(F32))
+        if n > 0:
+            flipped = jnp.transpose(parts[:, n * TILE : (n + 1) * TILE].astype(F32))
         wide[n * QUARTER : (n + 1) * QUARTER, :] = flipped[0:QUARTER]
     sorted_blocks[PADQ:512, :] = jnp.zeros((512 - PADQ, PAIRS), F32)
-    sorted_blocks[0:PADQ, :] = dot(wide[...].astype(BF16), sorted_order(place))
+    sorted_blocks[0:PADQ, :] = dot(wide[0:PADQ, :].astype(BF16), to_sorted)
     for n in range(WIDE):
         lanes = slice(n * TILE, (n + 1) * TILE)
         store_blocks(lambda a: sorted_blocks[a * Q : a * Q + QP, lanes], n, blocks)
     field[...] = own[...]
     add_field(keys_ref, bounds, blocks, far, hot, lhs, field)
 
-    my_codes = codes[...].astype(F32)
+    mine = pl.ds(pl.multiple_of(lax.axis_index("res") * RL, 16), RL)
+    my_codes = states[mine, :].astype(F32)
     state = iota((QP, SEQ), 0).astype(F32)
     weight = weights[...]
     lane = iota((QP, TILE), 1)
     local = jnp.concatenate([fields[...], jnp.full((QP - Q, RL), -1e30, F32)], axis=0)
-    for g in range(GROUPS):
+    field_part = jnp.zeros((QP, TILE), F32)
+    ones = jnp.ones((SEQ, TILE), BF16)
+    for r in range(0, RL, 2):
         pieces = []
-        for m in range(GROUP):
-            r = g * GROUP + m
-            logits = field[g, m * QP : (m + 1) * QP, :] + local[:, r : r + 1]
+        for m in (r, r + 1):
+            logits = field[m * QP : (m + 1) * QP, :] + local[:, m : m + 1]
             top = jnp.max(logits, axis=0, keepdims=True)
             raised = jnp.exp(logits - top)
             share = weight / jnp.sum(raised, axis=0, keepdims=True)
-            hot_own = jnp.where(state == my_codes[r : r + 1], weight, 0.0)
+            hot_own = jnp.where(state == my_codes[m : m + 1], weight, 0.0)
             pieces.append(raised * share - hot_own)
-        resid_out[g] = jnp.concatenate(pieces, axis=0).astype(BF16)
-    field_part = jnp.zeros((QP, TILE), F32)
-    ones = jnp.ones((SEQ, TILE), BF16)
-    for g in range(GROUPS):
-        sums = dot(resid_out[g], ones)
-        for m in range(GROUP):
-            piece = sums[m * QP : (m + 1) * QP]
-            field_part = jnp.where(lane == g * GROUP + m, piece, field_part)
+        resid_out[r * QP : (r + 2) * QP, :] = jnp.concatenate(pieces, axis=0).astype(BF16)
+    sums = dot(resid_out[...], ones)
+    for r in range(RL):
+        field_part = jnp.where(lane == r, sums[r * QP : (r + 1) * QP], field_part)
     field_out[...] = field_part
 
     add_grad(keys_ref, bounds, resid_out, hot, grad)
-    wide[Q * Q // 8 * 8 : PADQ, :] = jnp.zeros((PADQ - Q * Q // 8 * 8, PAIRS), F32)
+    for n in range(4):
+        wide[n * TILE + QUARTER : (n + 1) * TILE, :] = jnp.zeros((TILE - QUARTER, PAIRS), F32)
+    last = 3 * TILE + Q * Q - 3 * QUARTER
+    wide[last // 8 * 8 : 3 * TILE + QUARTER, :] = jnp.zeros((3 * TILE + QUARTER - last // 8 * 8, PAIRS), F32)
     for n in range(WIDE):
+        lanes = slice(n * TILE, (n + 1) * TILE)
         for a, column in enumerate(load_grad(grad, n)):
-            wide[a * Q : (a + 1) * Q, n * TILE : (n + 1) * TILE] = column[0:Q]
-    plain = dot(wide[...].astype(BF16), plain_order(place))
-    rest = jnp.zeros((TILE - QUARTER, PAIRS), F32)
+            done = 0
+            while done < Q:
+                quarter, row = divmod(a * Q + done, QUARTER)
+                size = min(Q - done, QUARTER - row)
+                start = quarter * TILE + row
+                wide[start : start + size, lanes] = column[done : done + size]
+                done += size
+    result = lax.dot_general(
+        to_sorted, wide[...].astype(BF16), (((1,), (1,)), ((), ())), preferred_element_type=F32
+    )
     for n in range(4):
-        part = jnp.concatenate([plain[n * QUARTER : (n + 1) * QUARTER], rest], axis=0)
-        grad_out[n] = jnp.transpose(part).astype(BF16)
-
-
-def recv_half(received, order, own, fields, weights):
+        grad_out[n] = result[:, n * TILE : (n + 1) * TILE].astype(BF16)
+
+
+def recv_half(received, states, own, fields, weights):
     return pl.pallas_call(
         recv_kernel,
         out_shape=(
             jax.ShapeDtypeStruct((4, PAIRS, TILE), BF16),
-            jax.ShapeDtypeStruct((GROUPS, GROWS, SEQ), BF16),
+            jax.ShapeDtypeStruct((ROWS, SEQ), BF16),
             jax.ShapeDtypeStruct((QP, TILE), F32),
         ),
-        in_specs=[VMEM] * 4 + [SMEM] + [VMEM] * 4,
+        in_specs=[VMEM] * 5,
         out_specs=(VMEM,) * 3,
         scratch_shapes=[
-            pltpu.VMEM((PADQ, PAIRS), F32),
+            pltpu.VMEM((4 * TILE, PAIRS), F32),
             pltpu.VMEM((512, PAIRS), F32),
             pltpu.VMEM((TILES, DUOS, QP, TILE), F32),
             pltpu.VMEM((TILES, DEEP, SEQ), BF16),
-            pltpu.VMEM((GROWS, DEEP), BF16),
-            pltpu.VMEM((GROUPS, GROWS, SEQ), F32),
+            pltpu.VMEM((WROWS, DEEP), BF16),
+            pltpu.VMEM((ROWS, SEQ), F32),
             pltpu.VMEM((TILES, DUOS, QP, TILE), F32),
+            pltpu.VMEM((PAIRS, SEQ), BF16),
+            pltpu.VMEM((PAIRS, SEQ), F32),
+            pltpu.VMEM((TILES, 8, TILE), F32),
+            pltpu.SMEM((2, TILES), jnp.int32),
         ],
         compiler_params=PARAMS,
         cost_estimate=pl.CostEstimate(
             flops=20_000_000_000, bytes_accessed=10_000_000, transcendentals=0
         ),
         name="recv_half",
-    )(received, *order, own, fields, weights)
+    )(received, states, own, fields, weights)
 
 
 def own_grad_kernel(
@@ -523,9 +510,7 @@
     )
     received = swap_blocks(pack)
     states, far, place, keys, bounds, field = own_field(alignment, pack, coup)
-    received, field, states = lax.optimization_barrier((received, field, states))
-    order = recv_order(received, states)
-    remote_grad, resid, field_part = recv_half(received, order, field, fields.T, seq_weights[None, :])
+    remote_grad, resid, field_part = recv_half(received, states, field, fields.T, seq_weights[None, :])
     swapped = swap_quarters(remote_grad)
     local_quarters = own_grad(keys, bounds, place, far, resid, field_part)
     local_chunks = scatter_seq(local_quarters)

time: 88.7 us -> 86 us (0.970)
  Pallas kernels: 31.3 us -> 22.9 us
  waiting for transfers between devices: 22.8 us -> 26.7 us
  local copies, waits for them, and re-layouts: 4.01 us -> 5.28 us
  starting transfers between devices: 29.1 us -> 30.1 us
    pallas_call x1, Pallas kernels: 11.1 us -> 8.81 us  [recv_half(): pl.pallas_call(recv_kernel, out_shape=(jax.ShapeDtypeStruct((4, PAIRS, TI...]
    pallas_call x1 -> x0, Pallas kernels: 2.25 us -> none  [recv_order(): pl.pallas_call(recv_order_kernel, out_shape=(jax.ShapeDtypeStruct((PAIRS,...]
    pallas_call x1, Pallas kernels: 6.63 us -> 4.66 us  [own_grad(): pl.pallas_call(own_grad_kernel, out_shape=(jax.ShapeDtypeStruct((TILE, PA...]
    pallas_call x1, Pallas kernels: 7.27 us -> 5.39 us  [own_field(): pl.pallas_call(own_field_kernel, out_shape=(jax.ShapeDtypeStruct((RES, SE...]
    all_to_all x1, waiting for transfers between devices: 6.02 us -> 7.89 us  [swap_blocks(): lax.all_to_all(blocks, 'res', split_axis=0, concat_axis=0, tiled=True)]
    unnamed x14, local copies, waits for them, and re-layouts: 4.01 us -> 5.28 us
    all_to_all x1, waiting for transfers between devices: 1.92 us -> 3.05 us  [swap_quarters(): lax.all_to_all(blocks, ('seq', 'res'), split_axis=0, concat_axis=0, tiled...]
    all_to_all x1, starting transfers between devices: 8.98 us -> 9.94 us  [swap_quarters(): lax.all_to_all(blocks, ('seq', 'res'), split_axis=0, concat_axis=0, tiled...]
  transfers between devices with their start and end apart: 8 -> 8, of which waited for: 7 -> 7; matrix products, arithmetic and copies ran while one was open for 0% -> 0% of each run, Pallas kernels for 16% -> 12%
where the time goes in v4:
time: 86 us; the launch traced here: 85.7 us
  starting transfers between devices  30.1 us (35%)
  waiting for transfers between devices  26.7 us (31%)
  Pallas kernels  22.9 us (27%)
  local copies, waits for them, and re-layouts  5.28 us (6%)
    ppermute x6, waiting for transfers between devices, shifted(): return lax.ppermute(array, 'seq', [(i, (i + k) % 4) for i in range(4)])  15.7 us
    all_to_all x1, starting transfers between devices, swap_blocks(): lax.all_to_all(blocks, 'res', split_axis=0, concat_axis=0, tiled=True)  13 us
    all_to_all x1, starting transfers between devices, swap_quarters(): lax.all_to_all(blocks, ('seq', 'res'), split_axis=0, concat_axis=0, tiled...  9.94 us
    pallas_call x1, Pallas kernels, recv_half(): pl.pallas_call(recv_kernel, out_shape=(jax.ShapeDtypeStruct((4, PAIRS, TI...  8.81 us
    all_to_all x1, waiting for transfers between devices, swap_blocks(): lax.all_to_all(blocks, 'res', split_axis=0, concat_axis=0, tiled=True)  7.89 us
    ppermute x6, starting transfers between devices, shifted(): return lax.ppermute(array, 'seq', [(i, (i + k) % 4) for i in range(4)])  7.18 us
    pallas_call x1, Pallas kernels, own_field(): pl.pallas_call(own_field_kernel, out_shape=(jax.ShapeDtypeStruct((RES, SE...  5.39 us
    unnamed x14, local copies, waits for them, and re-layouts  5.28 us
  transfers between devices with their start and end apart: 8, of which 7 were waited for; matrix products, arithmetic and copies ran while one was open for 0% of the time, Pallas kernels for 12%

profile of v4, /device:TPU:1, one launch (start us, length us, event | category | flops | bytes accessed | tf_op | source)
XLA Modules:
  0.0 85.7 jit_solution(10128123693070456828)
XLA Ops:
  0.6 0.0 copy-start.1
  0.6 2.3 %pack_pairs.1.pack = bf16[512,512]{1,0:T(8,128)(2,1)} custom-call(bf16[441,512]{1,0:T(8,128)(2,1)} %bitcast.16, s32[1,512]{1,0:T(1,128)} %bitcast.21, s32[1,512]{1,0:T(1,128)} %bitcast.22, s32[1,256]{1,0:T(1,128)} %bitcast.23, s32[1,64]{1,0:T(1,128)} %bitcast.24), custom_call_target="tpu_custom_call" | custom-call | tf_op jit(solution)/shard_map/pack_pairs/pallas_call | solution.py:71
  2.9 13.0 %all-to-all-start = ((bf16[64,8,512]{2,1,0:T(8,128)(2,1)}), bf16[64,8,512]{2,1,0:T(8,128)(2,1)S(1)}, u32[]{:S(2)}, u32[]{:S(2)}) async-start(bf16[64,8,512]{2,1,0:T(8,128)(2,1)} %bitcast.14), calls=%async_computation | async-start | bytes 1048576 | tf_op jit(solution)/shard_map/all_to_all | solution.py:493
  15.9 0.0 copy-done.1
  15.9 0.0 copy-start
  15.9 1.1 %copy-done = bf16[512,512]{1,0:T(8,128)(2,1)S(1)} copy-done((bf16[512,512]{1,0:T(8,128)(2,1)S(1)}, bf16[512,512]{1,0:T(8,128)(2,1)}, u32[]{:S(2)}) %copy-start) | copy-done | bytes 524312
  17.0 0.0 copy-start.2
  17.0 1.9 %copy-done.2 = s32[3072,256]{1,0:T(8,128)S(1)} copy-done((s32[3072,256]{1,0:T(8,128)S(1)}, s32[3072,256]{1,0:T(8,128)}, u32[]{:S(2)}) %copy-start.2) | copy-done | bytes 3145752
  18.9 0.0 copy-start.3
  18.9 0.0 copy-start.4
  18.9 5.4 %own_field.1 = (bf16[3072,256]{1,0:T(8,128)(2,1)S(1)}, s8[512,256]{1,0:T(32,128)(4,1)S(1)}, f32[8,512]{1,0:T(8,128)S(1)}, f32[8,8,128]{2,1,0:T(8,128)S(1)}, s32[2,8]{1,0:T(2,128)S(1)}, /*index=5*/f32[1152,256]{1,0:T(8,128)S(1)}) custom-call(s32[3072,256]{1,0:T(8,128)S(1)} %copy-done.2, bf16[512,512]{1,0:T(8,128)(2,1)S(1)} %copy-done, ...), custom_call_target="tpu_custom_call" | custom-call | flops 10000000000 | bytes 10000000 | tf_op jit(solution)/shard_map/own_field/pallas_call | solution.py:259
  24.3 0.0 copy-start.5
  24.3 1.0 %copy-done.5 = f32[1152,256]{1,0:T(8,128)} copy-done((f32[1152,256]{1,0:T(8,128)}, f32[1152,256]{1,0:T(8,128)S(1)}, u32[]{:S(2)}) %copy-start.5) | copy-done | bytes 1179672
  25.3 7.9 %all-to-all-done = bf16[64,8,512]{2,1,0:T(8,128)(2,1)S(1)} async-done(((bf16[64,8,512]{2,1,0:T(8,128)(2,1)}), bf16[64,8,512]{2,1,0:T(8,128)(2,1)S(1)}, u32[]{:S(2)}, u32[]{:S(2)}) %all-to-all-start) | async-done | bytes 524320 | tf_op jit(solution)/shard_map/all_to_all | solution.py:493
  33.2 0.0 copy-done.3
  33.2 0.0 copy-done.4
  33.2 0.0 copy-start.6
  33.2 1.3 %copy-done.6 = f32[1152,256]{1,0:T(8,128)S(1)} copy-done((f32[1152,256]{1,0:T(8,128)S(1)}, f32[1152,256]{1,0:T(8,128)}, u32[]{:S(2)}) %copy-start.6) | copy-done | bytes 1179672
  34.5 8.8 %recv_half.1 = (bf16[4,512,128]{2,1,0:T(8,128)(2,1)}, bf16[1152,256]{1,0:T(8,128)(2,1)S(1)}, f32[24,128]{1,0:T(8,128)S(1)}) custom-call(bf16[512,512]{1,0:T(8,128)(2,1)S(1)} %bitcast.15, bf16[3072,256]{1,0:T(8,128)(2,1)S(1)} %get-tuple-element.21.states, f32[1152,256]{1,0:T(8,128)S(1)} %copy-done.6, f32[21,48]{1,0:T(8,128)S(1)} %bitcast.18, ...), custom_call_target="tpu_custom_call" | custom-call | flops 20000000000 | bytes 10000000 | tf_op jit(solution)/shard_map/recv_half/pallas_call | solution.py:355
  43.3 9.9 %all-to-all-start.1 = ((bf16[256,8,128]{2,1,0:T(8,128)(2,1)}), bf16[256,8,128]{2,1,0:T(8,128)(2,1)S(1)}, u32[]{:S(2)}, u32[]{:S(2)}) async-start(bf16[256,8,128]{2,1,0:T(8,128)(2,1)} %bitcast.9), calls=%async_computation.1 | async-start | bytes 1048576 | tf_op jit(solution)/shard_map/all_to_all | solution.py:499
  53.2 4.7 %own_grad.1 = (bf16[128,512]{1,0:T(8,128)(2,1)S(1)}, bf16[128,512]{1,0:T(8,128)(2,1)S(1)}, bf16[128,512]{1,0:T(8,128)(2,1)S(1)}, bf16[128,512]{1,0:T(8,128)(2,1)S(1)}) custom-call(f32[8,8,128]{2,1,0:T(8,128)S(1)} %get-tuple-element.17.keys_ref, s32[2,8]{1,0:T(2,128)S(1)} %get-tuple-element.18.bounds, f32[8,512]{1,0:T(8,128)S(1)} %get-tuple-element.19.place, ...), custom_call_target="tpu_custom_call" | custom-call | flops 6000000000 | bytes 8000000 | tf_op jit(solution)/shard_map/own_grad/pallas_call | solution.py:411
  57.9 1.5 %collective-permute-start = (bf16[128,512]{1,0:T(8,128)(2,1)S(1)}, bf16[128,512]{1,0:T(8,128)(2,1)S(1)}, u32[]{:S(2)}, u32[]{:S(2)}) collective-permute-start(bf16[128,512]{1,0:T(8,128)(2,1)S(1)} %get-tuple-element.26), channel_id=1, source_target_pairs={{0,64},{64,128},{128,192},{192,0},{1,65},{65,129},{129,193},{193,1... | collective-permute-start | bytes 393224 | tf_op jit(solution)/shard_map/ppermute | solution.py:480
  59.4 2.4 %collective-permute-start.1 = (bf16[128,512]{1,0:T(8,128)(2,1)S(1)}, bf16[128,512]{1,0:T(8,128)(2,1)S(1)}, u32[]{:S(2)}, u32[]{:S(2)}) collective-permute-start(bf16[128,512]{1,0:T(8,128)(2,1)S(1)} %get-tuple-element.27), channel_id=1, source_target_pairs={{0,128},{64,192},{128,0},{192,64},{1,129},{65,193},{129,1},{193,65... | collective-permute-start | bytes 393224 | tf_op jit(solution)/shard_map/ppermute | solution.py:480
  61.8 1.1 %collective-permute-start.2 = (bf16[128,512]{1,0:T(8,128)(2,1)S(1)}, bf16[128,512]{1,0:T(8,128)(2,1)S(1)}, u32[]{:S(2)}, u32[]{:S(2)}) collective-permute-start(bf16[128,512]{1,0:T(8,128)(2,1)S(1)} %get-tuple-element.28), channel_id=1, source_target_pairs={{0,192},{64,0},{128,64},{192,128},{1,193},{65,1},{129,65},{193,129... | collective-permute-start | bytes 393224 | tf_op jit(solution)/shard_map/ppermute | solution.py:480
  63.0 1.6 %collective-permute-done.r1 = bf16[128,512]{1,0:T(8,128)(2,1)S(1)} collective-permute-done((bf16[128,512]{1,0:T(8,128)(2,1)S(1)}, bf16[128,512]{1,0:T(8,128)(2,1)S(1)}, u32[]{:S(2)}, u32[]{:S(2)}) %collective-permute-start) | collective-permute-done | bytes 131104 | tf_op jit(solution)/shard_map/ppermute | solution.py:480
  64.5 7.1 %collective-permute-done.1.r2 = bf16[128,512]{1,0:T(8,128)(2,1)S(1)} collective-permute-done((bf16[128,512]{1,0:T(8,128)(2,1)S(1)}, bf16[128,512]{1,0:T(8,128)(2,1)S(1)}, u32[]{:S(2)}, u32[]{:S(2)}) %collective-permute-start.1) | collective-permute-done | bytes 131104 | tf_op jit(solution)/shard_map/ppermute | solution.py:480
  71.6 0.0 collective-permute-done.2.r3
  71.6 3.0 %all-to-all-done.1 = bf16[256,8,128]{2,1,0:T(8,128)(2,1)S(1)} async-done(((bf16[256,8,128]{2,1,0:T(8,128)(2,1)}), bf16[256,8,128]{2,1,0:T(8,128)(2,1)S(1)}, u32[]{:S(2)}, u32[]{:S(2)}) %all-to-all-start.1) | async-done | bytes 524320 | tf_op jit(solution)/shard_map/all_to_all | solution.py:499
  74.7 0.7 join_parts.1
  75.4 0.7 collective-permute-start.5
  76.1 1.4 %collective-permute-start.4 = (bf16[112,512]{1,0:T(8,128)(2,1)S(1)}, bf16[112,512]{1,0:T(8,128)(2,1)S(1)}, u32[]{:S(2)}, u32[]{:S(2)}) collective-permute-start(bf16[112,512]{1,0:T(8,128)(2,1)S(1)} %get-tuple-element.30.c0), channel_id=1, source_target_pairs={{0,128},{64,192},{128,0},{192,64},{1,129},{65,193},{129,1},{193,65... | collective-permute-start | bytes 344072 | tf_op jit(solution)/shard_map/ppermute | solution.py:480
  77.5 0.0 collective-permute-start.3
  77.5 2.2 %collective-permute-done.5.c3 = bf16[112,512]{1,0:T(8,128)(2,1)S(1)} collective-permute-done((bf16[112,512]{1,0:T(8,128)(2,1)S(1)}, bf16[112,512]{1,0:T(8,128)(2,1)S(1)}, u32[]{:S(2)}, u32[]{:S(2)}) %collective-permute-start.5) | collective-permute-done | bytes 114720 | tf_op jit(solution)/shard_map/ppermute | solution.py:480
  79.7 1.9 %collective-permute-done.4.c2 = bf16[112,512]{1,0:T(8,128)(2,1)S(1)} collective-permute-done((bf16[112,512]{1,0:T(8,128)(2,1)S(1)}, bf16[112,512]{1,0:T(8,128)(2,1)S(1)}, u32[]{:S(2)}, u32[]{:S(2)}) %collective-permute-start.4) | collective-permute-done | bytes 114720 | tf_op jit(solution)/shard_map/ppermute | solution.py:480
  81.7 3.0 %collective-permute-done.3.c1 = bf16[112,512]{1,0:T(8,128)(2,1)S(1)} collective-permute-done((bf16[112,512]{1,0:T(8,128)(2,1)S(1)}, bf16[112,512]{1,0:T(8,128)(2,1)S(1)}, u32[]{:S(2)}, u32[]{:S(2)}) %collective-permute-start.3) | collective-permute-done | bytes 114720 | tf_op jit(solution)/shard_map/ppermute | solution.py:480
  84.6 1.1 %place_parts.1 = f32[441,512]{1,0:T(8,128)} custom-call(bf16[112,512]{1,0:T(8,128)(2,1)S(1)} %get-tuple-element.30.c0, bf16[112,512]{1,0:T(8,128)(2,1)S(1)} %collective-permute-done.3.c1, bf16[112,512]{1,0:T(8,128)(2,1)S(1)} %collective-permute-done.4.c2, bf16[112,512]{1,0:T(8,128)(2,1)S(1)} %collective-permute-done.5.c3), custom_call_target="tpu_custom_call" | custom-call | tf_op jit(solution)/shard_map/place_parts/pallas_call | solution.py:468
Async XLA Ops:
  0.6 15.3 %copy-start.1 = (bf16[512,441]{0,1:T(8,128)(2,1)S(1)}, bf16[512,441]{0,1:T(8,128)(2,1)}, u32[]{:S(2)}) copy-start(bf16[512,441]{0,1:T(8,128)(2,1)} %param.11) | copy-start | bytes 1354756
  2.9 30.3 %all-to-all-start = ((bf16[64,8,512]{2,1,0:T(8,128)(2,1)}), bf16[64,8,512]{2,1,0:T(8,128)(2,1)S(1)}, u32[]{:S(2)}, u32[]{:S(2)}) async-start(bf16[64,8,512]{2,1,0:T(8,128)(2,1)} %bitcast.14), calls=%async_computation | async-start | bytes 1048576 | tf_op jit(solution)/shard_map/all_to_all | solution.py:493
  15.9 1.1 %copy-start = (bf16[512,512]{1,0:T(8,128)(2,1)S(1)}, bf16[512,512]{1,0:T(8,128)(2,1)}, u32[]{:S(2)}) copy-start(bf16[512,512]{1,0:T(8,128)(2,1)} %pack_pairs.1.pack) | copy-start | bytes 1572868
  17.0 1.9 %copy-start.2 = (s32[3072,256]{1,0:T(8,128)S(1)}, s32[3072,256]{1,0:T(8,128)}, u32[]{:S(2)}) copy-start(s32[3072,256]{1,0:T(8,128)} %alignment.1) | copy-start | bytes 9437188
  18.9 14.3 %copy-start.3 = (f32[48,21]{0,1:T(8,128)S(1)}, f32[48,21]{0,1:T(8,128)}, u32[]{:S(2)}) copy-start(f32[48,21]{0,1:T(8,128)} %param.10) | copy-start | bytes 12100
  18.9 14.3 %copy-start.4 = (f32[256]{0:T(256)S(1)}, f32[256]{0:T(256)}, u32[]{:S(2)}) copy-start(f32[256]{0:T(256)} %param.9) | copy-start | bytes 3076
  24.3 1.0 %copy-start.5 = (f32[1152,256]{1,0:T(8,128)}, f32[1152,256]{1,0:T(8,128)S(1)}, u32[]{:S(2)}) copy-start(f32[1152,256]{1,0:T(8,128)S(1)} %get-tuple-element.22.own) | copy-start | bytes 3538948
  33.2 1.3 %copy-start.6 = (f32[1152,256]{1,0:T(8,128)S(1)}, f32[1152,256]{1,0:T(8,128)}, u32[]{:S(2)}) copy-start(f32[1152,256]{1,0:T(8,128)} %copy-done.5) | copy-start | bytes 3538948
  43.3 31.4 %all-to-all-start.1 = ((bf16[256,8,128]{2,1,0:T(8,128)(2,1)}), bf16[256,8,128]{2,1,0:T(8,128)(2,1)S(1)}, u32[]{:S(2)}, u32[]{:S(2)}) async-start(bf16[256,8,128]{2,1,0:T(8,128)(2,1)} %bitcast.9), calls=%async_computation.1 | async-start | bytes 1048576 | tf_op jit(solution)/shard_map/all_to_all | solution.py:499
  57.9 6.6 %collective-permute-start = (bf16[128,512]{1,0:T(8,128)(2,1)S(1)}, bf16[128,512]{1,0:T(8,128)(2,1)S(1)}, u32[]{:S(2)}, u32[]{:S(2)}) collective-permute-start(bf16[128,512]{1,0:T(8,128)(2,1)S(1)} %get-tuple-element.26), channel_id=1, source_target_pairs={{0,64},{64,128},{128,192},{192,0},{1,65},{65,129},{129,193},{193,1... | collective-permute-start | bytes 393224 | tf_op jit(solution)/shard_map/ppermute | solution.py:480
  59.4 12.2 %collective-permute-start.1 = (bf16[128,512]{1,0:T(8,128)(2,1)S(1)}, bf16[128,512]{1,0:T(8,128)(2,1)S(1)}, u32[]{:S(2)}, u32[]{:S(2)}) collective-permute-start(bf16[128,512]{1,0:T(8,128)(2,1)S(1)} %get-tuple-element.27), channel_id=1, source_target_pairs={{0,128},{64,192},{128,0},{192,64},{1,129},{65,193},{129,1},{193,65... | collective-permute-start | bytes 393224 | tf_op jit(solution)/shard_map/ppermute | solution.py:480
  61.8 9.8 %collective-permute-start.2 = (bf16[128,512]{1,0:T(8,128)(2,1)S(1)}, bf16[128,512]{1,0:T(8,128)(2,1)S(1)}, u32[]{:S(2)}, u32[]{:S(2)}) collective-permute-start(bf16[128,512]{1,0:T(8,128)(2,1)S(1)} %get-tuple-element.28), channel_id=1, source_target_pairs={{0,192},{64,0},{128,64},{192,128},{1,193},{65,1},{129,65},{193,129... | collective-permute-start | bytes 393224 | tf_op jit(solution)/shard_map/ppermute | solution.py:480
  75.4 4.3 %collective-permute-start.5 = (bf16[112,512]{1,0:T(8,128)(2,1)S(1)}, bf16[112,512]{1,0:T(8,128)(2,1)S(1)}, u32[]{:S(2)}, u32[]{:S(2)}) collective-permute-start(bf16[112,512]{1,0:T(8,128)(2,1)S(1)} %get-tuple-element.30.c0), channel_id=1, source_target_pairs={{0,192},{64,0},{128,64},{192,128},{1,193},{65,1},{129,65},{193,129... | collective-permute-start | bytes 344072 | tf_op jit(solution)/shard_map/ppermute | solution.py:480
  76.1 5.5 %collective-permute-start.4 = (bf16[112,512]{1,0:T(8,128)(2,1)S(1)}, bf16[112,512]{1,0:T(8,128)(2,1)S(1)}, u32[]{:S(2)}, u32[]{:S(2)}) collective-permute-start(bf16[112,512]{1,0:T(8,128)(2,1)S(1)} %get-tuple-element.30.c0), channel_id=1, source_target_pairs={{0,128},{64,192},{128,0},{192,64},{1,129},{65,193},{129,1},{193,65... | collective-permute-start | bytes 344072 | tf_op jit(solution)/shard_map/ppermute | solution.py:480
  77.5 7.1 %collective-permute-start.3 = (bf16[112,512]{1,0:T(8,128)(2,1)S(1)}, bf16[112,512]{1,0:T(8,128)(2,1)S(1)}, u32[]{:S(2)}, u32[]{:S(2)}) collective-permute-start(bf16[112,512]{1,0:T(8,128)(2,1)S(1)} %get-tuple-element.30.c0), channel_id=1, source_target_pairs={{0,64},{64,128},{128,192},{192,0},{1,65},{65,129},{129,193},{193,1... | collective-permute-start | bytes 344072 | tf_op jit(solution)/shard_map/ppermute | solution.py:480

commit v5 on v4

--- a/solution.py
+++ b/solution.py
@@ -45,8 +45,8 @@
     return jnp.dot(x, y, preferred_element_type=F32)
 
 
-def pack_kernel(coup, left, slot, residue, count, out, wide):
-    wide[...] = jnp.zeros_like(wide)
+def pack_kernel(coup, left, slot, residue, count, out, wide, held, sems):
+    wide[Q * Q // 8 * 8 : PADQ, :] = jnp.zeros((PADQ - Q * Q // 8 * 8, PAIRS), F32)
     wide[0 : Q * Q, :] = coup[...].astype(F32)
     lane = iota((1, PAIRS), 1)
     bucket = lax.shift_right_logical(lane, 3)
@@ -62,9 +62,15 @@
     index = jnp.where(sub == 2, live, index)
     index = jnp.where(sub == 3, lax.axis_index("res").astype(F32), index)
     index = jnp.where(sub == 4, bucket.astype(F32), index)
+    copies = []
     for n in range(4):
         part = jnp.concatenate([wide[n * QUARTER : (n + 1) * QUARTER, :], index], axis=0)
-        out[:, n * TILE : (n + 1) * TILE] = jnp.transpose(part).astype(BF16)
+        held[n] = jnp.transpose(part).astype(BF16)
+        lanes = slice(n * TILE, (n + 1) * TILE)
+        copies.append(pltpu.make_async_copy(held.at[n], out.at[:, lanes], sems.at[n]))
+        copies[n].start()
+    for copy in copies:
+        copy.wait()
 
 
 def pack_pairs(coup, left, slot, residue, count):
@@ -72,8 +78,12 @@
         pack_kernel,
         out_shape=jax.ShapeDtypeStruct((PAIRS, 4 * TILE), BF16),
         in_specs=[VMEM] * 5,
-        out_specs=VMEM,
-        scratch_shapes=[pltpu.VMEM((PADQ, PAIRS), F32)],
+        out_specs=pl.BlockSpec(memory_space=pl.ANY),
+        scratch_shapes=[
+            pltpu.VMEM((PADQ, PAIRS), F32),
+            pltpu.VMEM((4, PAIRS, TILE), BF16),
+            pltpu.SemaphoreType.DMA((4,)),
+        ],
         compiler_params=LARGE,
         name="pack_pairs",
     )(coup, left, slot, residue, count)
@@ -102,7 +112,7 @@
 
 
 def find_far(far, states, to_plain, plain):
-    count = 5
+    count = 4
     for start in range(0, BLOCKS, count):
         blocks = min(count, BLOCKS - start)
         pairs = slice(start * CAP, (start + blocks) * CAP)
@@ -110,7 +120,7 @@
         depth = min(256, RES - base)
         lane = iota((blocks * CAP, depth), 1).astype(F32)
         pick = jnp.where(far[pairs] - float(base) == lane, 1.0, 0.0).astype(BF16)
-        plain[pairs, :] = dot(pick, states[base : base + depth, :])
+        plain[pairs, :] = dot(pick, states[base : base + depth, :].astype(BF16))
     return dot(to_plain, plain[...].astype(BF16))
 
 
@@ -231,8 +241,8 @@
 
 
 def own_field_kernel(
-    alignment, pack, coup, states, far_out, place_out, keys_ref, bounds, field,
-    sorted_blocks, blocks, hot, lhs, codes, plain,
+    alignment, pack, coup, states_out, codes_out, far_out, place_out, keys_ref, bounds, field,
+    sorted_blocks, blocks, hot, lhs, codes, plain, states,
 ):
     chunk = 512
     parts = [slice(n * chunk, (n + 1) * chunk) for n in range(RES // chunk)]
@@ -248,7 +258,11 @@
         store_blocks(lambda c: sorted_blocks[n, pl.ds(c, QP, stride=Q), :], n, blocks)
     field[...] = jnp.zeros_like(field)
     for rows in parts:
-        states[rows, :] = alignment[rows, :].astype(F32).astype(BF16)
+        part = alignment[rows, :]
+        states[rows, :] = part.astype(F32).astype(BF16)
+        states_out[rows, :] = part.astype(jnp.int8)
+    mine = pl.ds(pl.multiple_of(lax.axis_index("res") * RL, 16), RL)
+    codes_out[...] = states[mine, :]
     far_states = find_far(far, states, to_plain, plain)
     far_out[...] = far_states.astype(jnp.int8)
     codes[...] = far_states.astype(BF16)
@@ -259,7 +273,8 @@
     return pl.pallas_call(
         own_field_kernel,
         out_shape=(
-            jax.ShapeDtypeStruct((RES, SEQ), BF16),
+            jax.ShapeDtypeStruct((RES, SEQ), jnp.int8),
+            jax.ShapeDtypeStruct((RL, SEQ), BF16),
             jax.ShapeDtypeStruct((PAIRS, SEQ), jnp.int8),
             jax.ShapeDtypeStruct((8, PAIRS), F32),
             jax.ShapeDtypeStruct((TILES, 8, TILE), F32),
@@ -267,7 +282,7 @@
             jax.ShapeDtypeStruct((ROWS, SEQ), F32),
         ),
         in_specs=[VMEM, VMEM, VMEM],
-        out_specs=(VMEM, VMEM, VMEM, VMEM, SMEM, VMEM),
+        out_specs=(VMEM,) * 5 + (SMEM, VMEM),
         scratch_shapes=[
             pltpu.VMEM((WIDE, 512, TILE), F32),
             pltpu.VMEM((TILES, DUOS, QP, TILE), F32),
@@ -275,6 +290,7 @@
             pltpu.VMEM((WROWS, DEEP), BF16),
             pltpu.VMEM((PAIRS, SEQ), BF16),
             pltpu.VMEM((PAIRS, SEQ), F32),
+            pltpu.VMEM((RES, SEQ), BF16),
         ],
         compiler_params=PARAMS,
         cost_estimate=pl.CostEstimate(
@@ -285,7 +301,7 @@
 
 
 def recv_kernel(
-    parts, states, own, fields, weights,
+    parts, states, codes, own, fields, weights,
     grad_out, resid_out, field_out,
     wide, sorted_blocks, blocks, hot, lhs, field, grad, far, plain, keys_ref, bounds,
 ):
@@ -306,8 +322,7 @@
     field[...] = own[...]
     add_field(keys_ref, bounds, blocks, far, hot, lhs, field)
 
-    mine = pl.ds(pl.multiple_of(lax.axis_index("res") * RL, 16), RL)
-    my_codes = states[mine, :].astype(F32)
+    my_codes = codes[...].astype(F32)
     state = iota((QP, SEQ), 0).astype(F32)
     weight = weights[...]
     lane = iota((QP, TILE), 1)
@@ -351,7 +366,7 @@
         grad_out[n] = result[:, n * TILE : (n + 1) * TILE].astype(BF16)
 
 
-def recv_half(received, states, own, fields, weights):
+def recv_half(received, states, codes, own, fields, weights):
     return pl.pallas_call(
         recv_kernel,
         out_shape=(
@@ -359,7 +374,7 @@
             jax.ShapeDtypeStruct((ROWS, SEQ), BF16),
             jax.ShapeDtypeStruct((QP, TILE), F32),
         ),
-        in_specs=[VMEM] * 5,
+        in_specs=[VMEM] * 6,
         out_specs=(VMEM,) * 3,
         scratch_shapes=[
             pltpu.VMEM((4 * TILE, PAIRS), F32),
@@ -379,21 +394,19 @@
             flops=20_000_000_000, bytes_accessed=10_000_000, transcendentals=0
         ),
         name="recv_half",
-    )(received, states, own, fields, weights)
+    )(received, states, codes, own, fields, weights)
 
 
 def own_grad_kernel(
-    keys_ref, bounds, place, far, resid, field_part, g0, g1, g2, g3, grad, wide, full, hot
+    keys_ref, bounds, place, far, resid, field_part, g0, g1, g2, g3, grad, wide, full, hot, rows
 ):
     add_grad(keys_ref, bounds, resid, hot, grad, far)
-    to_plain = plain_order(place)
-    total = jnp.zeros((PADQ, PAIRS), F32)
     for n in range(WIDE):
         wide[n, Q * Q // 8 * 8 : PADQ, :] = jnp.zeros((PADQ - Q * Q // 8 * 8, TILE), F32)
         for c, column in enumerate(load_grad(grad, n)):
             wide[n, pl.ds(c, Q, stride=Q), :] = column[0:Q]
-        total = total + dot(wide[n].astype(BF16), to_plain[n * TILE : (n + 1) * TILE, :])
-    full[...] = total
+        rows[:, n * TILE : (n + 1) * TILE] = wide[n].astype(BF16)
+    full[...] = dot(rows[...], plain_order(place))
     outs = (g0, g1, g2, g3)
     store_quarters(full, outs)
     exact = field_part[...]
@@ -418,6 +431,7 @@
             pltpu.VMEM((WIDE, PADQ, TILE), F32),
             pltpu.VMEM((PADQ, PAIRS), F32),
             pltpu.VMEM((TILES, DEEP, SEQ), BF16),
+            pltpu.VMEM((PADQ, PAIRS), BF16),
         ],
         compiler_params=PARAMS,
         cost_estimate=pl.CostEstimate(
@@ -457,11 +471,18 @@
     )(*chunks, remote)
 
 
-def place_kernel(c0, c1, c2, c3, out, wide):
+def place_kernel(c0, c1, c2, c3, out):
+    short = Q * Q - 3 * QUARTER
     for back, part in enumerate((c0, c1, c2, c3)):
         owner = lax.rem(lax.axis_index("seq") + (4 - back), 4)
-        wide[pl.ds(pl.multiple_of(owner * QUARTER, 8), QUARTER), :] = part[...].astype(F32)
-    out[...] = wide[0 : Q * Q, :]
+
+        @pl.when(owner < 3)
+        def _():
+            out[pl.ds(pl.multiple_of(owner * QUARTER, 8), QUARTER), :] = part[...].astype(F32)
+
+        @pl.when(owner == 3)
+        def _():
+            out[3 * QUARTER : Q * Q, :] = part[0:short, :].astype(F32)
 
 
 def place_parts(chunks):
@@ -470,7 +491,6 @@
         out_shape=jax.ShapeDtypeStruct((Q * Q, PAIRS), F32),
         in_specs=[VMEM] * 4,
         out_specs=VMEM,
-        scratch_shapes=[pltpu.VMEM((PADQ, PAIRS), F32)],
         compiler_params=SMALL,
         name="place_parts",
     )(*chunks)
@@ -509,8 +529,8 @@
         coup, pair_left[None, :], pair_slot[None, :], slot_residue[None, :], pair_count[None, :]
     )
     received = swap_blocks(pack)
-    states, far, place, keys, bounds, field = own_field(alignment, pack, coup)
-    remote_grad, resid, field_part = recv_half(received, states, field, fields.T, seq_weights[None, :])
+    states, codes, far, place, keys, bounds, field = own_field(alignment, pack, coup)
+    remote_grad, resid, field_part = recv_half(received, states, codes, field, fields.T, seq_weights[None, :])
     swapped = swap_quarters(remote_grad)
     local_quarters = own_grad(keys, bounds, place, far, resid, field_part)
     local_chunks = scatter_seq(local_quarters)

time: 86 us -> 84.6 us (0.984)
  local copies, waits for them, and re-layouts: 5.28 us -> 3.98 us
    unnamed x14 -> x10, local copies, waits for them, and re-layouts: 5.28 us -> 3.98 us
  transfers between devices with their start and end apart: 8 -> 8, of which waited for: 7 -> 7; matrix products, arithmetic and copies ran while one was open for 0% -> 0% of each run, Pallas kernels for 12% -> 11%
where the time goes in v5:
time: 84.6 us; the launch traced here: 84.3 us
  starting transfers between devices  30.1 us (36%)
  waiting for transfers between devices  27.2 us (32%)
  Pallas kernels  22.3 us (26%)
  local copies, waits for them, and re-layouts  3.98 us (5%)
    ppermute x6, waiting for transfers between devices, shifted(): return lax.ppermute(array, 'seq', [(i, (i + k) % 4) for i in range(4)])  15.7 us
    all_to_all x1, starting transfers between devices, swap_blocks(): lax.all_to_all(blocks, 'res', split_axis=0, concat_axis=0, tiled=True)  13 us
    all_to_all x1, starting transfers between devices, swap_quarters(): lax.all_to_all(blocks, ('seq', 'res'), split_axis=0, concat_axis=0, tiled...  9.94 us
    pallas_call x1, Pallas kernels, recv_half(): pl.pallas_call(recv_kernel, out_shape=(jax.ShapeDtypeStruct((4, PAIRS, TI...  8.82 us
    all_to_all x1, waiting for transfers between devices, swap_blocks(): lax.all_to_all(blocks, 'res', split_axis=0, concat_axis=0, tiled=True)  8.08 us
    ppermute x6, starting transfers between devices, shifted(): return lax.ppermute(array, 'seq', [(i, (i + k) % 4) for i in range(4)])  7.18 us
    pallas_call x1, Pallas kernels, own_field(): pl.pallas_call(own_field_kernel, out_shape=(jax.ShapeDtypeStruct((RES, SE...  5.24 us
    pallas_call x1, Pallas kernels, own_grad(): pl.pallas_call(own_grad_kernel, out_shape=(jax.ShapeDtypeStruct((TILE, PA...  4.32 us
  transfers between devices with their start and end apart: 8, of which 7 were waited for; matrix products, arithmetic and copies ran while one was open for 0% of the time, Pallas kernels for 11%

profile of v5, /device:TPU:1, one launch (start us, length us, event | category | flops | bytes accessed | tf_op | source)
XLA Modules:
  0.0 84.3 jit_solution(7319825724813308772)
XLA Ops:
  0.6 2.1 %pack_pairs.1.pack = bf16[512,512]{1,0:T(8,128)(2,1)} custom-call(bf16[441,512]{1,0:T(8,128)(2,1)} %bitcast.16, s32[1,512]{1,0:T(1,128)} %bitcast.21, s32[1,512]{1,0:T(1,128)} %bitcast.22, s32[1,256]{1,0:T(1,128)} %bitcast.23, s32[1,64]{1,0:T(1,128)} %bitcast.24), custom_call_target="tpu_custom_call" | custom-call | tf_op jit(solution)/shard_map/pack_pairs/pallas_call | solution.py:77
  2.8 13.0 %all-to-all-start = ((bf16[64,8,512]{2,1,0:T(8,128)(2,1)}), bf16[64,8,512]{2,1,0:T(8,128)(2,1)S(1)}, u32[]{:S(2)}, u32[]{:S(2)}) async-start(bf16[64,8,512]{2,1,0:T(8,128)(2,1)} %bitcast.14), calls=%async_computation | async-start | bytes 1048576 | tf_op jit(solution)/shard_map/all_to_all | solution.py:513
  15.8 0.0 copy-start
  15.8 1.1 %copy-done = bf16[512,512]{1,0:T(8,128)(2,1)S(1)} copy-done((bf16[512,512]{1,0:T(8,128)(2,1)S(1)}, bf16[512,512]{1,0:T(8,128)(2,1)}, u32[]{:S(2)}) %copy-start) | copy-done | bytes 524312
  16.8 0.0 copy-start.1
  16.8 1.0 %copy-done.1 = bf16[512,441]{0,1:T(8,128)(2,1)S(1)} copy-done((bf16[512,441]{0,1:T(8,128)(2,1)S(1)}, bf16[512,441]{0,1:T(8,128)(2,1)}, u32[]{:S(2)}) %copy-start.1) | copy-done | bytes 451608
  17.9 0.0 copy-start.2
  17.9 1.9 %copy-done.2 = s32[3072,256]{1,0:T(8,128)S(1)} copy-done((s32[3072,256]{1,0:T(8,128)S(1)}, s32[3072,256]{1,0:T(8,128)}, u32[]{:S(2)}) %copy-start.2) | copy-done | bytes 3145752
  19.8 0.0 copy-start.3
  19.8 0.0 copy-start.4
  19.8 5.2 %own_field.1 = (s8[3072,256]{1,0:T(32,128)(4,1)S(1)}, bf16[48,256]{1,0:T(8,128)(2,1)S(1)}, s8[512,256]{1,0:T(32,128)(4,1)S(1)}, f32[8,512]{1,0:T(8,128)S(1)}, f3...) custom-call(s32[3072,256]{1,0:T(8,128)S(1)} %copy-done.2, bf16[512,512]{1,0:T(8,128)(2,1)S(1)} %copy-done, ...), custom_call_target="tpu_custom_call" | custom-call | flops 10000000000 | bytes 10000000 | tf_op jit(solution)/shard_map/own_field/pallas_call | solution.py:273
  25.0 8.1 %all-to-all-done = bf16[64,8,512]{2,1,0:T(8,128)(2,1)S(1)} async-done(((bf16[64,8,512]{2,1,0:T(8,128)(2,1)}), bf16[64,8,512]{2,1,0:T(8,128)(2,1)S(1)}, u32[]{:S(2)}, u32[]{:S(2)}) %all-to-all-start) | async-done | bytes 524320 | tf_op jit(solution)/shard_map/all_to_all | solution.py:513
  33.1 0.0 copy-done.3
  33.1 0.0 copy-done.4
  33.1 8.8 %recv_half.1 = (bf16[4,512,128]{2,1,0:T(8,128)(2,1)}, bf16[1152,256]{1,0:T(8,128)(2,1)S(1)}, f32[24,128]{1,0:T(8,128)S(1)}) custom-call(bf16[512,512]{1,0:T(8,128)(2,1)S(1)} %bitcast.15, s8[3072,256]{1,0:T(32,128)(4,1)S(1)} %get-tuple-element.22.states, bf16[48,256]{1,0:T(8,128)(2,1)S(1)} %get-tuple-element.23.codes, f32[1152,256]{1,0:T(8,128)S(1)} %get-tuple-element.24.own, ...), custom_call_target="tpu_custom_call" | custom-call | flops 20000000000 | bytes 10000000 | tf_op jit(solution)/shard_map/recv_half/pallas_call | solution.py:370
  41.9 9.9 %all-to-all-start.1 = ((bf16[256,8,128]{2,1,0:T(8,128)(2,1)}), bf16[256,8,128]{2,1,0:T(8,128)(2,1)S(1)}, u32[]{:S(2)}, u32[]{:S(2)}) async-start(bf16[256,8,128]{2,1,0:T(8,128)(2,1)} %bitcast.9), calls=%async_computation.1 | async-start | bytes 1048576 | tf_op jit(solution)/shard_map/all_to_all | solution.py:519
  51.9 4.3 %own_grad.1 = (bf16[128,512]{1,0:T(8,128)(2,1)S(1)}, bf16[128,512]{1,0:T(8,128)(2,1)S(1)}, bf16[128,512]{1,0:T(8,128)(2,1)S(1)}, bf16[128,512]{1,0:T(8,128)(2,1)S(1)}) custom-call(f32[8,8,128]{2,1,0:T(8,128)S(1)} %get-tuple-element.18.keys_ref, s32[2,8]{1,0:T(2,128)S(1)} %get-tuple-element.19.bounds, f32[8,512]{1,0:T(8,128)S(1)} %get-tuple-element.20.place, ...), custom_call_target="tpu_custom_call" | custom-call | flops 6000000000 | bytes 8000000 | tf_op jit(solution)/shard_map/own_grad/pallas_call | solution.py:424
  56.2 1.5 %collective-permute-start = (bf16[128,512]{1,0:T(8,128)(2,1)S(1)}, bf16[128,512]{1,0:T(8,128)(2,1)S(1)}, u32[]{:S(2)}, u32[]{:S(2)}) collective-permute-start(bf16[128,512]{1,0:T(8,128)(2,1)S(1)} %get-tuple-element.28), channel_id=1, source_target_pairs={{0,64},{64,128},{128,192},{192,0},{1,65},{65,129},{129,193},{193,1... | collective-permute-start | bytes 393224 | tf_op jit(solution)/shard_map/ppermute | solution.py:500
  57.7 2.4 %collective-permute-start.1 = (bf16[128,512]{1,0:T(8,128)(2,1)S(1)}, bf16[128,512]{1,0:T(8,128)(2,1)S(1)}, u32[]{:S(2)}, u32[]{:S(2)}) collective-permute-start(bf16[128,512]{1,0:T(8,128)(2,1)S(1)} %get-tuple-element.29), channel_id=1, source_target_pairs={{0,128},{64,192},{128,0},{192,64},{1,129},{65,193},{129,1},{193,65... | collective-permute-start | bytes 393224 | tf_op jit(solution)/shard_map/ppermute | solution.py:500
  60.1 1.1 %collective-permute-start.2 = (bf16[128,512]{1,0:T(8,128)(2,1)S(1)}, bf16[128,512]{1,0:T(8,128)(2,1)S(1)}, u32[]{:S(2)}, u32[]{:S(2)}) collective-permute-start(bf16[128,512]{1,0:T(8,128)(2,1)S(1)} %get-tuple-element.30), channel_id=1, source_target_pairs={{0,192},{64,0},{128,64},{192,128},{1,193},{65,1},{129,65},{193,129... | collective-permute-start | bytes 393224 | tf_op jit(solution)/shard_map/ppermute | solution.py:500
  61.2 1.4 %collective-permute-done.r1 = bf16[128,512]{1,0:T(8,128)(2,1)S(1)} collective-permute-done((bf16[128,512]{1,0:T(8,128)(2,1)S(1)}, bf16[128,512]{1,0:T(8,128)(2,1)S(1)}, u32[]{:S(2)}, u32[]{:S(2)}) %collective-permute-start) | collective-permute-done | bytes 131104 | tf_op jit(solution)/shard_map/ppermute | solution.py:500
  62.6 7.2 %collective-permute-done.1.r2 = bf16[128,512]{1,0:T(8,128)(2,1)S(1)} collective-permute-done((bf16[128,512]{1,0:T(8,128)(2,1)S(1)}, bf16[128,512]{1,0:T(8,128)(2,1)S(1)}, u32[]{:S(2)}, u32[]{:S(2)}) %collective-permute-start.1) | collective-permute-done | bytes 131104 | tf_op jit(solution)/shard_map/ppermute | solution.py:500
  69.8 0.0 collective-permute-done.2.r3
  69.8 3.5 %all-to-all-done.1 = bf16[256,8,128]{2,1,0:T(8,128)(2,1)S(1)} async-done(((bf16[256,8,128]{2,1,0:T(8,128)(2,1)}), bf16[256,8,128]{2,1,0:T(8,128)(2,1)S(1)}, u32[]{:S(2)}, u32[]{:S(2)}) %all-to-all-start.1) | async-done | bytes 524320 | tf_op jit(solution)/shard_map/all_to_all | solution.py:519
  73.3 0.7 join_parts.1
  74.0 0.7 collective-permute-start.5
  74.8 1.4 %collective-permute-start.4 = (bf16[112,512]{1,0:T(8,128)(2,1)S(1)}, bf16[112,512]{1,0:T(8,128)(2,1)S(1)}, u32[]{:S(2)}, u32[]{:S(2)}) collective-permute-start(bf16[112,512]{1,0:T(8,128)(2,1)S(1)} %get-tuple-element.32.c0), channel_id=1, source_target_pairs={{0,128},{64,192},{128,0},{192,64},{1,129},{65,193},{129,1},{193,65... | collective-permute-start | bytes 344072 | tf_op jit(solution)/shard_map/ppermute | solution.py:500
  76.2 0.0 collective-permute-start.3
  76.2 2.2 %collective-permute-done.5.c3 = bf16[112,512]{1,0:T(8,128)(2,1)S(1)} collective-permute-done((bf16[112,512]{1,0:T(8,128)(2,1)S(1)}, bf16[112,512]{1,0:T(8,128)(2,1)S(1)}, u32[]{:S(2)}, u32[]{:S(2)}) %collective-permute-start.5) | collective-permute-done | bytes 114720 | tf_op jit(solution)/shard_map/ppermute | solution.py:500
  78.4 1.9 %collective-permute-done.4.c2 = bf16[112,512]{1,0:T(8,128)(2,1)S(1)} collective-permute-done((bf16[112,512]{1,0:T(8,128)(2,1)S(1)}, bf16[112,512]{1,0:T(8,128)(2,1)S(1)}, u32[]{:S(2)}, u32[]{:S(2)}) %collective-permute-start.4) | collective-permute-done | bytes 114720 | tf_op jit(solution)/shard_map/ppermute | solution.py:500
  80.3 3.0 %collective-permute-done.3.c1 = bf16[112,512]{1,0:T(8,128)(2,1)S(1)} collective-permute-done((bf16[112,512]{1,0:T(8,128)(2,1)S(1)}, bf16[112,512]{1,0:T(8,128)(2,1)S(1)}, u32[]{:S(2)}, u32[]{:S(2)}) %collective-permute-start.3) | collective-permute-done | bytes 114720 | tf_op jit(solution)/shard_map/ppermute | solution.py:500
  83.2 1.0 %place_parts.1 = f32[441,512]{1,0:T(8,128)} custom-call(bf16[112,512]{1,0:T(8,128)(2,1)S(1)} %get-tuple-element.32.c0, bf16[112,512]{1,0:T(8,128)(2,1)S(1)} %collective-permute-done.3.c1, bf16[112,512]{1,0:T(8,128)(2,1)S(1)} %collective-permute-done.4.c2, bf16[112,512]{1,0:T(8,128)(2,1)S(1)} %collective-permute-done.5.c3), custom_call_target="tpu_custom_call" | custom-call | tf_op jit(solution)/shard_map/place_parts/pallas_call | solution.py:489
Async XLA Ops:
  2.8 30.3 %all-to-all-start = ((bf16[64,8,512]{2,1,0:T(8,128)(2,1)}), bf16[64,8,512]{2,1,0:T(8,128)(2,1)S(1)}, u32[]{:S(2)}, u32[]{:S(2)}) async-start(bf16[64,8,512]{2,1,0:T(8,128)(2,1)} %bitcast.14), calls=%async_computation | async-start | bytes 1048576 | tf_op jit(solution)/shard_map/all_to_all | solution.py:513
  15.8 1.1 %copy-start = (bf16[512,512]{1,0:T(8,128)(2,1)S(1)}, bf16[512,512]{1,0:T(8,128)(2,1)}, u32[]{:S(2)}) copy-start(bf16[512,512]{1,0:T(8,128)(2,1)} %pack_pairs.1.pack) | copy-start | bytes 1572868
  16.8 1.0 %copy-start.1 = (bf16[512,441]{0,1:T(8,128)(2,1)S(1)}, bf16[512,441]{0,1:T(8,128)(2,1)}, u32[]{:S(2)}) copy-start(bf16[512,441]{0,1:T(8,128)(2,1)} %param.11) | copy-start | bytes 1354756
  17.9 1.9 %copy-start.2 = (s32[3072,256]{1,0:T(8,128)S(1)}, s32[3072,256]{1,0:T(8,128)}, u32[]{:S(2)}) copy-start(s32[3072,256]{1,0:T(8,128)} %alignment.1) | copy-start | bytes 9437188
  19.8 13.3 %copy-start.3 = (f32[48,21]{0,1:T(8,128)S(1)}, f32[48,21]{0,1:T(8,128)}, u32[]{:S(2)}) copy-start(f32[48,21]{0,1:T(8,128)} %param.10) | copy-start | bytes 12100
  19.8 13.3 %copy-start.4 = (f32[256]{0:T(256)S(1)}, f32[256]{0:T(256)}, u32[]{:S(2)}) copy-start(f32[256]{0:T(256)} %param.9) | copy-start | bytes 3076
  41.9 31.4 %all-to-all-start.1 = ((bf16[256,8,128]{2,1,0:T(8,128)(2,1)}), bf16[256,8,128]{2,1,0:T(8,128)(2,1)S(1)}, u32[]{:S(2)}, u32[]{:S(2)}) async-start(bf16[256,8,128]{2,1,0:T(8,128)(2,1)} %bitcast.9), calls=%async_computation.1 | async-start | bytes 1048576 | tf_op jit(solution)/shard_map/all_to_all | solution.py:519
  56.2 6.4 %collective-permute-start = (bf16[128,512]{1,0:T(8,128)(2,1)S(1)}, bf16[128,512]{1,0:T(8,128)(2,1)S(1)}, u32[]{:S(2)}, u32[]{:S(2)}) collective-permute-start(bf16[128,512]{1,0:T(8,128)(2,1)S(1)} %get-tuple-element.28), channel_id=1, source_target_pairs={{0,64},{64,128},{128,192},{192,0},{1,65},{65,129},{129,193},{193,1... | collective-permute-start | bytes 393224 | tf_op jit(solution)/shard_map/ppermute | solution.py:500
  57.7 12.2 %collective-permute-start.1 = (bf16[128,512]{1,0:T(8,128)(2,1)S(1)}, bf16[128,512]{1,0:T(8,128)(2,1)S(1)}, u32[]{:S(2)}, u32[]{:S(2)}) collective-permute-start(bf16[128,512]{1,0:T(8,128)(2,1)S(1)} %get-tuple-element.29), channel_id=1, source_target_pairs={{0,128},{64,192},{128,0},{192,64},{1,129},{65,193},{129,1},{193,65... | collective-permute-start | bytes 393224 | tf_op jit(solution)/shard_map/ppermute | solution.py:500
  60.1 9.7 %collective-permute-start.2 = (bf16[128,512]{1,0:T(8,128)(2,1)S(1)}, bf16[128,512]{1,0:T(8,128)(2,1)S(1)}, u32[]{:S(2)}, u32[]{:S(2)}) collective-permute-start(bf16[128,512]{1,0:T(8,128)(2,1)S(1)} %get-tuple-element.30), channel_id=1, source_target_pairs={{0,192},{64,0},{128,64},{192,128},{1,193},{65,1},{129,65},{193,129... | collective-permute-start | bytes 393224 | tf_op jit(solution)/shard_map/ppermute | solution.py:500
  74.0 4.3 %collective-permute-start.5 = (bf16[112,512]{1,0:T(8,128)(2,1)S(1)}, bf16[112,512]{1,0:T(8,128)(2,1)S(1)}, u32[]{:S(2)}, u32[]{:S(2)}) collective-permute-start(bf16[112,512]{1,0:T(8,128)(2,1)S(1)} %get-tuple-element.32.c0), channel_id=1, source_target_pairs={{0,192},{64,0},{128,64},{192,128},{1,193},{65,1},{129,65},{193,129... | collective-permute-start | bytes 344072 | tf_op jit(solution)/shard_map/ppermute | solution.py:500
  74.8 5.5 %collective-permute-start.4 = (bf16[112,512]{1,0:T(8,128)(2,1)S(1)}, bf16[112,512]{1,0:T(8,128)(2,1)S(1)}, u32[]{:S(2)}, u32[]{:S(2)}) collective-permute-start(bf16[112,512]{1,0:T(8,128)(2,1)S(1)} %get-tuple-element.32.c0), channel_id=1, source_target_pairs={{0,128},{64,192},{128,0},{192,64},{1,129},{65,193},{129,1},{193,65... | collective-permute-start | bytes 344072 | tf_op jit(solution)/shard_map/ppermute | solution.py:500
  76.2 7.1 %collective-permute-start.3 = (bf16[112,512]{1,0:T(8,128)(2,1)S(1)}, bf16[112,512]{1,0:T(8,128)(2,1)S(1)}, u32[]{:S(2)}, u32[]{:S(2)}) collective-permute-start(bf16[112,512]{1,0:T(8,128)(2,1)S(1)} %get-tuple-element.32.c0), channel_id=1, source_target_pairs={{0,64},{64,128},{128,192},{192,0},{1,65},{65,129},{129,193},{193,1... | collective-permute-start | bytes 344072 | tf_op jit(solution)/shard_map/ppermute | solution.py:500

commit v6 on v5

--- a/solution.py
+++ b/solution.py
@@ -125,9 +125,10 @@
 
 
 def fill_hot(far, j, hot):
-    tile = far[pl.ds(pl.multiple_of(j * SPAN, SPAN), SPAN), :].astype(F32)
+    tile = far[pl.ds(pl.multiple_of(j * SPAN, SPAN), SPAN), :].astype(BF16)
+    one, none = jnp.ones_like(tile), jnp.zeros_like(tile)
     for c in range(2 * DUOS):
-        hot[j, c * SPAN : (c + 1) * SPAN, :] = jnp.where(tile == float(c), 1.0, 0.0).astype(BF16)
+        hot[j, c * SPAN : (c + 1) * SPAN, :] = jnp.where(tile == jnp.array(c, BF16), one, none)
 
 
 def halves(first, second):

time: 84.6 us -> 84.6 us (level)
  transfers between devices with their start and end apart: 8 -> 8, of which waited for: 7 -> 7; matrix products, arithmetic and copies ran while one was open for 0% -> 0% of each run, Pallas kernels for 11% -> 12%
where the time goes in v6:
time: 84.6 us; the launch traced here: 83.8 us
  starting transfers between devices  29.8 us (35%)
  waiting for transfers between devices  27.1 us (32%)
  Pallas kernels  22.3 us (26%)
  local copies, waits for them, and re-layouts  3.98 us (5%)
    ppermute x6, waiting for transfers between devices, shifted(): return lax.ppermute(array, 'seq', [(i, (i + k) % 4) for i in range(4)])  16.4 us
    all_to_all x1, starting transfers between devices, swap_blocks(): lax.all_to_all(blocks, 'res', split_axis=0, concat_axis=0, tiled=True)  13 us
    all_to_all x1, starting transfers between devices, swap_quarters(): lax.all_to_all(blocks, ('seq', 'res'), split_axis=0, concat_axis=0, tiled...  9.61 us
    pallas_call x1, Pallas kernels, recv_half(): pl.pallas_call(recv_kernel, out_shape=(jax.ShapeDtypeStruct((4, PAIRS, TI...  8.7 us
    all_to_all x1, waiting for transfers between devices, swap_blocks(): lax.all_to_all(blocks, 'res', split_axis=0, concat_axis=0, tiled=True)  8.01 us
    ppermute x6, starting transfers between devices, shifted(): return lax.ppermute(array, 'seq', [(i, (i + k) % 4) for i in range(4)])  7.18 us
    pallas_call x1, Pallas kernels, own_field(): pl.pallas_call(own_field_kernel, out_shape=(jax.ShapeDtypeStruct((RES, SE...  5.32 us
    pallas_call x1, Pallas kernels, own_grad(): pl.pallas_call(own_grad_kernel, out_shape=(jax.ShapeDtypeStruct((TILE, PA...  4.35 us
  transfers between devices with their start and end apart: 8, of which 7 were waited for; matrix products, arithmetic and copies ran while one was open for 0% of the time, Pallas kernels for 12%

profile of v6, /device:TPU:1, one launch (start us, length us, event | category | flops | bytes accessed | tf_op | source)
XLA Modules:
  0.0 83.8 jit_solution(16305106785269872757)
XLA Ops:
  0.6 2.1 %pack_pairs.1.pack = bf16[512,512]{1,0:T(8,128)(2,1)} custom-call(bf16[441,512]{1,0:T(8,128)(2,1)} %bitcast.16, s32[1,512]{1,0:T(1,128)} %bitcast.21, s32[1,512]{1,0:T(1,128)} %bitcast.22, s32[1,256]{1,0:T(1,128)} %bitcast.23, s32[1,64]{1,0:T(1,128)} %bitcast.24), custom_call_target="tpu_custom_call" | custom-call | tf_op jit(solution)/shard_map/pack_pairs/pallas_call | solution.py:77
  2.8 13.0 %all-to-all-start = ((bf16[64,8,512]{2,1,0:T(8,128)(2,1)}), bf16[64,8,512]{2,1,0:T(8,128)(2,1)S(1)}, u32[]{:S(2)}, u32[]{:S(2)}) async-start(bf16[64,8,512]{2,1,0:T(8,128)(2,1)} %bitcast.14), calls=%async_computation | async-start | bytes 1048576 | tf_op jit(solution)/shard_map/all_to_all | solution.py:514
  15.8 0.0 copy-start
  15.8 1.1 %copy-done = bf16[512,512]{1,0:T(8,128)(2,1)S(1)} copy-done((bf16[512,512]{1,0:T(8,128)(2,1)S(1)}, bf16[512,512]{1,0:T(8,128)(2,1)}, u32[]{:S(2)}) %copy-start) | copy-done | bytes 524312
  16.8 0.0 copy-start.1
  16.8 1.0 %copy-done.1 = bf16[512,441]{0,1:T(8,128)(2,1)S(1)} copy-done((bf16[512,441]{0,1:T(8,128)(2,1)S(1)}, bf16[512,441]{0,1:T(8,128)(2,1)}, u32[]{:S(2)}) %copy-start.1) | copy-done | bytes 451608
  17.9 0.0 copy-start.2
  17.9 1.9 %copy-done.2 = s32[3072,256]{1,0:T(8,128)S(1)} copy-done((s32[3072,256]{1,0:T(8,128)S(1)}, s32[3072,256]{1,0:T(8,128)}, u32[]{:S(2)}) %copy-start.2) | copy-done | bytes 3145752
  19.8 0.0 copy-start.3
  19.8 0.0 copy-start.4
  19.8 5.3 %own_field.1 = (s8[3072,256]{1,0:T(32,128)(4,1)S(1)}, bf16[48,256]{1,0:T(8,128)(2,1)S(1)}, s8[512,256]{1,0:T(32,128)(4,1)S(1)}, f32[8,512]{1,0:T(8,128)S(1)}, f3...) custom-call(s32[3072,256]{1,0:T(8,128)S(1)} %copy-done.2, bf16[512,512]{1,0:T(8,128)(2,1)S(1)} %copy-done, ...), custom_call_target="tpu_custom_call" | custom-call | flops 10000000000 | bytes 10000000 | tf_op jit(solution)/shard_map/own_field/pallas_call | solution.py:274
  25.1 8.0 %all-to-all-done = bf16[64,8,512]{2,1,0:T(8,128)(2,1)S(1)} async-done(((bf16[64,8,512]{2,1,0:T(8,128)(2,1)}), bf16[64,8,512]{2,1,0:T(8,128)(2,1)S(1)}, u32[]{:S(2)}, u32[]{:S(2)}) %all-to-all-start) | async-done | bytes 524320 | tf_op jit(solution)/shard_map/all_to_all | solution.py:514
  33.1 0.0 copy-done.3
  33.1 0.0 copy-done.4
  33.1 8.7 %recv_half.1 = (bf16[4,512,128]{2,1,0:T(8,128)(2,1)}, bf16[1152,256]{1,0:T(8,128)(2,1)S(1)}, f32[24,128]{1,0:T(8,128)S(1)}) custom-call(bf16[512,512]{1,0:T(8,128)(2,1)S(1)} %bitcast.15, s8[3072,256]{1,0:T(32,128)(4,1)S(1)} %get-tuple-element.22.states, bf16[48,256]{1,0:T(8,128)(2,1)S(1)} %get-tuple-element.23.codes, f32[1152,256]{1,0:T(8,128)S(1)} %get-tuple-element.24.own, ...), custom_call_target="tpu_custom_call" | custom-call | flops 20000000000 | bytes 10000000 | tf_op jit(solution)/shard_map/recv_half/pallas_call | solution.py:371
  41.8 9.6 %all-to-all-start.1 = ((bf16[256,8,128]{2,1,0:T(8,128)(2,1)}), bf16[256,8,128]{2,1,0:T(8,128)(2,1)S(1)}, u32[]{:S(2)}, u32[]{:S(2)}) async-start(bf16[256,8,128]{2,1,0:T(8,128)(2,1)} %bitcast.9), calls=%async_computation.1 | async-start | bytes 1048576 | tf_op jit(solution)/shard_map/all_to_all | solution.py:520
  51.4 4.3 %own_grad.1 = (bf16[128,512]{1,0:T(8,128)(2,1)S(1)}, bf16[128,512]{1,0:T(8,128)(2,1)S(1)}, bf16[128,512]{1,0:T(8,128)(2,1)S(1)}, bf16[128,512]{1,0:T(8,128)(2,1)S(1)}) custom-call(f32[8,8,128]{2,1,0:T(8,128)S(1)} %get-tuple-element.18.keys_ref, s32[2,8]{1,0:T(2,128)S(1)} %get-tuple-element.19.bounds, f32[8,512]{1,0:T(8,128)S(1)} %get-tuple-element.20.place, ...), custom_call_target="tpu_custom_call" | custom-call | flops 6000000000 | bytes 8000000 | tf_op jit(solution)/shard_map/own_grad/pallas_call | solution.py:425
  55.8 1.5 %collective-permute-start = (bf16[128,512]{1,0:T(8,128)(2,1)S(1)}, bf16[128,512]{1,0:T(8,128)(2,1)S(1)}, u32[]{:S(2)}, u32[]{:S(2)}) collective-permute-start(bf16[128,512]{1,0:T(8,128)(2,1)S(1)} %get-tuple-element.28), channel_id=1, source_target_pairs={{0,64},{64,128},{128,192},{192,0},{1,65},{65,129},{129,193},{193,1... | collective-permute-start | bytes 393224 | tf_op jit(solution)/shard_map/ppermute | solution.py:501
  57.2 2.4 %collective-permute-start.1 = (bf16[128,512]{1,0:T(8,128)(2,1)S(1)}, bf16[128,512]{1,0:T(8,128)(2,1)S(1)}, u32[]{:S(2)}, u32[]{:S(2)}) collective-permute-start(bf16[128,512]{1,0:T(8,128)(2,1)S(1)} %get-tuple-element.29), channel_id=1, source_target_pairs={{0,128},{64,192},{128,0},{192,64},{1,129},{65,193},{129,1},{193,65... | collective-permute-start | bytes 393224 | tf_op jit(solution)/shard_map/ppermute | solution.py:501
  59.7 1.1 %collective-permute-start.2 = (bf16[128,512]{1,0:T(8,128)(2,1)S(1)}, bf16[128,512]{1,0:T(8,128)(2,1)S(1)}, u32[]{:S(2)}, u32[]{:S(2)}) collective-permute-start(bf16[128,512]{1,0:T(8,128)(2,1)S(1)} %get-tuple-element.30), channel_id=1, source_target_pairs={{0,192},{64,0},{128,64},{192,128},{1,193},{65,1},{129,65},{193,129... | collective-permute-start | bytes 393224 | tf_op jit(solution)/shard_map/ppermute | solution.py:501
  60.8 2.0 %collective-permute-done.r1 = bf16[128,512]{1,0:T(8,128)(2,1)S(1)} collective-permute-done((bf16[128,512]{1,0:T(8,128)(2,1)S(1)}, bf16[128,512]{1,0:T(8,128)(2,1)S(1)}, u32[]{:S(2)}, u32[]{:S(2)}) %collective-permute-start) | collective-permute-done | bytes 131104 | tf_op jit(solution)/shard_map/ppermute | solution.py:501
  62.8 7.4 %collective-permute-done.1.r2 = bf16[128,512]{1,0:T(8,128)(2,1)S(1)} collective-permute-done((bf16[128,512]{1,0:T(8,128)(2,1)S(1)}, bf16[128,512]{1,0:T(8,128)(2,1)S(1)}, u32[]{:S(2)}, u32[]{:S(2)}) %collective-permute-start.1) | collective-permute-done | bytes 131104 | tf_op jit(solution)/shard_map/ppermute | solution.py:501
  70.1 0.0 collective-permute-done.2.r3
  70.1 2.7 %all-to-all-done.1 = bf16[256,8,128]{2,1,0:T(8,128)(2,1)S(1)} async-done(((bf16[256,8,128]{2,1,0:T(8,128)(2,1)}), bf16[256,8,128]{2,1,0:T(8,128)(2,1)S(1)}, u32[]{:S(2)}, u32[]{:S(2)}) %all-to-all-start.1) | async-done | bytes 524320 | tf_op jit(solution)/shard_map/all_to_all | solution.py:520
  72.8 0.7 join_parts.1
  73.6 0.7 collective-permute-start.5
  74.3 1.4 %collective-permute-start.4 = (bf16[112,512]{1,0:T(8,128)(2,1)S(1)}, bf16[112,512]{1,0:T(8,128)(2,1)S(1)}, u32[]{:S(2)}, u32[]{:S(2)}) collective-permute-start(bf16[112,512]{1,0:T(8,128)(2,1)S(1)} %get-tuple-element.32.c0), channel_id=1, source_target_pairs={{0,128},{64,192},{128,0},{192,64},{1,129},{65,193},{129,1},{193,65... | collective-permute-start | bytes 344072 | tf_op jit(solution)/shard_map/ppermute | solution.py:501
  75.7 0.0 collective-permute-start.3
  75.7 2.2 %collective-permute-done.5.c3 = bf16[112,512]{1,0:T(8,128)(2,1)S(1)} collective-permute-done((bf16[112,512]{1,0:T(8,128)(2,1)S(1)}, bf16[112,512]{1,0:T(8,128)(2,1)S(1)}, u32[]{:S(2)}, u32[]{:S(2)}) %collective-permute-start.5) | collective-permute-done | bytes 114720 | tf_op jit(solution)/shard_map/ppermute | solution.py:501
  77.9 1.9 %collective-permute-done.4.c2 = bf16[112,512]{1,0:T(8,128)(2,1)S(1)} collective-permute-done((bf16[112,512]{1,0:T(8,128)(2,1)S(1)}, bf16[112,512]{1,0:T(8,128)(2,1)S(1)}, u32[]{:S(2)}, u32[]{:S(2)}) %collective-permute-start.4) | collective-permute-done | bytes 114720 | tf_op jit(solution)/shard_map/ppermute | solution.py:501
  79.8 3.0 %collective-permute-done.3.c1 = bf16[112,512]{1,0:T(8,128)(2,1)S(1)} collective-permute-done((bf16[112,512]{1,0:T(8,128)(2,1)S(1)}, bf16[112,512]{1,0:T(8,128)(2,1)S(1)}, u32[]{:S(2)}, u32[]{:S(2)}) %collective-permute-start.3) | collective-permute-done | bytes 114720 | tf_op jit(solution)/shard_map/ppermute | solution.py:501
  82.8 1.0 %place_parts.1 = f32[441,512]{1,0:T(8,128)} custom-call(bf16[112,512]{1,0:T(8,128)(2,1)S(1)} %get-tuple-element.32.c0, bf16[112,512]{1,0:T(8,128)(2,1)S(1)} %collective-permute-done.3.c1, bf16[112,512]{1,0:T(8,128)(2,1)S(1)} %collective-permute-done.4.c2, bf16[112,512]{1,0:T(8,128)(2,1)S(1)} %collective-permute-done.5.c3), custom_call_target="tpu_custom_call" | custom-call | tf_op jit(solution)/shard_map/place_parts/pallas_call | solution.py:490
Async XLA Ops:
  2.8 30.3 %all-to-all-start = ((bf16[64,8,512]{2,1,0:T(8,128)(2,1)}), bf16[64,8,512]{2,1,0:T(8,128)(2,1)S(1)}, u32[]{:S(2)}, u32[]{:S(2)}) async-start(bf16[64,8,512]{2,1,0:T(8,128)(2,1)} %bitcast.14), calls=%async_computation | async-start | bytes 1048576 | tf_op jit(solution)/shard_map/all_to_all | solution.py:514
  15.8 1.1 %copy-start = (bf16[512,512]{1,0:T(8,128)(2,1)S(1)}, bf16[512,512]{1,0:T(8,128)(2,1)}, u32[]{:S(2)}) copy-start(bf16[512,512]{1,0:T(8,128)(2,1)} %pack_pairs.1.pack) | copy-start | bytes 1572868
  16.8 1.0 %copy-start.1 = (bf16[512,441]{0,1:T(8,128)(2,1)S(1)}, bf16[512,441]{0,1:T(8,128)(2,1)}, u32[]{:S(2)}) copy-start(bf16[512,441]{0,1:T(8,128)(2,1)} %param.11) | copy-start | bytes 1354756
  17.9 1.9 %copy-start.2 = (s32[3072,256]{1,0:T(8,128)S(1)}, s32[3072,256]{1,0:T(8,128)}, u32[]{:S(2)}) copy-start(s32[3072,256]{1,0:T(8,128)} %alignment.1) | copy-start | bytes 9437188
  19.8 13.3 %copy-start.3 = (f32[48,21]{0,1:T(8,128)S(1)}, f32[48,21]{0,1:T(8,128)}, u32[]{:S(2)}) copy-start(f32[48,21]{0,1:T(8,128)} %param.10) | copy-start | bytes 12100
  19.8 13.3 %copy-start.4 = (f32[256]{0:T(256)S(1)}, f32[256]{0:T(256)}, u32[]{:S(2)}) copy-start(f32[256]{0:T(256)} %param.9) | copy-start | bytes 3076
  41.8 31.0 %all-to-all-start.1 = ((bf16[256,8,128]{2,1,0:T(8,128)(2,1)}), bf16[256,8,128]{2,1,0:T(8,128)(2,1)S(1)}, u32[]{:S(2)}, u32[]{:S(2)}) async-start(bf16[256,8,128]{2,1,0:T(8,128)(2,1)} %bitcast.9), calls=%async_computation.1 | async-start | bytes 1048576 | tf_op jit(solution)/shard_map/all_to_all | solution.py:520
  55.8 7.0 %collective-permute-start = (bf16[128,512]{1,0:T(8,128)(2,1)S(1)}, bf16[128,512]{1,0:T(8,128)(2,1)S(1)}, u32[]{:S(2)}, u32[]{:S(2)}) collective-permute-start(bf16[128,512]{1,0:T(8,128)(2,1)S(1)} %get-tuple-element.28), channel_id=1, source_target_pairs={{0,64},{64,128},{128,192},{192,0},{1,65},{65,129},{129,193},{193,1... | collective-permute-start | bytes 393224 | tf_op jit(solution)/shard_map/ppermute | solution.py:501
  57.2 12.9 %collective-permute-start.1 = (bf16[128,512]{1,0:T(8,128)(2,1)S(1)}, bf16[128,512]{1,0:T(8,128)(2,1)S(1)}, u32[]{:S(2)}, u32[]{:S(2)}) collective-permute-start(bf16[128,512]{1,0:T(8,128)(2,1)S(1)} %get-tuple-element.29), channel_id=1, source_target_pairs={{0,128},{64,192},{128,0},{192,64},{1,129},{65,193},{129,1},{193,65... | collective-permute-start | bytes 393224 | tf_op jit(solution)/shard_map/ppermute | solution.py:501
  59.7 10.4 %collective-permute-start.2 = (bf16[128,512]{1,0:T(8,128)(2,1)S(1)}, bf16[128,512]{1,0:T(8,128)(2,1)S(1)}, u32[]{:S(2)}, u32[]{:S(2)}) collective-permute-start(bf16[128,512]{1,0:T(8,128)(2,1)S(1)} %get-tuple-element.30), channel_id=1, source_target_pairs={{0,192},{64,0},{128,64},{192,128},{1,193},{65,1},{129,65},{193,129... | collective-permute-start | bytes 393224 | tf_op jit(solution)/shard_map/ppermute | solution.py:501
  73.6 4.3 %collective-permute-start.5 = (bf16[112,512]{1,0:T(8,128)(2,1)S(1)}, bf16[112,512]{1,0:T(8,128)(2,1)S(1)}, u32[]{:S(2)}, u32[]{:S(2)}) collective-permute-start(bf16[112,512]{1,0:T(8,128)(2,1)S(1)} %get-tuple-element.32.c0), channel_id=1, source_target_pairs={{0,192},{64,0},{128,64},{192,128},{1,193},{65,1},{129,65},{193,129... | collective-permute-start | bytes 344072 | tf_op jit(solution)/shard_map/ppermute | solution.py:501
  74.3 5.5 %collective-permute-start.4 = (bf16[112,512]{1,0:T(8,128)(2,1)S(1)}, bf16[112,512]{1,0:T(8,128)(2,1)S(1)}, u32[]{:S(2)}, u32[]{:S(2)}) collective-permute-start(bf16[112,512]{1,0:T(8,128)(2,1)S(1)} %get-tuple-element.32.c0), channel_id=1, source_target_pairs={{0,128},{64,192},{128,0},{192,64},{1,129},{65,193},{129,1},{193,65... | collective-permute-start | bytes 344072 | tf_op jit(solution)/shard_map/ppermute | solution.py:501
  75.7 7.1 %collective-permute-start.3 = (bf16[112,512]{1,0:T(8,128)(2,1)S(1)}, bf16[112,512]{1,0:T(8,128)(2,1)S(1)}, u32[]{:S(2)}, u32[]{:S(2)}) collective-permute-start(bf16[112,512]{1,0:T(8,128)(2,1)S(1)} %get-tuple-element.32.c0), channel_id=1, source_target_pairs={{0,64},{64,128},{128,192},{192,0},{1,65},{65,129},{129,193},{193,1... | collective-permute-start | bytes 344072 | tf_op jit(solution)/shard_map/ppermute | solution.py:501

commit v7 on v6

--- a/solution.py
+++ b/solution.py
@@ -118,8 +118,9 @@
         pairs = slice(start * CAP, (start + blocks) * CAP)
         base = start * RL
         depth = min(256, RES - base)
-        lane = iota((blocks * CAP, depth), 1).astype(F32)
-        pick = jnp.where(far[pairs] - float(base) == lane, 1.0, 0.0).astype(BF16)
+        lane = iota((blocks * CAP, depth), 1).astype(F32).astype(BF16)
+        wanted = jnp.broadcast_to(far[pairs] - float(base), lane.shape).astype(BF16)
+        pick = jnp.where(wanted == lane, jnp.ones_like(lane), jnp.zeros_like(lane))
         plain[pairs, :] = dot(pick, states[base : base + depth, :].astype(BF16))
     return dot(to_plain, plain[...].astype(BF16))
 

time: 84.6 us -> 84.5 us (level)
  Pallas kernels: 22.3 us -> 20.7 us
  waiting for transfers between devices: 27.1 us -> 28.6 us
    all_to_all x1, waiting for transfers between devices: 2.71 us -> 3.77 us  [swap_quarters(): lax.all_to_all(blocks, ('seq', 'res'), split_axis=0, concat_axis=0, tiled...]
  transfers between devices with their start and end apart: 8 -> 8, of which waited for: 7 -> 7; matrix products, arithmetic and copies ran while one was open for 0% -> 0% of each run, Pallas kernels for 12% -> 10%
where the time goes in v7:
time: 84.5 us; the launch traced here: 84.2 us
  starting transfers between devices  30.2 us (36%)
  waiting for transfers between devices  28.6 us (34%)
  Pallas kernels  20.7 us (24%)
  local copies, waits for them, and re-layouts  3.98 us (5%)
    ppermute x6, waiting for transfers between devices, shifted(): return lax.ppermute(array, 'seq', [(i, (i + k) % 4) for i in range(4)])  16 us
    all_to_all x1, starting transfers between devices, swap_blocks(): lax.all_to_all(blocks, 'res', split_axis=0, concat_axis=0, tiled=True)  13 us
    all_to_all x1, starting transfers between devices, swap_quarters(): lax.all_to_all(blocks, ('seq', 'res'), split_axis=0, concat_axis=0, tiled...  10.1 us
    all_to_all x1, waiting for transfers between devices, swap_blocks(): lax.all_to_all(blocks, 'res', split_axis=0, concat_axis=0, tiled=True)  8.78 us
    pallas_call x1, Pallas kernels, recv_half(): pl.pallas_call(recv_kernel, out_shape=(jax.ShapeDtypeStruct((4, PAIRS, TI...  8.68 us
    ppermute x6, starting transfers between devices, shifted(): return lax.ppermute(array, 'seq', [(i, (i + k) % 4) for i in range(4)])  7.19 us
    pallas_call x1, Pallas kernels, own_field(): pl.pallas_call(own_field_kernel, out_shape=(jax.ShapeDtypeStruct((RES, SE...  4.55 us
    unnamed x10, local copies, waits for them, and re-layouts  3.98 us
  transfers between devices with their start and end apart: 8, of which 7 were waited for; matrix products, arithmetic and copies ran while one was open for 0% of the time, Pallas kernels for 10%

profile of v7, /device:TPU:1, one launch (start us, length us, event | category | flops | bytes accessed | tf_op | source)
XLA Modules:
  0.0 84.2 jit_solution(1491562777353443253)
XLA Ops:
  0.6 2.1 %pack_pairs.1.pack = bf16[512,512]{1,0:T(8,128)(2,1)} custom-call(bf16[441,512]{1,0:T(8,128)(2,1)} %bitcast.16, s32[1,512]{1,0:T(1,128)} %bitcast.21, s32[1,512]{1,0:T(1,128)} %bitcast.22, s32[1,256]{1,0:T(1,128)} %bitcast.23, s32[1,64]{1,0:T(1,128)} %bitcast.24), custom_call_target="tpu_custom_call" | custom-call | tf_op jit(solution)/shard_map/pack_pairs/pallas_call | solution.py:77
  2.8 13.0 %all-to-all-start = ((bf16[64,8,512]{2,1,0:T(8,128)(2,1)}), bf16[64,8,512]{2,1,0:T(8,128)(2,1)S(1)}, u32[]{:S(2)}, u32[]{:S(2)}) async-start(bf16[64,8,512]{2,1,0:T(8,128)(2,1)} %bitcast.14), calls=%async_computation | async-start | bytes 1048576 | tf_op jit(solution)/shard_map/all_to_all | solution.py:515
  15.8 0.0 copy-start
  15.8 1.1 %copy-done = bf16[512,512]{1,0:T(8,128)(2,1)S(1)} copy-done((bf16[512,512]{1,0:T(8,128)(2,1)S(1)}, bf16[512,512]{1,0:T(8,128)(2,1)}, u32[]{:S(2)}) %copy-start) | copy-done | bytes 524312
  16.8 0.0 copy-start.1
  16.8 1.0 %copy-done.1 = bf16[512,441]{0,1:T(8,128)(2,1)S(1)} copy-done((bf16[512,441]{0,1:T(8,128)(2,1)S(1)}, bf16[512,441]{0,1:T(8,128)(2,1)}, u32[]{:S(2)}) %copy-start.1) | copy-done | bytes 451608
  17.9 0.0 copy-start.2
  17.9 1.9 %copy-done.2 = s32[3072,256]{1,0:T(8,128)S(1)} copy-done((s32[3072,256]{1,0:T(8,128)S(1)}, s32[3072,256]{1,0:T(8,128)}, u32[]{:S(2)}) %copy-start.2) | copy-done | bytes 3145752
  19.8 0.0 copy-start.3
  19.8 0.0 copy-start.4
  19.8 4.5 %own_field.1 = (s8[3072,256]{1,0:T(32,128)(4,1)S(1)}, bf16[48,256]{1,0:T(8,128)(2,1)S(1)}, s8[512,256]{1,0:T(32,128)(4,1)S(1)}, f32[8,512]{1,0:T(8,128)S(1)}, f3...) custom-call(s32[3072,256]{1,0:T(8,128)S(1)} %copy-done.2, bf16[512,512]{1,0:T(8,128)(2,1)S(1)} %copy-done, ...), custom_call_target="tpu_custom_call" | custom-call | flops 10000000000 | bytes 10000000 | tf_op jit(solution)/shard_map/own_field/pallas_call | solution.py:275
  24.3 8.8 %all-to-all-done = bf16[64,8,512]{2,1,0:T(8,128)(2,1)S(1)} async-done(((bf16[64,8,512]{2,1,0:T(8,128)(2,1)}), bf16[64,8,512]{2,1,0:T(8,128)(2,1)S(1)}, u32[]{:S(2)}, u32[]{:S(2)}) %all-to-all-start) | async-done | bytes 524320 | tf_op jit(solution)/shard_map/all_to_all | solution.py:515
  33.1 0.0 copy-done.3
  33.1 0.0 copy-done.4
  33.1 8.7 %recv_half.1 = (bf16[4,512,128]{2,1,0:T(8,128)(2,1)}, bf16[1152,256]{1,0:T(8,128)(2,1)S(1)}, f32[24,128]{1,0:T(8,128)S(1)}) custom-call(bf16[512,512]{1,0:T(8,128)(2,1)S(1)} %bitcast.15, s8[3072,256]{1,0:T(32,128)(4,1)S(1)} %get-tuple-element.22.states, bf16[48,256]{1,0:T(8,128)(2,1)S(1)} %get-tuple-element.23.codes, f32[1152,256]{1,0:T(8,128)S(1)} %get-tuple-element.24.own, ...), custom_call_target="tpu_custom_call" | custom-call | flops 20000000000 | bytes 10000000 | tf_op jit(solution)/shard_map/recv_half/pallas_call | solution.py:372
  41.8 10.1 %all-to-all-start.1 = ((bf16[256,8,128]{2,1,0:T(8,128)(2,1)}), bf16[256,8,128]{2,1,0:T(8,128)(2,1)S(1)}, u32[]{:S(2)}, u32[]{:S(2)}) async-start(bf16[256,8,128]{2,1,0:T(8,128)(2,1)} %bitcast.9), calls=%async_computation.1 | async-start | bytes 1048576 | tf_op jit(solution)/shard_map/all_to_all | solution.py:521
  51.9 3.6 %own_grad.1 = (bf16[128,512]{1,0:T(8,128)(2,1)S(1)}, bf16[128,512]{1,0:T(8,128)(2,1)S(1)}, bf16[128,512]{1,0:T(8,128)(2,1)S(1)}, bf16[128,512]{1,0:T(8,128)(2,1)S(1)}) custom-call(f32[8,8,128]{2,1,0:T(8,128)S(1)} %get-tuple-element.18.keys_ref, s32[2,8]{1,0:T(2,128)S(1)} %get-tuple-element.19.bounds, f32[8,512]{1,0:T(8,128)S(1)} %get-tuple-element.20.place, ...), custom_call_target="tpu_custom_call" | custom-call | flops 6000000000 | bytes 8000000 | tf_op jit(solution)/shard_map/own_grad/pallas_call | solution.py:426
  55.5 1.5 %collective-permute-start = (bf16[128,512]{1,0:T(8,128)(2,1)S(1)}, bf16[128,512]{1,0:T(8,128)(2,1)S(1)}, u32[]{:S(2)}, u32[]{:S(2)}) collective-permute-start(bf16[128,512]{1,0:T(8,128)(2,1)S(1)} %get-tuple-element.28), channel_id=1, source_target_pairs={{0,64},{64,128},{128,192},{192,0},{1,65},{65,129},{129,193},{193,1... | collective-permute-start | bytes 393224 | tf_op jit(solution)/shard_map/ppermute | solution.py:502
  57.0 2.4 %collective-permute-start.1 = (bf16[128,512]{1,0:T(8,128)(2,1)S(1)}, bf16[128,512]{1,0:T(8,128)(2,1)S(1)}, u32[]{:S(2)}, u32[]{:S(2)}) collective-permute-start(bf16[128,512]{1,0:T(8,128)(2,1)S(1)} %get-tuple-element.29), channel_id=1, source_target_pairs={{0,128},{64,192},{128,0},{192,64},{1,129},{65,193},{129,1},{193,65... | collective-permute-start | bytes 393224 | tf_op jit(solution)/shard_map/ppermute | solution.py:502
  59.4 1.1 %collective-permute-start.2 = (bf16[128,512]{1,0:T(8,128)(2,1)S(1)}, bf16[128,512]{1,0:T(8,128)(2,1)S(1)}, u32[]{:S(2)}, u32[]{:S(2)}) collective-permute-start(bf16[128,512]{1,0:T(8,128)(2,1)S(1)} %get-tuple-element.30), channel_id=1, source_target_pairs={{0,192},{64,0},{128,64},{192,128},{1,193},{65,1},{129,65},{193,129... | collective-permute-start | bytes 393224 | tf_op jit(solution)/shard_map/ppermute | solution.py:502
  60.5 1.1 %collective-permute-done.r1 = bf16[128,512]{1,0:T(8,128)(2,1)S(1)} collective-permute-done((bf16[128,512]{1,0:T(8,128)(2,1)S(1)}, bf16[128,512]{1,0:T(8,128)(2,1)S(1)}, u32[]{:S(2)}, u32[]{:S(2)}) %collective-permute-start) | collective-permute-done | bytes 131104 | tf_op jit(solution)/shard_map/ppermute | solution.py:502
  61.7 7.8 %collective-permute-done.1.r2 = bf16[128,512]{1,0:T(8,128)(2,1)S(1)} collective-permute-done((bf16[128,512]{1,0:T(8,128)(2,1)S(1)}, bf16[128,512]{1,0:T(8,128)(2,1)S(1)}, u32[]{:S(2)}, u32[]{:S(2)}) %collective-permute-start.1) | collective-permute-done | bytes 131104 | tf_op jit(solution)/shard_map/ppermute | solution.py:502
  69.5 0.0 collective-permute-done.2.r3
  69.5 3.8 %all-to-all-done.1 = bf16[256,8,128]{2,1,0:T(8,128)(2,1)S(1)} async-done(((bf16[256,8,128]{2,1,0:T(8,128)(2,1)}), bf16[256,8,128]{2,1,0:T(8,128)(2,1)S(1)}, u32[]{:S(2)}, u32[]{:S(2)}) %all-to-all-start.1) | async-done | bytes 524320 | tf_op jit(solution)/shard_map/all_to_all | solution.py:521
  73.3 0.7 join_parts.1
  74.0 0.7 collective-permute-start.5
  74.7 1.4 %collective-permute-start.4 = (bf16[112,512]{1,0:T(8,128)(2,1)S(1)}, bf16[112,512]{1,0:T(8,128)(2,1)S(1)}, u32[]{:S(2)}, u32[]{:S(2)}) collective-permute-start(bf16[112,512]{1,0:T(8,128)(2,1)S(1)} %get-tuple-element.32.c0), channel_id=1, source_target_pairs={{0,128},{64,192},{128,0},{192,64},{1,129},{65,193},{129,1},{193,65... | collective-permute-start | bytes 344072 | tf_op jit(solution)/shard_map/ppermute | solution.py:502
  76.2 0.0 collective-permute-start.3
  76.2 2.2 %collective-permute-done.5.c3 = bf16[112,512]{1,0:T(8,128)(2,1)S(1)} collective-permute-done((bf16[112,512]{1,0:T(8,128)(2,1)S(1)}, bf16[112,512]{1,0:T(8,128)(2,1)S(1)}, u32[]{:S(2)}, u32[]{:S(2)}) %collective-permute-start.5) | collective-permute-done | bytes 114720 | tf_op jit(solution)/shard_map/ppermute | solution.py:502
  78.3 1.9 %collective-permute-done.4.c2 = bf16[112,512]{1,0:T(8,128)(2,1)S(1)} collective-permute-done((bf16[112,512]{1,0:T(8,128)(2,1)S(1)}, bf16[112,512]{1,0:T(8,128)(2,1)S(1)}, u32[]{:S(2)}, u32[]{:S(2)}) %collective-permute-start.4) | collective-permute-done | bytes 114720 | tf_op jit(solution)/shard_map/ppermute | solution.py:502
  80.3 3.0 %collective-permute-done.3.c1 = bf16[112,512]{1,0:T(8,128)(2,1)S(1)} collective-permute-done((bf16[112,512]{1,0:T(8,128)(2,1)S(1)}, bf16[112,512]{1,0:T(8,128)(2,1)S(1)}, u32[]{:S(2)}, u32[]{:S(2)}) %collective-permute-start.3) | collective-permute-done | bytes 114720 | tf_op jit(solution)/shard_map/ppermute | solution.py:502
  83.2 1.0 %place_parts.1 = f32[441,512]{1,0:T(8,128)} custom-call(bf16[112,512]{1,0:T(8,128)(2,1)S(1)} %get-tuple-element.32.c0, bf16[112,512]{1,0:T(8,128)(2,1)S(1)} %collective-permute-done.3.c1, bf16[112,512]{1,0:T(8,128)(2,1)S(1)} %collective-permute-done.4.c2, bf16[112,512]{1,0:T(8,128)(2,1)S(1)} %collective-permute-done.5.c3), custom_call_target="tpu_custom_call" | custom-call | tf_op jit(solution)/shard_map/place_parts/pallas_call | solution.py:491
Async XLA Ops:
  2.8 30.3 %all-to-all-start = ((bf16[64,8,512]{2,1,0:T(8,128)(2,1)}), bf16[64,8,512]{2,1,0:T(8,128)(2,1)S(1)}, u32[]{:S(2)}, u32[]{:S(2)}) async-start(bf16[64,8,512]{2,1,0:T(8,128)(2,1)} %bitcast.14), calls=%async_computation | async-start | bytes 1048576 | tf_op jit(solution)/shard_map/all_to_all | solution.py:515
  15.8 1.1 %copy-start = (bf16[512,512]{1,0:T(8,128)(2,1)S(1)}, bf16[512,512]{1,0:T(8,128)(2,1)}, u32[]{:S(2)}) copy-start(bf16[512,512]{1,0:T(8,128)(2,1)} %pack_pairs.1.pack) | copy-start | bytes 1572868
  16.8 1.0 %copy-start.1 = (bf16[512,441]{0,1:T(8,128)(2,1)S(1)}, bf16[512,441]{0,1:T(8,128)(2,1)}, u32[]{:S(2)}) copy-start(bf16[512,441]{0,1:T(8,128)(2,1)} %param.11) | copy-start | bytes 1354756
  17.9 1.9 %copy-start.2 = (s32[3072,256]{1,0:T(8,128)S(1)}, s32[3072,256]{1,0:T(8,128)}, u32[]{:S(2)}) copy-start(s32[3072,256]{1,0:T(8,128)} %alignment.1) | copy-start | bytes 9437188
  19.8 13.3 %copy-start.3 = (f32[48,21]{0,1:T(8,128)S(1)}, f32[48,21]{0,1:T(8,128)}, u32[]{:S(2)}) copy-start(f32[48,21]{0,1:T(8,128)} %param.10) | copy-start | bytes 12100
  19.8 13.3 %copy-start.4 = (f32[256]{0:T(256)S(1)}, f32[256]{0:T(256)}, u32[]{:S(2)}) copy-start(f32[256]{0:T(256)} %param.9) | copy-start | bytes 3076
  41.8 31.5 %all-to-all-start.1 = ((bf16[256,8,128]{2,1,0:T(8,128)(2,1)}), bf16[256,8,128]{2,1,0:T(8,128)(2,1)S(1)}, u32[]{:S(2)}, u32[]{:S(2)}) async-start(bf16[256,8,128]{2,1,0:T(8,128)(2,1)} %bitcast.9), calls=%async_computation.1 | async-start | bytes 1048576 | tf_op jit(solution)/shard_map/all_to_all | solution.py:521
  55.5 6.2 %collective-permute-start = (bf16[128,512]{1,0:T(8,128)(2,1)S(1)}, bf16[128,512]{1,0:T(8,128)(2,1)S(1)}, u32[]{:S(2)}, u32[]{:S(2)}) collective-permute-start(bf16[128,512]{1,0:T(8,128)(2,1)S(1)} %get-tuple-element.28), channel_id=1, source_target_pairs={{0,64},{64,128},{128,192},{192,0},{1,65},{65,129},{129,193},{193,1... | collective-permute-start | bytes 393224 | tf_op jit(solution)/shard_map/ppermute | solution.py:502
  57.0 12.5 %collective-permute-start.1 = (bf16[128,512]{1,0:T(8,128)(2,1)S(1)}, bf16[128,512]{1,0:T(8,128)(2,1)S(1)}, u32[]{:S(2)}, u32[]{:S(2)}) collective-permute-start(bf16[128,512]{1,0:T(8,128)(2,1)S(1)} %get-tuple-element.29), channel_id=1, source_target_pairs={{0,128},{64,192},{128,0},{192,64},{1,129},{65,193},{129,1},{193,65... | collective-permute-start | bytes 393224 | tf_op jit(solution)/shard_map/ppermute | solution.py:502
  59.4 10.1 %collective-permute-start.2 = (bf16[128,512]{1,0:T(8,128)(2,1)S(1)}, bf16[128,512]{1,0:T(8,128)(2,1)S(1)}, u32[]{:S(2)}, u32[]{:S(2)}) collective-permute-start(bf16[128,512]{1,0:T(8,128)(2,1)S(1)} %get-tuple-element.30), channel_id=1, source_target_pairs={{0,192},{64,0},{128,64},{192,128},{1,193},{65,1},{129,65},{193,129... | collective-permute-start | bytes 393224 | tf_op jit(solution)/shard_map/ppermute | solution.py:502
  74.0 4.3 %collective-permute-start.5 = (bf16[112,512]{1,0:T(8,128)(2,1)S(1)}, bf16[112,512]{1,0:T(8,128)(2,1)S(1)}, u32[]{:S(2)}, u32[]{:S(2)}) collective-permute-start(bf16[112,512]{1,0:T(8,128)(2,1)S(1)} %get-tuple-element.32.c0), channel_id=1, source_target_pairs={{0,192},{64,0},{128,64},{192,128},{1,193},{65,1},{129,65},{193,129... | collective-permute-start | bytes 344072 | tf_op jit(solution)/shard_map/ppermute | solution.py:502
  74.7 5.5 %collective-permute-start.4 = (bf16[112,512]{1,0:T(8,128)(2,1)S(1)}, bf16[112,512]{1,0:T(8,128)(2,1)S(1)}, u32[]{:S(2)}, u32[]{:S(2)}) collective-permute-start(bf16[112,512]{1,0:T(8,128)(2,1)S(1)} %get-tuple-element.32.c0), channel_id=1, source_target_pairs={{0,128},{64,192},{128,0},{192,64},{1,129},{65,193},{129,1},{193,65... | collective-permute-start | bytes 344072 | tf_op jit(solution)/shard_map/ppermute | solution.py:502
  76.2 7.1 %collective-permute-start.3 = (bf16[112,512]{1,0:T(8,128)(2,1)S(1)}, bf16[112,512]{1,0:T(8,128)(2,1)S(1)}, u32[]{:S(2)}, u32[]{:S(2)}) collective-permute-start(bf16[112,512]{1,0:T(8,128)(2,1)S(1)} %get-tuple-element.32.c0), channel_id=1, source_target_pairs={{0,64},{64,128},{128,192},{192,0},{1,65},{65,129},{129,193},{193,1... | collective-permute-start | bytes 344072 | tf_op jit(solution)/shard_map/ppermute | solution.py:502
